TPU v7x, 32 devices: a whole 2x2x4 slice. The times are simulated.
32 devices in a mesh: gr: 4 (over y, core), gc: 8 (over z, x).
Axes of the slice: x: 2, y: 2, z: 4, core: 2. Of those that a mesh axis runs over, the one named last changes fastest.
Arguments:
- weights: bfloat16 [2048, 2048], P('gc', 'gr'), may hold values from 0.049804688 to 5
- in_pattern: int32 [16, 16], P('gc', 'gr'), may hold values from 0 to 1, as said below
- out_pattern: int32 [16, 16], P('gc', 'gr'), may hold values from 0 to 1, as said below
Outputs:
- next_matrix: bfloat16 [2048, 2048], P('gc', 'gr')
Inputs may be any that keep to these rules, and one draw needn't show every extreme that they name: `in_pattern`: 0 or 1 a block; every diagonal block is 1; each aligned tile of 2 block rows by 4 block columns holds at most 4 ones, and one such tile holds exactly 4. `out_pattern`: 0 or 1 a block; every diagonal block is 1.
All inputs are finite; a program needn't handle non-finite values.
Results may differ from a plain program's by a relative error of at most 0.0055.
Values may be sent and summed in bfloat16 or wider, within the bound.
No kernel may reach another device: no remote copies, remote signals or barrier semaphores. Data moves between devices by JAX's collectives and lax.ppermute only.
A program may use at most 128 MiB of HBM per device.

v0:
```python
import jax
import jax.numpy as jnp
from jax import lax
from jax.sharding import PartitionSpec as P


def mask_blocks(local_tile, block_flags, block_size):
    blk_rows, blk_cols = block_flags.shape
    shaped = local_tile.reshape(blk_rows, block_size, blk_cols, block_size)
    return (shaped * block_flags[:, None, :, None].astype(local_tile.dtype)).reshape(
        local_tile.shape
    )


def shards(weights, in_pattern, out_pattern):
    blk_rows, blk_cols = in_pattern.shape
    local_rows, local_cols = weights.shape
    block_size = local_rows // blk_rows
    grid_cols = lax.axis_size("gc")
    order_size = local_rows * grid_cols
    masked = mask_blocks(weights, in_pattern, block_size)
    column_part = jnp.sum(masked, axis=0, dtype=jnp.float32)
    input_total = lax.psum(column_part, "gc")
    inverse_local = 1.0 / input_total
    source = (masked.astype(jnp.float32) * inverse_local[None, :]).astype(jnp.bfloat16)
    row_panel = lax.all_gather(source, "gr", axis=1, tiled=True)
    product = jnp.dot(
        row_panel,
        lax.all_gather(source, "gc", axis=0, tiled=True),
        preferred_element_type=jnp.float32,
    )
    pruned = product.reshape(blk_rows, block_size, blk_cols, block_size) * out_pattern[
        :, None, :, None
    ].astype(jnp.float32)
    inflated = (pruned * pruned).reshape(local_rows, local_cols)
    output_total = lax.psum(jnp.sum(inflated, axis=0), "gc")
    return (inflated / output_total[None, :] * float(order_size)).astype(jnp.bfloat16)


def solution(mesh):
    in_specs = (P("gc", "gr"), P("gc", "gr"), P("gc", "gr"))
    out_specs = P("gc", "gr")
    return jax.shard_map(shards, mesh=mesh, in_specs=in_specs, out_specs=out_specs, check_vma=False)
```

profile of v0, /device:TPU:0, one launch (start us, length us, event | category | flops | bytes accessed | tf_op | source)
XLA Modules:
  0.0 128.2 jit_solution(260756495730400470)
XLA Ops:
  6.5 0.0 copy-start
  6.5 0.0 all-gather.3.cloned.1.call-start
  6.5 0.7 convert_element_type.18
  7.2 0.1 mul.40
  7.4 1.0 convert_reduce_fusion
  8.4 23.1 %psum.14 = f32[512]{0:T(512)S(1)} all-reduce(f32[512]{0:T(512)S(1)} %convert_reduce_fusion), channel_id=1, replica_groups=mesh['gr'=4,'gc'=8] {'gc'}, use_global_device_ids=true, to_apply=%region_1.0 | all-reduce | flops 512 | bytes 4096 | tf_op jit(solution)/shard_map/psum | solution.py:23
  31.5 1.7 %fusion.1 = bf16[256,512]{1,0:T(8,128)(2,1)} fusion(f32[512]{0:T(512)S(1)} %broadcast_divide_fusion, bf16[256,512]{1,0:T(8,128)(2,1)} %param.3, bf16[32,8,4,128]{3,2,1,0:T(4,128)(2,1)S(1)} %bitcast.15), kind=kLoop, calls=%fused_computation.4 | loop fusion | flops 524288 | bytes 788480 | tf_op jit(solution)/shard_map/convert_element_type | solution.py:25
  33.3 0.0 all-gather.3.cloned.1.call-update
  33.3 0.0 all-gather.5.cloned.1.call-start
  33.3 0.7 all-gather.5.cloned.1.call-update
  34.0 0.0 copy-done
  34.1 13.4 %all-gather.3.cloned.1.call-done = bf16[256,2048]{1,0:T(8,128)(2,1)} async-done(((bf16[256,512]{1,0:T(8,128)(2,1)}), bf16[256,2048]{1,0:T(8,128)(2,1)}) %all-gather.3.cloned.1.call-update) | async-done | bytes 1048592 | tf_op jit(solution)/shard_map/all_gather | solution.py:26
  47.5 51.5 %all-gather.5.cloned.1.call-done = bf16[2048,512]{1,0:T(8,128)(2,1)} async-done(((bf16[256,512]{1,0:T(8,128)(2,1)}), bf16[2048,512]{1,0:T(8,128)(2,1)}) %all-gather.5.cloned.1.call-update) | async-done | bytes 2097168 | tf_op jit(solution)/shard_map/all_gather | solution.py:29
  98.9 0.1 mul.45
  99.0 2.6 %fusion.2 = (f32[512]{0:T(512)S(1)}, f32[256,512]{1,0:T(8,128)S(1)}) fusion(f32[32,8,4,128]{3,2,1,0:T(4,128)S(1)} %bitcast.16, bf16[256,2048]{1,0:T(8,128)(2,1)} %all-gather.3.cloned.1.call-done, bf16[2048,512]{1,0:T(8,128)(2,1)} %all-gather.5.cloned.1.call-done), kind=kOutput, calls=%fused_computation.8 | convolution fusion | flops 537263616 | bytes 4196352 | tf_op jit(solution)/shard_map/dot_general | solution.py:27
  101.7 18.9 %psum.15 = f32[512]{0:T(512)S(1)} all-reduce(f32[512]{0:T(512)S(1)} %get-tuple-element.5), channel_id=1, replica_groups=mesh['gr'=4,'gc'=8] {'gc'}, use_global_device_ids=true, to_apply=%region_3.0 | all-reduce | flops 512 | bytes 4096 | tf_op jit(solution)/shard_map/psum | solution.py:36
  120.6 0.8 multiply_convert_fusion
  (2 shorter events, 0.0 us)
Async XLA Ops:
  6.5 27.5 %copy-start = (s32[2,4]{1,0:T(2,128)S(1)}, s32[2,4]{1,0:T(2,128)}, u32[]{:S(2)}) copy-start(s32[2,4]{1,0:T(2,128)} %param.5) | copy-start | bytes 100
  6.5 40.9 %all-gather.3.cloned.1.call-start = ((), (), s32[]{:S(2)}) async-start(), calls=%async_computation | async-start | bytes 1310720 | tf_op jit(solution)/shard_map/all_gather | solution.py:26
  33.3 65.6 %all-gather.5.cloned.1.call-start = ((), (), s32[]{:S(2)}) async-start(), calls=%async_computation.1 | async-start | bytes 2359296 | tf_op jit(solution)/shard_map/all_gather | solution.py:29
Sparse Core Ops, SparseCore 0:
  33.4 14.0 all-gather.2
  49.6 49.2 all-gather.4
where the time goes:
time: 128 us
  waiting for transfers between devices  65.6 us (51%)
  blocking collectives  42 us (33%)
  between operations  13.4 us (10%)
  other arithmetic  4.25 us (3%)
  matrix products  2.64 us (2%)
    all_gather x1, waiting for transfers between devices, shards(): lax.all_gather(source, 'gc', axis=0, tiled=True)  51.5 us
    psum x1, blocking collectives, shards(): input_total = lax.psum(column_part, 'gc')  23.1 us
    psum x1, blocking collectives, shards(): output_total = lax.psum(jnp.sum(inflated, axis=0), 'gc')  18.9 us
    all_gather x1, waiting for transfers between devices, shards(): row_panel = lax.all_gather(source, 'gr', axis=1, tiled=True)  13.4 us
    dot_general x1, matrix products, shards(): jnp.dot(row_panel, lax.all_gather(source, 'gc', axis=0, tiled=True), pref...  2.64 us
  transfers between devices with their start and end apart: 2, of which 2 were waited for; matrix products, arithmetic and copies ran while one was open for 0% of the time, Pallas kernels for 0%

commit v1 on v0

v1 whole, which is shorter than its diff:
```python
import functools

import jax
import jax.numpy as jnp
from jax import lax
from jax.experimental import pallas as pl
from jax.experimental.pallas import tpu as pltpu
from jax.sharding import PartitionSpec as P

SLOTS = 4
META = 16
VMEM = pl.BlockSpec(memory_space=pltpu.VMEM)
SMEM = pl.BlockSpec(memory_space=pltpu.SMEM)


def bits_of(size):
    return [1 << b for b in reversed(range(size.bit_length() - 1))]


def swap(x, axis, bit):
    return lax.ppermute(x, axis, [(i, i ^ bit) for i in range(lax.axis_size(axis))])


def gather_xor(x, axis):
    held = {0: x}
    for bit in bits_of(lax.axis_size(axis)):
        held.update({m | bit: swap(v, axis, bit) for m, v in list(held.items())})
    return [held[m] for m in range(len(held))]


def total_over(x, axis):
    for bit in bits_of(lax.axis_size(axis)):
        x = x + swap(x, axis, bit)
    return x


def pack_kernel(flags_ref, weights_ref, packet_ref, sums_ref):
    blk_rows, blk_cols = flags_ref.shape
    size = weights_ref.shape[0] // blk_rows
    blocks = blk_rows * blk_cols
    flags = [flags_ref[b // blk_cols, b % blk_cols] for b in range(blocks)]
    count = sum(flags)
    ones, zeros, slots = 0, 0, []
    for b in range(blocks):
        slots.append(jnp.where(flags[b] == 1, ones, count + zeros))
        ones, zeros = ones + flags[b], zeros + (1 - flags[b])
    sums_ref[...] = jnp.zeros_like(sums_ref)
    row_ids = lax.broadcasted_iota(jnp.int32, (META, size), 0)
    meta = jnp.zeros((META, size), jnp.float32)
    for s in range(SLOTS):
        place = sum(jnp.where(slots[b] == s, b, 0) for b in range(blocks))
        row = pl.multiple_of(place // blk_cols * size, size)
        col = pl.multiple_of(place % blk_cols * size, size)
        block = weights_ref[pl.ds(row, size), pl.ds(col, size)]
        block = jnp.where(s < count, block, jnp.zeros_like(block))
        packet_ref[pl.ds(s * size, size), :] = block
        sums_ref[:, pl.ds(col, size)] += jnp.sum(block.astype(jnp.float32), axis=0, keepdims=True)
        meta = jnp.where(row_ids == s, place.astype(jnp.float32), meta)
    packet_ref[pl.ds(SLOTS * size, META), :] = meta.astype(packet_ref.dtype)


def expand_kernel(gr_size, gc_size, blk_rows, blk_cols, *refs):
    out_flags_ref, totals_ref = refs[:2]
    left_refs = refs[2 : 2 + gr_size]
    right_refs = refs[2 + gr_size : 2 + gr_size + gc_size]
    inflated_ref, sums_ref, left, right = refs[2 + gr_size + gc_size :]
    size = left.shape[0] // blk_rows
    my_col, my_row = lax.axis_index("gr"), lax.axis_index("gc")

    def places(ref):
        meta = ref[pl.ds(SLOTS * size, META), :].astype(jnp.float32)
        return [jnp.max(meta[s : s + 1, :]).astype(jnp.int32) for s in range(SLOTS)]

    inverse = 1.0 / totals_ref[...]
    left[...] = jnp.zeros_like(left)
    right[...] = jnp.zeros_like(right)
    for m, ref in enumerate(left_refs):
        base = (my_col ^ m) * blk_cols
        for s, place in enumerate(places(ref)):
            row = pl.multiple_of(place // blk_cols * size, size)
            col = place % blk_cols
            scale = inverse[m : m + 1, :size]
            for j in range(1, blk_cols):
                scale = jnp.where(col == j, inverse[m : m + 1, j * size : (j + 1) * size], scale)
            block = ref[pl.ds(s * size, size), :].astype(jnp.float32) * scale
            at = pl.multiple_of((base + col) * size, size)
            left[pl.ds(row, size), pl.ds(at, size)] = block.astype(left.dtype)
    for m, ref in enumerate(right_refs):
        base = (my_row ^ m) * blk_rows
        for s, place in enumerate(places(ref)):
            row = pl.multiple_of((base + place // blk_cols) * size, size)
            col = pl.multiple_of(place % blk_cols * size, size)
            right[pl.ds(row, size), pl.ds(col, size)] = ref[pl.ds(s * size, size), :]
    product = jnp.dot(left[...], right[...], preferred_element_type=jnp.float32)
    for j in range(blk_cols):
        at = slice(j * size, (j + 1) * size)
        total = jnp.zeros((1, size), jnp.float32)
        for i in range(blk_rows):
            rows = slice(i * size, (i + 1) * size)
            kept = product[rows, at] * inverse[0:1, at]
            kept = kept * out_flags_ref[i, j].astype(jnp.float32)
            squared = kept * kept
            inflated_ref[rows, at] = squared
            total = total + jnp.sum(squared, axis=0, keepdims=True)
        sums_ref[:, at] = total


def shards(weights, in_pattern, out_pattern):
    blk_rows, blk_cols = in_pattern.shape
    local_rows, local_cols = weights.shape
    size = local_rows // blk_rows
    gr_size, gc_size = lax.axis_size("gr"), lax.axis_size("gc")
    order_size = local_rows * gc_size
    packet, sums = pl.pallas_call(
        pack_kernel,
        out_shape=(
            jax.ShapeDtypeStruct((SLOTS * size + META, size), weights.dtype),
            jax.ShapeDtypeStruct((1, local_cols), jnp.float32),
        ),
        in_specs=[SMEM, VMEM],
        out_specs=(VMEM, VMEM),
        name="pack",
    )(in_pattern, weights)
    totals = total_over(jnp.concatenate(gather_xor(sums, "gr"), axis=0), "gc")
    left = gather_xor(packet, "gr")
    right = gather_xor(packet, "gc")
    inflated, sums = pl.pallas_call(
        functools.partial(expand_kernel, gr_size, gc_size, blk_rows, blk_cols),
        out_shape=(
            jax.ShapeDtypeStruct((local_rows, local_cols), jnp.float32),
            jax.ShapeDtypeStruct((1, local_cols), jnp.float32),
        ),
        in_specs=[SMEM, VMEM] + [VMEM] * (gr_size + gc_size),
        out_specs=(VMEM, VMEM),
        scratch_shapes=[
            pltpu.VMEM((local_rows, order_size), jnp.bfloat16),
            pltpu.VMEM((order_size, local_cols), jnp.bfloat16),
        ],
        compiler_params=pltpu.CompilerParams(vmem_limit_bytes=40 << 20),
        name="expand",
    )(out_pattern, totals, *left, *right)
    output_total = total_over(sums, "gc")
    return (inflated / output_total * float(order_size)).astype(jnp.bfloat16)


def solution(mesh):
    in_specs = (P("gc", "gr"), P("gc", "gr"), P("gc", "gr"))
    out_specs = P("gc", "gr")
    return jax.shard_map(shards, mesh=mesh, in_specs=in_specs, out_specs=out_specs, check_vma=False)
```

time: 128 us -> 53.4 us (0.42)
  blocking collectives: 42 us -> 0 us
  waiting for transfers between devices: 65.6 us -> 24.3 us
  starting transfers between devices: 0.04 us -> 22.4 us
  between operations: 13.4 us -> 0.05 us
  Pallas kernels: 0 us -> 4.01 us
  other arithmetic: 4.25 us -> 1.56 us
  matrix products: 2.64 us -> 0 us
    all_gather x2 -> x0, waiting for transfers between devices: 64.8 us -> none  [the longest x1 51.5 us: shards(): lax.all_gather(source, 'gc', axis=0, tiled=True)]
    psum x2 -> x0, blocking collectives: 42 us -> none  [the longest x1 23.1 us: shards(): input_total = lax.psum(column_part, 'gc')]
    ppermute x0 -> x19, waiting for transfers between devices: none -> 24.3 us  [swap(): lax.ppermute(x, axis, [(i, i ^ bit) for i in range(lax.axis_size(axis))])]
    ppermute x0 -> x19, starting transfers between devices: none -> 22.4 us  [swap(): lax.ppermute(x, axis, [(i, i ^ bit) for i in range(lax.axis_size(axis))])]
    pallas_call x0 -> x2, Pallas kernels: none -> 4.01 us  [the longest x1 2.3 us: shards(): pl.pallas_call(functools.partial(expand_kernel, gr_size, gc_size, blk_row...]
    dot_general x1 -> x0, matrix products: 2.64 us -> none  [shards(): jnp.dot(row_panel, lax.all_gather(source, 'gc', axis=0, tiled=True), pref...]
    convert_element_type x4 -> x1, other arithmetic: 3.2 us -> 0.76 us  [shards(): return (inflated / output_total * float(order_size)).astype(jnp.bfloat16)]
  transfers between devices with their start and end apart: 2 -> 19, of which waited for: 2 -> 11; matrix products, arithmetic and copies ran while one was open for 0% -> 0% of each run, Pallas kernels for 0% -> 0%
where the time goes in v1:
time: 53.4 us; the launch traced here: 53.2 us
  waiting for transfers between devices  24.3 us (46%)
  starting transfers between devices  22.4 us (42%)
  Pallas kernels  4.01 us (8%)
  other arithmetic  1.56 us (3%)
  local copies, waits for them, and re-layouts  0.92 us (2%)
    ppermute x19, waiting for transfers between devices, swap(): lax.ppermute(x, axis, [(i, i ^ bit) for i in range(lax.axis_size(axis))])  24.3 us
    ppermute x19, starting transfers between devices, swap(): lax.ppermute(x, axis, [(i, i ^ bit) for i in range(lax.axis_size(axis))])  22.4 us
    pallas_call x1, Pallas kernels, shards(): pl.pallas_call(functools.partial(expand_kernel, gr_size, gc_size, blk_row...  2.3 us
    pallas_call x1, Pallas kernels, shards(): pl.pallas_call(pack_kernel, out_shape=(jax.ShapeDtypeStruct((SLOTS * size...  1.71 us
  transfers between devices with their start and end apart: 19, of which 11 were waited for; matrix products, arithmetic and copies ran while one was open for 0% of the time, Pallas kernels for 0%

profile of v1, /device:TPU:0, one launch (start us, length us, event | category | flops | bytes accessed | tf_op | source)
XLA Modules:
  0.0 53.2 jit_solution(9976541477658785933)
XLA Ops:
  0.0 1.7 %pack.1 = (bf16[528,128]{1,0:T(8,128)(2,1)}, f32[1,512]{1,0:T(1,128)}) custom-call(s32[2,4]{1,0:T(2,128)} %flags_ref.1, bf16[256,512]{1,0:T(8,128)(2,1)} %weights_ref.1), custom_call_target="tpu_custom_call" | custom-call | tf_op jit(solution)/shard_map/pack/pallas_call | solution.py:114
  1.7 3.0 %collective-permute-start.1 = (f32[1,512]{1,0:T(1,128)}, f32[1,512]{1,0:T(1,128)S(1)}, u32[]{:S(2)}, u32[]{:S(2)}) collective-permute-start(f32[1,512]{1,0:T(1,128)} %get-tuple-element.9), channel_id=1, source_target_pairs={{0,16},{8,24},{16,0},{24,8},{1,17},{9,25},{17,1},{25,9},{2,18},{10... | collective-permute-start | bytes 6152 | tf_op jit(solution)/shard_map/ppermute | solution.py:21
  4.7 1.8 %collective-permute-done.1 = f32[1,512]{1,0:T(1,128)S(1)} collective-permute-done((f32[1,512]{1,0:T(1,128)}, f32[1,512]{1,0:T(1,128)S(1)}, u32[]{:S(2)}, u32[]{:S(2)}) %collective-permute-start.1) | collective-permute-done | bytes 2080 | tf_op jit(solution)/shard_map/ppermute | solution.py:21
  6.5 1.2 %collective-permute-done.2 = f32[1,512]{1,0:T(1,128)S(1)} collective-permute-done((f32[1,512]{1,0:T(1,128)S(1)}, f32[1,512]{1,0:T(1,128)S(1)}, u32[]{:S(2)}, u32[]{:S(2)}) %collective-permute-start.2) | collective-permute-done | bytes 2080 | tf_op jit(solution)/shard_map/ppermute | solution.py:21
  8.4 3.2 %collective-permute-start.3 = (f32[4,512]{1,0:T(4,128)S(1)}, f32[4,512]{1,0:T(4,128)S(1)}, u32[]{:S(2)}, u32[]{:S(2)}) collective-permute-start(f32[4,512]{1,0:T(4,128)S(1)} %pad_maximum_fusion), channel_id=1, source_target_pairs={{0,4},{1,5},{2,6},{3,7},{4,0},{5,1},{6,2},{7,3},{8,12},{9,13},{10,... | collective-permute-start | bytes 24584 | tf_op jit(solution)/shard_map/ppermute | solution.py:21
  11.6 1.6 %collective-permute-done.3 = f32[4,512]{1,0:T(4,128)S(1)} collective-permute-done((f32[4,512]{1,0:T(4,128)S(1)}, f32[4,512]{1,0:T(4,128)S(1)}, u32[]{:S(2)}, u32[]{:S(2)}) %collective-permute-start.3) | collective-permute-done | bytes 8224 | tf_op jit(solution)/shard_map/ppermute | solution.py:21
  13.2 2.0 %collective-permute-start.4 = (f32[4,512]{1,0:T(4,128)S(1)}, f32[4,512]{1,0:T(4,128)S(1)}, u32[]{:S(2)}, u32[]{:S(2)}) collective-permute-start(f32[4,512]{1,0:T(4,128)S(1)} %fusion), channel_id=1, source_target_pairs={{0,2},{1,3},{2,0},{3,1},{4,6},{5,7},{6,4},{7,5},{8,10},{9,11},{10,... | collective-permute-start | bytes 24584 | tf_op jit(solution)/shard_map/ppermute | solution.py:21
  15.3 1.8 %collective-permute-start.9 = (bf16[528,128]{1,0:T(8,128)(2,1)}, bf16[528,128]{1,0:T(8,128)(2,1)S(1)}, u32[]{:S(2)}, u32[]{:S(2)}) collective-permute-start(bf16[528,128]{1,0:T(8,128)(2,1)} %get-tuple-element.10.refs_2_.refs_6_), channel_id=1, source_target_pairs={{0,1},{1,0},{2,3},{3,2},{4,5},{5,4},{6,7},{7,6},{8,9},{9,8},{10,11... | collective-permute-start | bytes 405512 | tf_op jit(solution)/shard_map/ppermute | solution.py:21
  17.1 1.5 %collective-permute-start.7 = (bf16[528,128]{1,0:T(8,128)(2,1)}, bf16[528,128]{1,0:T(8,128)(2,1)S(1)}, u32[]{:S(2)}, u32[]{:S(2)}) collective-permute-start(bf16[528,128]{1,0:T(8,128)(2,1)} %get-tuple-element.10.refs_2_.refs_6_), channel_id=1, source_target_pairs={{0,16},{8,24},{16,0},{24,8},{1,17},{9,25},{17,1},{25,9},{2,18},{10... | collective-permute-start | bytes 405512 | tf_op jit(solution)/shard_map/ppermute | solution.py:21
  18.6 2.4 %collective-permute-done.12.refs_10_ = bf16[528,128]{1,0:T(8,128)(2,1)S(1)} collective-permute-done((bf16[528,128]{1,0:T(8,128)(2,1)}, bf16[528,128]{1,0:T(8,128)(2,1)S(1)}, u32[]{:S(2)}, u32[]{:S(2)}) %collective-permute-start.12) | collective-permute-done | bytes 135200 | tf_op jit(solution)/shard_map/ppermute | solution.py:21
  21.1 1.6 %collective-permute-start.5 = (f32[4,512]{1,0:T(4,128)S(1)}, f32[4,512]{1,0:T(4,128)S(1)}, u32[]{:S(2)}, u32[]{:S(2)}) collective-permute-start(f32[4,512]{1,0:T(4,128)S(1)} %fusion.1), channel_id=1, source_target_pairs={{0,1},{1,0},{2,3},{3,2},{4,5},{5,4},{6,7},{7,6},{8,9},{9,8},{10,11... | collective-permute-start | bytes 24584 | tf_op jit(solution)/shard_map/ppermute | solution.py:21
  22.6 2.2 %collective-permute-done.5 = f32[4,512]{1,0:T(4,128)S(1)} collective-permute-done((f32[4,512]{1,0:T(4,128)S(1)}, f32[4,512]{1,0:T(4,128)S(1)}, u32[]{:S(2)}, u32[]{:S(2)}) %collective-permute-start.5) | collective-permute-done | bytes 8224 | tf_op jit(solution)/shard_map/ppermute | solution.py:21
  24.8 1.5 %collective-permute-start.13 = (bf16[528,128]{1,0:T(8,128)(2,1)S(1)}, bf16[528,128]{1,0:T(8,128)(2,1)S(1)}, u32[]{:S(2)}, u32[]{:S(2)}) collective-permute-start(bf16[528,128]{1,0:T(8,128)(2,1)S(1)} %collective-permute-done.12.refs_10_), channel_id=1, source_target_pairs={{0,1},{1,0},{2,3},{3,2},{4,5},{5,4},{6,7},{7,6},{8,9},{9,8},{10,11... | collective-permute-start | bytes 405512 | tf_op jit(solution)/shard_map/ppermute | solution.py:21
  26.8 1.6 %collective-permute-start.15 = (bf16[528,128]{1,0:T(8,128)(2,1)S(1)}, bf16[528,128]{1,0:T(8,128)(2,1)S(1)}, u32[]{:S(2)}, u32[]{:S(2)}) collective-permute-start(bf16[528,128]{1,0:T(8,128)(2,1)S(1)} %collective-permute-done.14.refs_12_), channel_id=1, source_target_pairs={{0,1},{1,0},{2,3},{3,2},{4,5},{5,4},{6,7},{7,6},{8,9},{9,8},{10,11... | collective-permute-start | bytes 405512 | tf_op jit(solution)/shard_map/ppermute | solution.py:21
  28.4 2.8 %collective-permute-done.13.refs_11_ = bf16[528,128]{1,0:T(8,128)(2,1)S(1)} collective-permute-done((bf16[528,128]{1,0:T(8,128)(2,1)S(1)}, bf16[528,128]{1,0:T(8,128)(2,1)S(1)}, u32[]{:S(2)}, u32[]{:S(2)}) %collective-permute-start.13) | collective-permute-done | bytes 135200 | tf_op jit(solution)/shard_map/ppermute | solution.py:21
  31.2 2.9 %collective-permute-done.11.refs_9_ = bf16[528,128]{1,0:T(8,128)(2,1)S(1)} collective-permute-done((bf16[528,128]{1,0:T(8,128)(2,1)S(1)}, bf16[528,128]{1,0:T(8,128)(2,1)S(1)}, u32[]{:S(2)}, u32[]{:S(2)}) %collective-permute-start.11) | collective-permute-done | bytes 135200 | tf_op jit(solution)/shard_map/ppermute | solution.py:21
  34.1 2.5 %collective-permute-done.15.refs_13_ = bf16[528,128]{1,0:T(8,128)(2,1)S(1)} collective-permute-done((bf16[528,128]{1,0:T(8,128)(2,1)S(1)}, bf16[528,128]{1,0:T(8,128)(2,1)S(1)}, u32[]{:S(2)}, u32[]{:S(2)}) %collective-permute-start.15) | collective-permute-done | bytes 135200 | tf_op jit(solution)/shard_map/ppermute | solution.py:21
  36.6 0.9 %copy-done = bf16[528,128]{1,0:T(8,128)(2,1)S(1)} copy-done((bf16[528,128]{1,0:T(8,128)(2,1)S(1)}, bf16[528,128]{1,0:T(8,128)(2,1)}, u32[]{:S(2)}) %copy-start) | copy-done | bytes 135192
  37.5 2.3 %expand.1 = (f32[256,512]{1,0:T(8,128)S(1)}, f32[1,512]{1,0:T(1,128)S(1)}) custom-call(s32[2,4]{1,0:T(2,128)S(1)} %copy-done.1, f32[4,512]{1,0:T(4,128)S(1)} %add.20.refs_1_, bf16[528,128]{1,0:T(8,128)(2,1)S(1)} %copy-done, bf16[528,128]{1,0:T(8,128)(2,1)S(1)} %collective-permute-done.6.refs_3_, bf16[528,128]{1,0:T(8,128)(2,1)S(1)} %collective-permute-done.7.refs_4_, ...), custom_call_target="tpu_custom_call" | custom-call | tf_op jit(solution)/shard_map/expand/pallas_call | solution.py:127
  39.8 3.9 %collective-permute-start.16 = (f32[1,512]{1,0:T(1,128)S(1)}, f32[1,512]{1,0:T(1,128)S(1)}, u32[]{:S(2)}, u32[]{:S(2)}) collective-permute-start(f32[1,512]{1,0:T(1,128)S(1)} %get-tuple-element.12), channel_id=1, source_target_pairs={{0,4},{1,5},{2,6},{3,7},{4,0},{5,1},{6,2},{7,3},{8,12},{9,13},{10,... | collective-permute-start | bytes 6152 | tf_op jit(solution)/shard_map/ppermute | solution.py:21
  43.7 1.6 %collective-permute-done.16 = f32[1,512]{1,0:T(1,128)S(1)} collective-permute-done((f32[1,512]{1,0:T(1,128)S(1)}, f32[1,512]{1,0:T(1,128)S(1)}, u32[]{:S(2)}, u32[]{:S(2)}) %collective-permute-start.16) | collective-permute-done | bytes 2080 | tf_op jit(solution)/shard_map/ppermute | solution.py:21
  45.3 1.1 %collective-permute-start.17 = (f32[1,512]{1,0:T(1,128)S(1)}, f32[1,512]{1,0:T(1,128)S(1)}, u32[]{:S(2)}, u32[]{:S(2)}) collective-permute-start(f32[1,512]{1,0:T(1,128)S(1)} %add.21), channel_id=1, source_target_pairs={{0,2},{1,3},{2,0},{3,1},{4,6},{5,7},{6,4},{7,5},{8,10},{9,11},{10,... | collective-permute-start | bytes 6152 | tf_op jit(solution)/shard_map/ppermute | solution.py:21
  46.4 2.5 %collective-permute-done.17 = f32[1,512]{1,0:T(1,128)S(1)} collective-permute-done((f32[1,512]{1,0:T(1,128)S(1)}, f32[1,512]{1,0:T(1,128)S(1)}, u32[]{:S(2)}, u32[]{:S(2)}) %collective-permute-start.17) | collective-permute-done | bytes 2080 | tf_op jit(solution)/shard_map/ppermute | solution.py:21
  49.4 3.0 %collective-permute-done.18 = f32[1,512]{1,0:T(1,128)S(1)} collective-permute-done((f32[1,512]{1,0:T(1,128)S(1)}, f32[1,512]{1,0:T(1,128)S(1)}, u32[]{:S(2)}, u32[]{:S(2)}) %collective-permute-start.18) | collective-permute-done | bytes 2080 | tf_op jit(solution)/shard_map/ppermute | solution.py:21
  (30 shorter events, 2.9 us)
Async XLA Ops:
  1.7 4.7 %collective-permute-start.1 = (f32[1,512]{1,0:T(1,128)}, f32[1,512]{1,0:T(1,128)S(1)}, u32[]{:S(2)}, u32[]{:S(2)}) collective-permute-start(f32[1,512]{1,0:T(1,128)} %get-tuple-element.9), channel_id=1, source_target_pairs={{0,16},{8,24},{16,0},{24,8},{1,17},{9,25},{17,1},{25,9},{2,18},{10... | collective-permute-start | bytes 6152 | tf_op jit(solution)/shard_map/ppermute | solution.py:21
  4.7 1.8 %collective-permute-start = (f32[1,512]{1,0:T(1,128)}, f32[1,512]{1,0:T(1,128)S(1)}, u32[]{:S(2)}, u32[]{:S(2)}) collective-permute-start(f32[1,512]{1,0:T(1,128)} %get-tuple-element.9), channel_id=1, source_target_pairs={{0,8},{8,0},{16,24},{24,16},{1,9},{9,1},{17,25},{25,17},{2,10},{10... | collective-permute-start | bytes 6152 | tf_op jit(solution)/shard_map/ppermute | solution.py:21
  6.5 1.2 %collective-permute-start.2 = (f32[1,512]{1,0:T(1,128)S(1)}, f32[1,512]{1,0:T(1,128)S(1)}, u32[]{:S(2)}, u32[]{:S(2)}) collective-permute-start(f32[1,512]{1,0:T(1,128)S(1)} %collective-permute-done.1), channel_id=1, source_target_pairs={{0,8},{8,0},{16,24},{24,16},{1,9},{9,1},{17,25},{25,17},{2,10},{10... | collective-permute-start | bytes 6152 | tf_op jit(solution)/shard_map/ppermute | solution.py:21
  7.6 5.5 %copy-start.2 = (f32[1,512]{1,0:T(1,128)S(1)}, f32[1,512]{1,0:T(1,128)}, u32[]{:S(2)}) copy-start(f32[1,512]{1,0:T(1,128)} %get-tuple-element.9) | copy-start | bytes 6148
  8.4 4.8 %collective-permute-start.3 = (f32[4,512]{1,0:T(4,128)S(1)}, f32[4,512]{1,0:T(4,128)S(1)}, u32[]{:S(2)}, u32[]{:S(2)}) collective-permute-start(f32[4,512]{1,0:T(4,128)S(1)} %pad_maximum_fusion), channel_id=1, source_target_pairs={{0,4},{1,5},{2,6},{3,7},{4,0},{5,1},{6,2},{7,3},{8,12},{9,13},{10,... | collective-permute-start | bytes 24584 | tf_op jit(solution)/shard_map/ppermute | solution.py:21
  11.5 9.5 %collective-permute-start.12 = (bf16[528,128]{1,0:T(8,128)(2,1)}, bf16[528,128]{1,0:T(8,128)(2,1)S(1)}, u32[]{:S(2)}, u32[]{:S(2)}) collective-permute-start(bf16[528,128]{1,0:T(8,128)(2,1)} %get-tuple-element.10.refs_2_.refs_6_), channel_id=1, source_target_pairs={{0,4},{1,5},{2,6},{3,7},{4,0},{5,1},{6,2},{7,3},{8,12},{9,13},{10,... | collective-permute-start | bytes 405512 | tf_op jit(solution)/shard_map/ppermute | solution.py:21
  13.2 7.8 %collective-permute-start.4 = (f32[4,512]{1,0:T(4,128)S(1)}, f32[4,512]{1,0:T(4,128)S(1)}, u32[]{:S(2)}, u32[]{:S(2)}) collective-permute-start(f32[4,512]{1,0:T(4,128)S(1)} %fusion), channel_id=1, source_target_pairs={{0,2},{1,3},{2,0},{3,1},{4,6},{5,7},{6,4},{7,5},{8,10},{9,11},{10,... | collective-permute-start | bytes 24584 | tf_op jit(solution)/shard_map/ppermute | solution.py:21
  15.1 9.6 %collective-permute-start.10 = (bf16[528,128]{1,0:T(8,128)(2,1)}, bf16[528,128]{1,0:T(8,128)(2,1)S(1)}, u32[]{:S(2)}, u32[]{:S(2)}) collective-permute-start(bf16[528,128]{1,0:T(8,128)(2,1)} %get-tuple-element.10.refs_2_.refs_6_), channel_id=1, source_target_pairs={{0,2},{1,3},{2,0},{3,1},{4,6},{5,7},{6,4},{7,5},{8,10},{9,11},{10,... | collective-permute-start | bytes 405512 | tf_op jit(solution)/shard_map/ppermute | solution.py:21
  15.3 11.0 %collective-permute-start.9 = (bf16[528,128]{1,0:T(8,128)(2,1)}, bf16[528,128]{1,0:T(8,128)(2,1)S(1)}, u32[]{:S(2)}, u32[]{:S(2)}) collective-permute-start(bf16[528,128]{1,0:T(8,128)(2,1)} %get-tuple-element.10.refs_2_.refs_6_), channel_id=1, source_target_pairs={{0,1},{1,0},{2,3},{3,2},{4,5},{5,4},{6,7},{7,6},{8,9},{9,8},{10,11... | collective-permute-start | bytes 405512 | tf_op jit(solution)/shard_map/ppermute | solution.py:21
  17.1 9.7 %collective-permute-start.7 = (bf16[528,128]{1,0:T(8,128)(2,1)}, bf16[528,128]{1,0:T(8,128)(2,1)S(1)}, u32[]{:S(2)}, u32[]{:S(2)}) collective-permute-start(bf16[528,128]{1,0:T(8,128)(2,1)} %get-tuple-element.10.refs_2_.refs_6_), channel_id=1, source_target_pairs={{0,16},{8,24},{16,0},{24,8},{1,17},{9,25},{17,1},{25,9},{2,18},{10... | collective-permute-start | bytes 405512 | tf_op jit(solution)/shard_map/ppermute | solution.py:21
  21.0 5.8 %collective-permute-start.14 = (bf16[528,128]{1,0:T(8,128)(2,1)S(1)}, bf16[528,128]{1,0:T(8,128)(2,1)S(1)}, u32[]{:S(2)}, u32[]{:S(2)}) collective-permute-start(bf16[528,128]{1,0:T(8,128)(2,1)S(1)} %collective-permute-done.12.refs_10_), channel_id=1, source_target_pairs={{0,2},{1,3},{2,0},{3,1},{4,6},{5,7},{6,4},{7,5},{8,10},{9,11},{10,... | collective-permute-start | bytes 405512 | tf_op jit(solution)/shard_map/ppermute | solution.py:21
  21.0 15.5 %copy-start.1 = (s32[2,4]{1,0:T(2,128)S(1)}, s32[2,4]{1,0:T(2,128)}, u32[]{:S(2)}) copy-start(s32[2,4]{1,0:T(2,128)} %refs_0_.1) | copy-start | bytes 100
  21.1 3.7 %collective-permute-start.5 = (f32[4,512]{1,0:T(4,128)S(1)}, f32[4,512]{1,0:T(4,128)S(1)}, u32[]{:S(2)}, u32[]{:S(2)}) collective-permute-start(f32[4,512]{1,0:T(4,128)S(1)} %fusion.1), channel_id=1, source_target_pairs={{0,1},{1,0},{2,3},{3,2},{4,5},{5,4},{6,7},{7,6},{8,9},{9,8},{10,11... | collective-permute-start | bytes 24584 | tf_op jit(solution)/shard_map/ppermute | solution.py:21
  24.8 3.6 %collective-permute-start.6 = (bf16[528,128]{1,0:T(8,128)(2,1)}, bf16[528,128]{1,0:T(8,128)(2,1)S(1)}, u32[]{:S(2)}, u32[]{:S(2)}) collective-permute-start(bf16[528,128]{1,0:T(8,128)(2,1)} %get-tuple-element.10.refs_2_.refs_6_), channel_id=1, source_target_pairs={{0,8},{8,0},{16,24},{24,16},{1,9},{9,1},{17,25},{25,17},{2,10},{10... | collective-permute-start | bytes 405512 | tf_op jit(solution)/shard_map/ppermute | solution.py:21
  24.8 6.4 %collective-permute-start.13 = (bf16[528,128]{1,0:T(8,128)(2,1)S(1)}, bf16[528,128]{1,0:T(8,128)(2,1)S(1)}, u32[]{:S(2)}, u32[]{:S(2)}) collective-permute-start(bf16[528,128]{1,0:T(8,128)(2,1)S(1)} %collective-permute-done.12.refs_10_), channel_id=1, source_target_pairs={{0,1},{1,0},{2,3},{3,2},{4,5},{5,4},{6,7},{7,6},{8,9},{9,8},{10,11... | collective-permute-start | bytes 405512 | tf_op jit(solution)/shard_map/ppermute | solution.py:21
  26.3 7.8 %collective-permute-start.11 = (bf16[528,128]{1,0:T(8,128)(2,1)S(1)}, bf16[528,128]{1,0:T(8,128)(2,1)S(1)}, u32[]{:S(2)}, u32[]{:S(2)}) collective-permute-start(bf16[528,128]{1,0:T(8,128)(2,1)S(1)} %collective-permute-done.10.refs_8_), channel_id=1, source_target_pairs={{0,1},{1,0},{2,3},{3,2},{4,5},{5,4},{6,7},{7,6},{8,9},{9,8},{10,11... | collective-permute-start | bytes 405512 | tf_op jit(solution)/shard_map/ppermute | solution.py:21
  26.8 7.2 %collective-permute-start.8 = (bf16[528,128]{1,0:T(8,128)(2,1)S(1)}, bf16[528,128]{1,0:T(8,128)(2,1)S(1)}, u32[]{:S(2)}, u32[]{:S(2)}) collective-permute-start(bf16[528,128]{1,0:T(8,128)(2,1)S(1)} %collective-permute-done.7.refs_4_), channel_id=1, source_target_pairs={{0,8},{8,0},{16,24},{24,16},{1,9},{9,1},{17,25},{25,17},{2,10},{10... | collective-permute-start | bytes 405512 | tf_op jit(solution)/shard_map/ppermute | solution.py:21
  26.8 9.7 %collective-permute-start.15 = (bf16[528,128]{1,0:T(8,128)(2,1)S(1)}, bf16[528,128]{1,0:T(8,128)(2,1)S(1)}, u32[]{:S(2)}, u32[]{:S(2)}) collective-permute-start(bf16[528,128]{1,0:T(8,128)(2,1)S(1)} %collective-permute-done.14.refs_12_), channel_id=1, source_target_pairs={{0,1},{1,0},{2,3},{3,2},{4,5},{5,4},{6,7},{7,6},{8,9},{9,8},{10,11... | collective-permute-start | bytes 405512 | tf_op jit(solution)/shard_map/ppermute | solution.py:21
  36.6 0.9 %copy-start = (bf16[528,128]{1,0:T(8,128)(2,1)S(1)}, bf16[528,128]{1,0:T(8,128)(2,1)}, u32[]{:S(2)}) copy-start(bf16[528,128]{1,0:T(8,128)(2,1)} %get-tuple-element.10.refs_2_.refs_6_) | copy-start | bytes 405508
  39.8 5.5 %collective-permute-start.16 = (f32[1,512]{1,0:T(1,128)S(1)}, f32[1,512]{1,0:T(1,128)S(1)}, u32[]{:S(2)}, u32[]{:S(2)}) collective-permute-start(f32[1,512]{1,0:T(1,128)S(1)} %get-tuple-element.12), channel_id=1, source_target_pairs={{0,4},{1,5},{2,6},{3,7},{4,0},{5,1},{6,2},{7,3},{8,12},{9,13},{10,... | collective-permute-start | bytes 6152 | tf_op jit(solution)/shard_map/ppermute | solution.py:21
  45.3 3.6 %collective-permute-start.17 = (f32[1,512]{1,0:T(1,128)S(1)}, f32[1,512]{1,0:T(1,128)S(1)}, u32[]{:S(2)}, u32[]{:S(2)}) collective-permute-start(f32[1,512]{1,0:T(1,128)S(1)} %add.21), channel_id=1, source_target_pairs={{0,2},{1,3},{2,0},{3,1},{4,6},{5,7},{6,4},{7,5},{8,10},{9,11},{10,... | collective-permute-start | bytes 6152 | tf_op jit(solution)/shard_map/ppermute | solution.py:21
  48.9 3.6 %collective-permute-start.18 = (f32[1,512]{1,0:T(1,128)S(1)}, f32[1,512]{1,0:T(1,128)S(1)}, u32[]{:S(2)}, u32[]{:S(2)}) collective-permute-start(f32[1,512]{1,0:T(1,128)S(1)} %add.22), channel_id=1, source_target_pairs={{0,1},{1,0},{2,3},{3,2},{4,5},{5,4},{6,7},{7,6},{8,9},{9,8},{10,11... | collective-permute-start | bytes 6152 | tf_op jit(solution)/shard_map/ppermute | solution.py:21

commit v2 on v1

--- a/solution.py
+++ b/solution.py
@@ -23,8 +23,10 @@
 
 def gather_xor(x, axis):
     held = {0: x}
-    for bit in bits_of(lax.axis_size(axis)):
-        held.update({m | bit: swap(v, axis, bit) for m, v in list(held.items())})
+    for m in sorted(range(1, lax.axis_size(axis)), key=lambda m: (m.bit_count(), -m)):
+        bits = [bit for bit in bits_of(lax.axis_size(axis)) if m & bit]
+        last = bits[min(1, len(bits) - 1)]
+        held[m] = swap(held[m ^ last], axis, last)
     return [held[m] for m in range(len(held))]
 
 
@@ -34,7 +36,18 @@
     return x
 
 
-def pack_kernel(flags_ref, weights_ref, packet_ref, sums_ref):
+def total_at_once(x, axis):
+    size = lax.axis_size(axis)
+    parts = lax.all_to_all(jnp.broadcast_to(x[None], (size,) + x.shape), axis, 0, 0)
+    return jnp.sum(parts, axis=0)
+
+
+def places_in(packet_ref, size):
+    meta = packet_ref[pl.ds(SLOTS * size, META), :].astype(jnp.float32)
+    return [jnp.max(meta[s : s + 1, :]).astype(jnp.int32) for s in range(SLOTS)]
+
+
+def pack_kernel(flags_ref, weights_ref, packet_ref):
     blk_rows, blk_cols = flags_ref.shape
     size = weights_ref.shape[0] // blk_rows
     blocks = blk_rows * blk_cols
@@ -44,7 +57,6 @@
     for b in range(blocks):
         slots.append(jnp.where(flags[b] == 1, ones, count + zeros))
         ones, zeros = ones + flags[b], zeros + (1 - flags[b])
-    sums_ref[...] = jnp.zeros_like(sums_ref)
     row_ids = lax.broadcasted_iota(jnp.int32, (META, size), 0)
     meta = jnp.zeros((META, size), jnp.float32)
     for s in range(SLOTS):
@@ -54,9 +66,19 @@
         block = weights_ref[pl.ds(row, size), pl.ds(col, size)]
         block = jnp.where(s < count, block, jnp.zeros_like(block))
         packet_ref[pl.ds(s * size, size), :] = block
-        sums_ref[:, pl.ds(col, size)] += jnp.sum(block.astype(jnp.float32), axis=0, keepdims=True)
         meta = jnp.where(row_ids == s, place.astype(jnp.float32), meta)
     packet_ref[pl.ds(SLOTS * size, META), :] = meta.astype(packet_ref.dtype)
+
+
+def sums_kernel(blk_cols, *refs):
+    *packet_refs, sums_ref = refs
+    size = packet_refs[0].shape[1]
+    sums_ref[...] = jnp.zeros_like(sums_ref)
+    for m, ref in enumerate(packet_refs):
+        for s, place in enumerate(places_in(ref, size)):
+            col = pl.multiple_of(place % blk_cols * size, size)
+            block = ref[pl.ds(s * size, size), :].astype(jnp.float32)
+            sums_ref[m : m + 1, pl.ds(col, size)] += jnp.sum(block, axis=0, keepdims=True)
 
 
 def expand_kernel(gr_size, gc_size, blk_rows, blk_cols, *refs):
@@ -67,16 +89,12 @@
     size = left.shape[0] // blk_rows
     my_col, my_row = lax.axis_index("gr"), lax.axis_index("gc")
 
-    def places(ref):
-        meta = ref[pl.ds(SLOTS * size, META), :].astype(jnp.float32)
-        return [jnp.max(meta[s : s + 1, :]).astype(jnp.int32) for s in range(SLOTS)]
-
     inverse = 1.0 / totals_ref[...]
     left[...] = jnp.zeros_like(left)
     right[...] = jnp.zeros_like(right)
     for m, ref in enumerate(left_refs):
         base = (my_col ^ m) * blk_cols
-        for s, place in enumerate(places(ref)):
+        for s, place in enumerate(places_in(ref, size)):
             row = pl.multiple_of(place // blk_cols * size, size)
             col = place % blk_cols
             scale = inverse[m : m + 1, :size]
@@ -87,7 +105,7 @@
             left[pl.ds(row, size), pl.ds(at, size)] = block.astype(left.dtype)
     for m, ref in enumerate(right_refs):
         base = (my_row ^ m) * blk_rows
-        for s, place in enumerate(places(ref)):
+        for s, place in enumerate(places_in(ref, size)):
             row = pl.multiple_of((base + place // blk_cols) * size, size)
             col = pl.multiple_of(place % blk_cols * size, size)
             right[pl.ds(row, size), pl.ds(col, size)] = ref[pl.ds(s * size, size), :]
@@ -111,19 +129,28 @@
     size = local_rows // blk_rows
     gr_size, gc_size = lax.axis_size("gr"), lax.axis_size("gc")
     order_size = local_rows * gc_size
-    packet, sums = pl.pallas_call(
+    small = pltpu.CompilerParams(vmem_limit_bytes=8 << 20)
+    packet = pl.pallas_call(
         pack_kernel,
-        out_shape=(
-            jax.ShapeDtypeStruct((SLOTS * size + META, size), weights.dtype),
-            jax.ShapeDtypeStruct((1, local_cols), jnp.float32),
-        ),
+        out_shape=jax.ShapeDtypeStruct((SLOTS * size + META, size), weights.dtype),
         in_specs=[SMEM, VMEM],
-        out_specs=(VMEM, VMEM),
+        out_specs=VMEM,
+        compiler_params=small,
         name="pack",
     )(in_pattern, weights)
-    totals = total_over(jnp.concatenate(gather_xor(sums, "gr"), axis=0), "gc")
+    right = gather_xor(packet, "gc")
     left = gather_xor(packet, "gr")
-    right = gather_xor(packet, "gc")
+    totals = pl.pallas_call(
+        functools.partial(sums_kernel, blk_cols),
+        out_shape=jax.ShapeDtypeStruct((2, local_cols), jnp.float32),
+        in_specs=[VMEM, VMEM],
+        out_specs=VMEM,
+        compiler_params=small,
+        name="sums",
+    )(*left[:2])
+    for bit in reversed(bits_of(gr_size)[:-1]):
+        totals = jnp.concatenate([totals, swap(totals, "gr", bit)], axis=0)
+    totals = total_over(totals, "gc")
     inflated, sums = pl.pallas_call(
         functools.partial(expand_kernel, gr_size, gc_size, blk_rows, blk_cols),
         out_shape=(
@@ -139,7 +166,7 @@
         compiler_params=pltpu.CompilerParams(vmem_limit_bytes=40 << 20),
         name="expand",
     )(out_pattern, totals, *left, *right)
-    output_total = total_over(sums, "gc")
+    output_total = total_at_once(sums, "gc")
     return (inflated / output_total * float(order_size)).astype(jnp.bfloat16)
 
 

time: 53.4 us -> 43.6 us (0.82)
  waiting for transfers between devices: 24.3 us -> 10.6 us
  blocking collectives: 0 us -> 10.4 us
  starting transfers between devices: 22.4 us -> 16.9 us
  Pallas kernels: 4.01 us -> 3.11 us
  other arithmetic: 1.56 us -> 0.82 us
  local copies, waits for them, and re-layouts: 0.92 us -> 1.64 us
    ppermute x19 -> x14, waiting for transfers between devices: 24.3 us -> 10.6 us  [swap(): lax.ppermute(x, axis, [(i, i ^ bit) for i in range(lax.axis_size(axis))])]
    all_to_all x0 -> x1, blocking collectives: none -> 10.4 us  [total_at_once(): lax.all_to_all(jnp.broadcast_to(x[None], (size,) + x.shape), axis, 0, 0)]
    ppermute x19 -> x14, starting transfers between devices: 22.4 us -> 16.9 us  [swap(): lax.ppermute(x, axis, [(i, i ^ bit) for i in range(lax.axis_size(axis))])]
    pallas_call x1 -> x2, Pallas kernels: 1.71 us -> 0.81 us  [the longest x1 0.65 us: shards(): pl.pallas_call(pack_kernel, out_shape=jax.ShapeDtypeStruct((SLOTS * size...]
    concatenate x1, other arithmetic: 0.75 us -> 0.01 us  [shards(): totals = jnp.concatenate([totals, swap(totals, 'gr', bit)], axis=0)]
    unnamed x6, local copies, waits for them, and re-layouts: 0.92 us -> 1.63 us
  transfers between devices with their start and end apart: 19 -> 14, of which waited for: 11 -> 6; matrix products, arithmetic and copies ran while one was open for 0% -> 0% of each run, Pallas kernels for 0% -> 0%
where the time goes in v2:
time: 43.6 us; the launch traced here: 43.4 us
  starting transfers between devices  16.9 us (39%)
  waiting for transfers between devices  10.6 us (24%)
  blocking collectives  10.4 us (24%)
  Pallas kernels  3.11 us (7%)
  local copies, waits for them, and re-layouts  1.64 us (4%)
  other arithmetic  0.82 us (2%)
    ppermute x14, starting transfers between devices, swap(): lax.ppermute(x, axis, [(i, i ^ bit) for i in range(lax.axis_size(axis))])  16.9 us
    ppermute x14, waiting for transfers between devices, swap(): lax.ppermute(x, axis, [(i, i ^ bit) for i in range(lax.axis_size(axis))])  10.6 us
    all_to_all x1, blocking collectives, total_at_once(): lax.all_to_all(jnp.broadcast_to(x[None], (size,) + x.shape), axis, 0, 0)  10.4 us
    pallas_call x1, Pallas kernels, shards(): pl.pallas_call(functools.partial(expand_kernel, gr_size, gc_size, blk_row...  2.3 us
    unnamed x6, local copies, waits for them, and re-layouts  1.63 us
  transfers between devices with their start and end apart: 14, of which 6 were waited for; matrix products, arithmetic and copies ran while one was open for 0% of the time, Pallas kernels for 0%

profile of v2, /device:TPU:0, one launch (start us, length us, event | category | flops | bytes accessed | tf_op | source)
XLA Modules:
  0.0 43.4 jit_solution(2434377351191554562)
XLA Ops:
  0.0 0.9 %copy-done = bf16[256,512]{1,0:T(8,128)(2,1)S(1)} copy-done((bf16[256,512]{1,0:T(8,128)(2,1)S(1)}, bf16[256,512]{1,0:T(8,128)(2,1)}, u32[]{:S(2)}) %copy-start) | copy-done | bytes 262168
  1.0 0.7 %copy-done.1 = s32[2,4]{1,0:T(2,128)S(1)} copy-done((s32[2,4]{1,0:T(2,128)S(1)}, s32[2,4]{1,0:T(2,128)}, u32[]{:S(2)}) %copy-start.1) | copy-done | bytes 56
  1.6 0.6 %pack.1.refs_0_.refs_2_.refs_6_ = bf16[528,128]{1,0:T(8,128)(2,1)S(1)} custom-call(s32[2,4]{1,0:T(2,128)S(1)} %copy-done.1, bf16[256,512]{1,0:T(8,128)(2,1)S(1)} %copy-done), custom_call_target="tpu_custom_call" | custom-call | tf_op jit(solution)/shard_map/pack/pallas_call | solution.py:133
  2.3 0.5 %collective-permute-start = (bf16[528,128]{1,0:T(8,128)(2,1)S(1)}, bf16[528,128]{1,0:T(8,128)(2,1)S(1)}, u32[]{:S(2)}, u32[]{:S(2)}) collective-permute-start(bf16[528,128]{1,0:T(8,128)(2,1)S(1)} %pack.1.refs_0_.refs_2_.refs_6_), channel_id=1, source_target_pairs={{0,8},{8,0},{16,24},{24,16},{1,9},{9,1},{17,25},{25,17},{2,10},{10... | collective-permute-start | bytes 405512 | tf_op jit(solution)/shard_map/ppermute | solution.py:21
  2.8 3.7 %collective-permute-start.10 = (bf16[528,128]{1,0:T(8,128)(2,1)S(1)}, bf16[528,128]{1,0:T(8,128)(2,1)S(1)}, u32[]{:S(2)}, u32[]{:S(2)}) collective-permute-start(bf16[528,128]{1,0:T(8,128)(2,1)S(1)} %pack.1.refs_0_.refs_2_.refs_6_), channel_id=1, source_target_pairs={{0,4},{1,5},{2,6},{3,7},{4,0},{5,1},{6,2},{7,3},{8,12},{9,13},{10,... | collective-permute-start | bytes 405512 | tf_op jit(solution)/shard_map/ppermute | solution.py:21
  6.6 1.6 %collective-permute-start.1 = (f32[2,512]{1,0:T(2,128)S(1)}, f32[2,512]{1,0:T(2,128)S(1)}, u32[]{:S(2)}, u32[]{:S(2)}) collective-permute-start(f32[2,512]{1,0:T(2,128)S(1)} %sums.1), channel_id=1, source_target_pairs={{0,16},{8,24},{16,0},{24,8},{1,17},{9,25},{17,1},{25,9},{2,18},{10... | collective-permute-start | bytes 12296 | tf_op jit(solution)/shard_map/ppermute | solution.py:21
  8.2 2.1 %collective-permute-done.1 = f32[2,512]{1,0:T(2,128)S(1)} collective-permute-done((f32[2,512]{1,0:T(2,128)S(1)}, f32[2,512]{1,0:T(2,128)S(1)}, u32[]{:S(2)}, u32[]{:S(2)}) %collective-permute-start.1) | collective-permute-done | bytes 4128 | tf_op jit(solution)/shard_map/ppermute | solution.py:21
  10.3 1.3 %collective-permute-start.2 = (f32[4,512]{1,0:T(4,128)S(1)}, f32[4,512]{1,0:T(4,128)S(1)}, u32[]{:S(2)}, u32[]{:S(2)}) collective-permute-start(f32[4,512]{1,0:T(4,128)S(1)} %pad_maximum_fusion), channel_id=1, source_target_pairs={{0,4},{1,5},{2,6},{3,7},{4,0},{5,1},{6,2},{7,3},{8,12},{9,13},{10,... | collective-permute-start | bytes 24584 | tf_op jit(solution)/shard_map/ppermute | solution.py:21
  11.7 1.6 %collective-permute-start.8 = (bf16[528,128]{1,0:T(8,128)(2,1)S(1)}, bf16[528,128]{1,0:T(8,128)(2,1)S(1)}, u32[]{:S(2)}, u32[]{:S(2)}) collective-permute-start(bf16[528,128]{1,0:T(8,128)(2,1)S(1)} %pack.1.refs_0_.refs_2_.refs_6_), channel_id=1, source_target_pairs={{0,2},{1,3},{2,0},{3,1},{4,6},{5,7},{6,4},{7,5},{8,10},{9,11},{10,... | collective-permute-start | bytes 405512 | tf_op jit(solution)/shard_map/ppermute | solution.py:21
  13.2 1.5 %collective-permute-start.5 = (bf16[528,128]{1,0:T(8,128)(2,1)S(1)}, bf16[528,128]{1,0:T(8,128)(2,1)S(1)}, u32[]{:S(2)}, u32[]{:S(2)}) collective-permute-start(bf16[528,128]{1,0:T(8,128)(2,1)S(1)} %pack.1.refs_0_.refs_2_.refs_6_), channel_id=1, source_target_pairs={{0,16},{8,24},{16,0},{24,8},{1,17},{9,25},{17,1},{25,9},{2,18},{10... | collective-permute-start | bytes 405512 | tf_op jit(solution)/shard_map/ppermute | solution.py:21
  14.8 1.5 %collective-permute-start.11 = (bf16[528,128]{1,0:T(8,128)(2,1)S(1)}, bf16[528,128]{1,0:T(8,128)(2,1)S(1)}, u32[]{:S(2)}, u32[]{:S(2)}) collective-permute-start(bf16[528,128]{1,0:T(8,128)(2,1)S(1)} %collective-permute-done.10.refs_10_), channel_id=1, source_target_pairs={{0,1},{1,0},{2,3},{3,2},{4,5},{5,4},{6,7},{7,6},{8,9},{9,8},{10,11... | collective-permute-start | bytes 405512 | tf_op jit(solution)/shard_map/ppermute | solution.py:21
  16.3 0.5 %collective-permute-start.3 = (f32[4,512]{1,0:T(4,128)S(1)}, f32[4,512]{1,0:T(4,128)S(1)}, u32[]{:S(2)}, u32[]{:S(2)}) collective-permute-start(f32[4,512]{1,0:T(4,128)S(1)} %fusion), channel_id=1, source_target_pairs={{0,2},{1,3},{2,0},{3,1},{4,6},{5,7},{6,4},{7,5},{8,10},{9,11},{10,... | collective-permute-start | bytes 24584 | tf_op jit(solution)/shard_map/ppermute | solution.py:21
  16.8 3.2 %collective-permute-done.3 = f32[4,512]{1,0:T(4,128)S(1)} collective-permute-done((f32[4,512]{1,0:T(4,128)S(1)}, f32[4,512]{1,0:T(4,128)S(1)}, u32[]{:S(2)}, u32[]{:S(2)}) %collective-permute-start.3) | collective-permute-done | bytes 8224 | tf_op jit(solution)/shard_map/ppermute | solution.py:21
  20.0 0.5 %collective-permute-start.4 = (f32[4,512]{1,0:T(4,128)S(1)}, f32[4,512]{1,0:T(4,128)S(1)}, u32[]{:S(2)}, u32[]{:S(2)}) collective-permute-start(f32[4,512]{1,0:T(4,128)S(1)} %add.10), channel_id=1, source_target_pairs={{0,1},{1,0},{2,3},{3,2},{4,5},{5,4},{6,7},{7,6},{8,9},{9,8},{10,11... | collective-permute-start | bytes 24584 | tf_op jit(solution)/shard_map/ppermute | solution.py:21
  20.5 1.5 %collective-permute-start.7 = (bf16[528,128]{1,0:T(8,128)(2,1)S(1)}, bf16[528,128]{1,0:T(8,128)(2,1)S(1)}, u32[]{:S(2)}, u32[]{:S(2)}) collective-permute-start(bf16[528,128]{1,0:T(8,128)(2,1)S(1)} %pack.1.refs_0_.refs_2_.refs_6_), channel_id=1, source_target_pairs={{0,1},{1,0},{2,3},{3,2},{4,5},{5,4},{6,7},{7,6},{8,9},{9,8},{10,11... | collective-permute-start | bytes 405512 | tf_op jit(solution)/shard_map/ppermute | solution.py:21
  22.0 0.5 %collective-permute-start.12 = (bf16[528,128]{1,0:T(8,128)(2,1)S(1)}, bf16[528,128]{1,0:T(8,128)(2,1)S(1)}, u32[]{:S(2)}, u32[]{:S(2)}) collective-permute-start(bf16[528,128]{1,0:T(8,128)(2,1)S(1)} %collective-permute-done.10.refs_10_), channel_id=1, source_target_pairs={{0,2},{1,3},{2,0},{3,1},{4,6},{5,7},{6,4},{7,5},{8,10},{9,11},{10,... | collective-permute-start | bytes 405512 | tf_op jit(solution)/shard_map/ppermute | solution.py:21
  22.5 1.3 %collective-permute-start.9 = (bf16[528,128]{1,0:T(8,128)(2,1)S(1)}, bf16[528,128]{1,0:T(8,128)(2,1)S(1)}, u32[]{:S(2)}, u32[]{:S(2)}) collective-permute-start(bf16[528,128]{1,0:T(8,128)(2,1)S(1)} %collective-permute-done.8.refs_8_), channel_id=1, source_target_pairs={{0,1},{1,0},{2,3},{3,2},{4,5},{5,4},{6,7},{7,6},{8,9},{9,8},{10,11... | collective-permute-start | bytes 405512 | tf_op jit(solution)/shard_map/ppermute | solution.py:21
  23.8 0.9 %collective-permute-start.13 = (bf16[528,128]{1,0:T(8,128)(2,1)S(1)}, bf16[528,128]{1,0:T(8,128)(2,1)S(1)}, u32[]{:S(2)}, u32[]{:S(2)}) collective-permute-start(bf16[528,128]{1,0:T(8,128)(2,1)S(1)} %collective-permute-done.11.refs_11_), channel_id=1, source_target_pairs={{0,2},{1,3},{2,0},{3,1},{4,6},{5,7},{6,4},{7,5},{8,10},{9,11},{10,... | collective-permute-start | bytes 405512 | tf_op jit(solution)/shard_map/ppermute | solution.py:21
  24.7 0.9 %collective-permute-done.7.refs_7_ = bf16[528,128]{1,0:T(8,128)(2,1)S(1)} collective-permute-done((bf16[528,128]{1,0:T(8,128)(2,1)S(1)}, bf16[528,128]{1,0:T(8,128)(2,1)S(1)}, u32[]{:S(2)}, u32[]{:S(2)}) %collective-permute-start.7) | collective-permute-done | bytes 135200 | tf_op jit(solution)/shard_map/ppermute | solution.py:21
  25.5 1.6 %collective-permute-done.12.refs_12_ = bf16[528,128]{1,0:T(8,128)(2,1)S(1)} collective-permute-done((bf16[528,128]{1,0:T(8,128)(2,1)S(1)}, bf16[528,128]{1,0:T(8,128)(2,1)S(1)}, u32[]{:S(2)}, u32[]{:S(2)}) %collective-permute-start.12) | collective-permute-done | bytes 135200 | tf_op jit(solution)/shard_map/ppermute | solution.py:21
  27.5 2.4 %collective-permute-done.13.refs_13_ = bf16[528,128]{1,0:T(8,128)(2,1)S(1)} collective-permute-done((bf16[528,128]{1,0:T(8,128)(2,1)S(1)}, bf16[528,128]{1,0:T(8,128)(2,1)S(1)}, u32[]{:S(2)}, u32[]{:S(2)}) %collective-permute-start.13) | collective-permute-done | bytes 135200 | tf_op jit(solution)/shard_map/ppermute | solution.py:21
  29.9 2.3 %expand.1 = (f32[256,512]{1,0:T(8,128)S(1)}, f32[1,512]{1,0:T(1,128)S(1)}) custom-call(s32[2,4]{1,0:T(2,128)S(1)} %copy-done.2, f32[4,512]{1,0:T(4,128)S(1)} %add.11.refs_1_, bf16[528,128]{1,0:T(8,128)(2,1)S(1)} %pack.1.refs_0_.refs_2_.refs_6_, bf16[528,128]{1,0:T(8,128)(2,1)S(1)} %collective-permute-done.refs_1_.refs_3_, ...), custom_call_target="tpu_custom_call" | custom-call | tf_op jit(solution)/shard_map/expand/pallas_call | solution.py:154
  32.3 10.4 %all_to_all.5 = f32[8,1,512]{2,1,0:T(1,128)S(1)} all-to-all(f32[8,1,512]{2,1,0:T(1,128)S(1)} %broadcast_in_dim.9), channel_id=1, replica_groups=mesh['gr'=4,'gc'=8] {'gc'}, dimensions={0} | all-to-all | bytes 32768 | tf_op jit(solution)/shard_map/all_to_all | solution.py:41
  42.7 0.8 %multiply_convert_fusion = bf16[256,512]{1,0:T(8,128)(2,1)} fusion(f32[256,512]{1,0:T(8,128)S(1)} %get-tuple-element.7, f32[512]{0:T(512)S(1)} %reduce_sum.9), kind=kLoop, calls=%fused_computation | loop fusion | flops 393216 | bytes 788480 | tf_op jit(solution)/shard_map/convert_element_type | solution.py:170
  (21 shorter events, 0.6 us)
Async XLA Ops:
  0.0 0.9 %copy-start = (bf16[256,512]{1,0:T(8,128)(2,1)S(1)}, bf16[256,512]{1,0:T(8,128)(2,1)}, u32[]{:S(2)}) copy-start(bf16[256,512]{1,0:T(8,128)(2,1)} %weights_ref.1) | copy-start | bytes 786436
  1.0 0.7 %copy-start.1 = (s32[2,4]{1,0:T(2,128)S(1)}, s32[2,4]{1,0:T(2,128)}, u32[]{:S(2)}) copy-start(s32[2,4]{1,0:T(2,128)} %flags_ref.1) | copy-start | bytes 100
  2.3 4.2 %collective-permute-start = (bf16[528,128]{1,0:T(8,128)(2,1)S(1)}, bf16[528,128]{1,0:T(8,128)(2,1)S(1)}, u32[]{:S(2)}, u32[]{:S(2)}) collective-permute-start(bf16[528,128]{1,0:T(8,128)(2,1)S(1)} %pack.1.refs_0_.refs_2_.refs_6_), channel_id=1, source_target_pairs={{0,8},{8,0},{16,24},{24,16},{1,9},{9,1},{17,25},{25,17},{2,10},{10... | collective-permute-start | bytes 405512 | tf_op jit(solution)/shard_map/ppermute | solution.py:21
  2.8 12.0 %collective-permute-start.10 = (bf16[528,128]{1,0:T(8,128)(2,1)S(1)}, bf16[528,128]{1,0:T(8,128)(2,1)S(1)}, u32[]{:S(2)}, u32[]{:S(2)}) collective-permute-start(bf16[528,128]{1,0:T(8,128)(2,1)S(1)} %pack.1.refs_0_.refs_2_.refs_6_), channel_id=1, source_target_pairs={{0,4},{1,5},{2,6},{3,7},{4,0},{5,1},{6,2},{7,3},{8,12},{9,13},{10,... | collective-permute-start | bytes 405512 | tf_op jit(solution)/shard_map/ppermute | solution.py:21
  6.6 3.7 %collective-permute-start.1 = (f32[2,512]{1,0:T(2,128)S(1)}, f32[2,512]{1,0:T(2,128)S(1)}, u32[]{:S(2)}, u32[]{:S(2)}) collective-permute-start(f32[2,512]{1,0:T(2,128)S(1)} %sums.1), channel_id=1, source_target_pairs={{0,16},{8,24},{16,0},{24,8},{1,17},{9,25},{17,1},{25,9},{2,18},{10... | collective-permute-start | bytes 12296 | tf_op jit(solution)/shard_map/ppermute | solution.py:21
  10.3 5.9 %collective-permute-start.2 = (f32[4,512]{1,0:T(4,128)S(1)}, f32[4,512]{1,0:T(4,128)S(1)}, u32[]{:S(2)}, u32[]{:S(2)}) collective-permute-start(f32[4,512]{1,0:T(4,128)S(1)} %pad_maximum_fusion), channel_id=1, source_target_pairs={{0,4},{1,5},{2,6},{3,7},{4,0},{5,1},{6,2},{7,3},{8,12},{9,13},{10,... | collective-permute-start | bytes 24584 | tf_op jit(solution)/shard_map/ppermute | solution.py:21
  11.7 10.4 %collective-permute-start.8 = (bf16[528,128]{1,0:T(8,128)(2,1)S(1)}, bf16[528,128]{1,0:T(8,128)(2,1)S(1)}, u32[]{:S(2)}, u32[]{:S(2)}) collective-permute-start(bf16[528,128]{1,0:T(8,128)(2,1)S(1)} %pack.1.refs_0_.refs_2_.refs_6_), channel_id=1, source_target_pairs={{0,2},{1,3},{2,0},{3,1},{4,6},{5,7},{6,4},{7,5},{8,10},{9,11},{10,... | collective-permute-start | bytes 405512 | tf_op jit(solution)/shard_map/ppermute | solution.py:21
  13.2 9.2 %collective-permute-start.5 = (bf16[528,128]{1,0:T(8,128)(2,1)S(1)}, bf16[528,128]{1,0:T(8,128)(2,1)S(1)}, u32[]{:S(2)}, u32[]{:S(2)}) collective-permute-start(bf16[528,128]{1,0:T(8,128)(2,1)S(1)} %pack.1.refs_0_.refs_2_.refs_6_), channel_id=1, source_target_pairs={{0,16},{8,24},{16,0},{24,8},{1,17},{9,25},{17,1},{25,9},{2,18},{10... | collective-permute-start | bytes 405512 | tf_op jit(solution)/shard_map/ppermute | solution.py:21
  14.8 9.0 %collective-permute-start.11 = (bf16[528,128]{1,0:T(8,128)(2,1)S(1)}, bf16[528,128]{1,0:T(8,128)(2,1)S(1)}, u32[]{:S(2)}, u32[]{:S(2)}) collective-permute-start(bf16[528,128]{1,0:T(8,128)(2,1)S(1)} %collective-permute-done.10.refs_10_), channel_id=1, source_target_pairs={{0,1},{1,0},{2,3},{3,2},{4,5},{5,4},{6,7},{7,6},{8,9},{9,8},{10,11... | collective-permute-start | bytes 405512 | tf_op jit(solution)/shard_map/ppermute | solution.py:21
  16.3 3.7 %collective-permute-start.3 = (f32[4,512]{1,0:T(4,128)S(1)}, f32[4,512]{1,0:T(4,128)S(1)}, u32[]{:S(2)}, u32[]{:S(2)}) collective-permute-start(f32[4,512]{1,0:T(4,128)S(1)} %fusion), channel_id=1, source_target_pairs={{0,2},{1,3},{2,0},{3,1},{4,6},{5,7},{6,4},{7,5},{8,10},{9,11},{10,... | collective-permute-start | bytes 24584 | tf_op jit(solution)/shard_map/ppermute | solution.py:21
  20.0 9.9 %copy-start.2 = (s32[2,4]{1,0:T(2,128)S(1)}, s32[2,4]{1,0:T(2,128)}, u32[]{:S(2)}) copy-start(s32[2,4]{1,0:T(2,128)} %refs_0_.1) | copy-start | bytes 100
  20.0 3.8 %collective-permute-start.4 = (f32[4,512]{1,0:T(4,128)S(1)}, f32[4,512]{1,0:T(4,128)S(1)}, u32[]{:S(2)}, u32[]{:S(2)}) collective-permute-start(f32[4,512]{1,0:T(4,128)S(1)} %add.10), channel_id=1, source_target_pairs={{0,1},{1,0},{2,3},{3,2},{4,5},{5,4},{6,7},{7,6},{8,9},{9,8},{10,11... | collective-permute-start | bytes 24584 | tf_op jit(solution)/shard_map/ppermute | solution.py:21
  20.5 5.0 %collective-permute-start.7 = (bf16[528,128]{1,0:T(8,128)(2,1)S(1)}, bf16[528,128]{1,0:T(8,128)(2,1)S(1)}, u32[]{:S(2)}, u32[]{:S(2)}) collective-permute-start(bf16[528,128]{1,0:T(8,128)(2,1)S(1)} %pack.1.refs_0_.refs_2_.refs_6_), channel_id=1, source_target_pairs={{0,1},{1,0},{2,3},{3,2},{4,5},{5,4},{6,7},{7,6},{8,9},{9,8},{10,11... | collective-permute-start | bytes 405512 | tf_op jit(solution)/shard_map/ppermute | solution.py:21
  22.0 5.1 %collective-permute-start.12 = (bf16[528,128]{1,0:T(8,128)(2,1)S(1)}, bf16[528,128]{1,0:T(8,128)(2,1)S(1)}, u32[]{:S(2)}, u32[]{:S(2)}) collective-permute-start(bf16[528,128]{1,0:T(8,128)(2,1)S(1)} %collective-permute-done.10.refs_10_), channel_id=1, source_target_pairs={{0,2},{1,3},{2,0},{3,1},{4,6},{5,7},{6,4},{7,5},{8,10},{9,11},{10,... | collective-permute-start | bytes 405512 | tf_op jit(solution)/shard_map/ppermute | solution.py:21
  22.5 5.0 %collective-permute-start.9 = (bf16[528,128]{1,0:T(8,128)(2,1)S(1)}, bf16[528,128]{1,0:T(8,128)(2,1)S(1)}, u32[]{:S(2)}, u32[]{:S(2)}) collective-permute-start(bf16[528,128]{1,0:T(8,128)(2,1)S(1)} %collective-permute-done.8.refs_8_), channel_id=1, source_target_pairs={{0,1},{1,0},{2,3},{3,2},{4,5},{5,4},{6,7},{7,6},{8,9},{9,8},{10,11... | collective-permute-start | bytes 405512 | tf_op jit(solution)/shard_map/ppermute | solution.py:21
  23.8 3.7 %collective-permute-start.6 = (bf16[528,128]{1,0:T(8,128)(2,1)S(1)}, bf16[528,128]{1,0:T(8,128)(2,1)S(1)}, u32[]{:S(2)}, u32[]{:S(2)}) collective-permute-start(bf16[528,128]{1,0:T(8,128)(2,1)S(1)} %collective-permute-done.5.refs_4_), channel_id=1, source_target_pairs={{0,8},{8,0},{16,24},{24,16},{1,9},{9,1},{17,25},{25,17},{2,10},{10... | collective-permute-start | bytes 405512 | tf_op jit(solution)/shard_map/ppermute | solution.py:21
  23.8 6.1 %collective-permute-start.13 = (bf16[528,128]{1,0:T(8,128)(2,1)S(1)}, bf16[528,128]{1,0:T(8,128)(2,1)S(1)}, u32[]{:S(2)}, u32[]{:S(2)}) collective-permute-start(bf16[528,128]{1,0:T(8,128)(2,1)S(1)} %collective-permute-done.11.refs_11_), channel_id=1, source_target_pairs={{0,2},{1,3},{2,0},{3,1},{4,6},{5,7},{6,4},{7,5},{8,10},{9,11},{10,... | collective-permute-start | bytes 405512 | tf_op jit(solution)/shard_map/ppermute | solution.py:21

commit v3 on v1

v3 whole, which is shorter than its diff:
```python
import functools

import jax
import jax.numpy as jnp
from jax import lax
from jax.experimental import pallas as pl
from jax.experimental.pallas import tpu as pltpu
from jax.sharding import PartitionSpec as P

SLOTS = 4
META = 16
VMEM = pl.BlockSpec(memory_space=pltpu.VMEM)
SMEM = pl.BlockSpec(memory_space=pltpu.SMEM)
HBM = pl.BlockSpec(memory_space=pltpu.HBM)
SMALL = pltpu.CompilerParams(vmem_limit_bytes=16 << 20)


def bits_of(size):
    return [1 << b for b in reversed(range(size.bit_length() - 1))]


def swap(x, axis, mask):
    return lax.ppermute(x, axis, [(i, i ^ mask) for i in range(lax.axis_size(axis))])


def in_hbm(x):
    return pltpu.with_memory_space_constraint(x, pltpu.HBM)


def way_to(mask, axis):
    full = lax.axis_size(axis) - 1
    if mask == full and mask.bit_count() > 2:
        return 1, mask ^ 1
    bits = [bit for bit in bits_of(full + 1) if mask & bit]
    last = bits[min(1, len(bits) - 1)]
    return mask ^ last, last


def total_at_once(x, axis):
    size = lax.axis_size(axis)
    parts = lax.all_to_all(jnp.broadcast_to(x[None], (size,) + x.shape), axis, 0, 0)
    return jnp.sum(parts, axis=0)


def places_in(packet_ref, size):
    meta = packet_ref[pl.ds(SLOTS * size, META), :].astype(jnp.float32)
    return [jnp.max(meta[s : s + 1, :]).astype(jnp.int32) for s in range(SLOTS)]


def add_sums(packet_ref, sums_ref, at, blk_cols):
    size = packet_ref.shape[1]
    for s, place in enumerate(places_in(packet_ref, size)):
        col = pl.multiple_of(place % blk_cols * size, size)
        block = packet_ref[pl.ds(s * size, size), :].astype(jnp.float32)
        sums_ref[at : at + 1, pl.ds(col, size)] += jnp.sum(block, axis=0, keepdims=True)


def pack_kernel(flags_hbm, weights_hbm, packet_ref, sums_ref, flags_ref, weights_ref, sems):
    copies = [
        pltpu.make_async_copy(flags_hbm, flags_ref, sems.at[0]),
        pltpu.make_async_copy(weights_hbm, weights_ref, sems.at[1]),
    ]
    for copy in copies:
        copy.start()
    for copy in copies:
        copy.wait()
    blk_rows, blk_cols = flags_ref.shape
    size = weights_ref.shape[0] // blk_rows
    blocks = blk_rows * blk_cols
    flags = [flags_ref[b // blk_cols, b % blk_cols] for b in range(blocks)]
    count = sum(flags)
    ones, zeros, slots = 0, 0, []
    for b in range(blocks):
        slots.append(jnp.where(flags[b] == 1, ones, count + zeros))
        ones, zeros = ones + flags[b], zeros + (1 - flags[b])
    sums_ref[...] = jnp.zeros_like(sums_ref)
    row_ids = lax.broadcasted_iota(jnp.int32, (META, size), 0)
    meta = jnp.zeros((META, size), jnp.float32)
    for s in range(SLOTS):
        place = sum(jnp.where(slots[b] == s, b, 0) for b in range(blocks))
        row = pl.multiple_of(place // blk_cols * size, size)
        col = pl.multiple_of(place % blk_cols * size, size)
        block = weights_ref[pl.ds(row, size), pl.ds(col, size)]
        block = jnp.where(s < count, block, jnp.zeros_like(block))
        packet_ref[0, pl.ds(s * size, size), :] = block
        sums_ref[:, pl.ds(col, size)] += jnp.sum(block.astype(jnp.float32), axis=0, keepdims=True)
        meta = jnp.where(row_ids == s, place.astype(jnp.float32), meta)
    packet_ref[0, pl.ds(SLOTS * size, META), :] = meta.astype(packet_ref.dtype)


def relay_kernel(blk_cols, held, routes, *refs):
    sent_refs, sums_ref = refs[-len(routes) - 1 : -1], refs[-1]
    sums_ref[...] = refs[0][...]
    for n in held:
        add_sums(refs[1 + n].at[0], sums_ref, 0, blk_cols)
    for sent_ref, route in zip(sent_refs, routes):
        for at, source in enumerate(route):
            sent_ref[at] = refs[1 + source][0]


def total_of_halves(sums):
    gr_size, gc_size = lax.axis_size("gr"), lax.axis_size("gc")
    groups = [
        [r * gc_size + c for r in range(gr_size) for c in (i, i ^ (gc_size - 1))]
        for i in range(gc_size // 2)
    ]
    parts = jnp.broadcast_to(sums[None], (2 * gr_size,) + sums.shape)
    parts = lax.all_to_all(parts, ("gr", "gc"), 0, 0, axis_index_groups=groups)
    return jnp.sum(parts.reshape(gr_size, 2, -1), axis=1)


def spread(blk_rows, blk_cols, left_refs, right_refs, left, right):
    size = left.shape[0] // blk_rows
    my_col, my_row = lax.axis_index("gr"), lax.axis_index("gc")
    for m, ref in left_refs.items():
        for s, place in enumerate(places_in(ref, size)):
            row = pl.multiple_of(place // blk_cols * size, size)
            at = pl.multiple_of(((my_col ^ m) * blk_cols + place % blk_cols) * size, size)
            left[pl.ds(row, size), pl.ds(at, size)] = ref[pl.ds(s * size, size), :]
    for m, ref in right_refs.items():
        base = (my_row ^ m) * blk_rows
        for s, place in enumerate(places_in(ref, size)):
            row = pl.multiple_of((base + place // blk_cols) * size, size)
            col = pl.multiple_of(place % blk_cols * size, size)
            right[pl.ds(row, size), pl.ds(col, size)] = ref[pl.ds(s * size, size), :]


def spread_kernel(blk_rows, blk_cols, left_at, right_at, *refs):
    left, right = refs[-2:]
    left[...] = jnp.zeros_like(left)
    right[...] = jnp.zeros_like(right)
    left_refs = {m: refs[n].at[at] for m, (n, at) in left_at.items()}
    right_refs = {m: refs[n].at[at] for m, (n, at) in right_at.items()}
    spread(blk_rows, blk_cols, left_refs, right_refs, left, right)


def expand_kernel(flags_hbm, totals_ref, left, right, inflated_ref, sums_ref, flags_ref, scaled, sem):
    copy = pltpu.make_async_copy(flags_hbm, flags_ref, sem)
    copy.start()
    blk_rows, blk_cols = flags_ref.shape
    size = left.shape[0] // blk_rows
    width = totals_ref.shape[1]
    inverse = 1.0 / totals_ref[...]
    for m in range(totals_ref.shape[0]):
        at = slice(m * width, (m + 1) * width)
        scaled[:, at] = (left[:, at].astype(jnp.float32) * inverse[m : m + 1]).astype(scaled.dtype)
    own = 1.0 / totals_ref[pl.ds(lax.axis_index("gr"), 1), :]
    product = jnp.dot(scaled[...], right[...], preferred_element_type=jnp.float32)
    copy.wait()
    for j in range(blk_cols):
        at = slice(j * size, (j + 1) * size)
        total = jnp.zeros((1, size), jnp.float32)
        for i in range(blk_rows):
            rows = slice(i * size, (i + 1) * size)
            kept = product[rows, at] * own[:, at]
            kept = kept * flags_ref[i, j].astype(jnp.float32)
            squared = kept * kept
            inflated_ref[rows, at] = squared
            total = total + jnp.sum(squared, axis=0, keepdims=True)
        sums_ref[:, at] = total


def shards(weights, in_pattern, out_pattern):
    blk_rows, blk_cols = in_pattern.shape
    local_rows, local_cols = weights.shape
    size = local_rows // blk_rows
    gr_size, gc_size = lax.axis_size("gr"), lax.axis_size("gc")
    order_size = local_rows * gc_size
    sums_shape = jax.ShapeDtypeStruct((1, local_cols), jnp.float32)
    packet, sums = pl.pallas_call(
        pack_kernel,
        out_shape=(jax.ShapeDtypeStruct((1, SLOTS * size + META, size), weights.dtype), sums_shape),
        in_specs=[HBM, HBM],
        out_specs=(VMEM, VMEM),
        scratch_shapes=[
            pltpu.SMEM(in_pattern.shape, in_pattern.dtype),
            pltpu.VMEM(weights.shape, weights.dtype),
            pltpu.SemaphoreType.DMA((2,)),
        ],
        compiler_params=SMALL,
        name="pack",
    )(in_hbm(in_pattern), in_hbm(weights))
    full = gc_size - 1
    arrays, right_at, left_at = [packet], {0: (0, 0)}, {0: (0, 0)}

    def keep(array, table, masks):
        arrays.append(array)
        table.update({m: (len(arrays) - 1, at) for at, m in enumerate(masks)})

    for bit in bits_of(gc_size):
        keep(swap(packet, "gc", bit), right_at, [bit])
    for bit in bits_of(gr_size)[:-1]:
        keep(swap(packet, "gr", bit), left_at, [bit])
    hops = {}
    later = [m for m in range(gc_size) if m not in right_at]
    for mask in later:
        if min(mask.bit_count(), max(2, full.bit_count() - 1)) == 2:
            parent, hop = way_to(mask, "gc")
            hops.setdefault(hop, []).append((mask, parent))
    evens = sorted(left_at)
    routes = [[right_at[parent][0] for _, parent in hop] for hop in hops.values()]
    routes.append([left_at[m][0] for m in evens])
    *sent, sums = pl.pallas_call(
        functools.partial(relay_kernel, blk_cols, range(1, len(right_at)), routes),
        out_shape=[jax.ShapeDtypeStruct((len(r),) + packet.shape[1:], packet.dtype) for r in routes]
        + [sums_shape],
        in_specs=[VMEM] * (1 + len(arrays)),
        out_specs=[VMEM] * (1 + len(routes)),
        compiler_params=SMALL,
        name="relay",
    )(sums, *arrays)
    for (hop, masks), buffer in zip(hops.items(), sent):
        keep(swap(buffer, "gc", hop), right_at, [m for m, _ in masks])
    keep(swap(sent[-1], "gr", 1), left_at, [m | 1 for m in evens])
    totals = total_of_halves(sums)
    left, right = pl.pallas_call(
        functools.partial(spread_kernel, blk_rows, blk_cols, left_at, right_at),
        out_shape=(
            jax.ShapeDtypeStruct((local_rows, order_size), weights.dtype),
            jax.ShapeDtypeStruct((order_size, local_cols), weights.dtype),
        ),
        in_specs=[VMEM] * len(arrays),
        out_specs=(VMEM, VMEM),
        compiler_params=SMALL,
        name="spread",
    )(*arrays)
    inflated, sums = pl.pallas_call(
        expand_kernel,
        out_shape=(jax.ShapeDtypeStruct(weights.shape, jnp.float32), sums_shape),
        in_specs=[HBM] + [VMEM] * 3,
        out_specs=(VMEM, VMEM),
        scratch_shapes=[
            pltpu.SMEM(out_pattern.shape, out_pattern.dtype),
            pltpu.VMEM((local_rows, order_size), weights.dtype),
            pltpu.SemaphoreType.DMA,
        ],
        compiler_params=SMALL,
        name="expand",
    )(in_hbm(out_pattern), totals, left, right)
    output_total = total_at_once(sums, "gc")
    return (inflated / output_total * float(order_size)).astype(jnp.bfloat16)


def solution(mesh):
    in_specs = (P("gc", "gr"), P("gc", "gr"), P("gc", "gr"))
    out_specs = P("gc", "gr")
    return jax.shard_map(shards, mesh=mesh, in_specs=in_specs, out_specs=out_specs, check_vma=False)
```

time: 53.4 us -> 40.9 us (0.77)
  waiting for transfers between devices: 24.3 us -> 3.5 us
  blocking collectives: 0 us -> 20.7 us
  starting transfers between devices: 22.4 us -> 12.2 us
  local copies, waits for them, and re-layouts: 0.92 us -> 0.03 us
  other arithmetic: 1.56 us -> 0.86 us
  Pallas kernels: 4.01 us -> 3.37 us
    ppermute x19 -> x8, waiting for transfers between devices: 24.3 us -> 3.5 us  [swap(): lax.ppermute(x, axis, [(i, i ^ mask) for i in range(lax.axis_size(axis))])]
    all_to_all x0 -> x2, blocking collectives: none -> 20.7 us  [the longest x1 11.7 us: total_of_halves(): parts = lax.all_to_all(parts, ('gr', 'gc'), 0, 0, axis_index_groups=groups)]
    ppermute x19 -> x8, starting transfers between devices: 22.4 us -> 12.2 us  [swap(): lax.ppermute(x, axis, [(i, i ^ mask) for i in range(lax.axis_size(axis))])]
    unnamed x6 -> x0, local copies, waits for them, and re-layouts: 0.92 us -> none
    concatenate x1 -> x0, other arithmetic: 0.75 us -> none  [shards(): totals = total_over(jnp.concatenate(gather_xor(sums, 'gr'), axis=0), 'gc')]
    pallas_call x2 -> x4, Pallas kernels: 4.01 us -> 3.37 us  [the longest x1 1.35 us: shards(): pl.pallas_call(expand_kernel, out_shape=(jax.ShapeDtypeStruct(weights.sha...]
  transfers between devices with their start and end apart: 19 -> 8, of which waited for: 11 -> 3; matrix products, arithmetic and copies ran while one was open for 0% -> 0% of each run, Pallas kernels for 0% -> 0%
where the time goes in v3:
time: 40.9 us; the launch traced here: 40.7 us
  blocking collectives  20.7 us (51%)
  starting transfers between devices  12.2 us (30%)
  waiting for transfers between devices  3.5 us (9%)
  Pallas kernels  3.37 us (8%)
  other arithmetic  0.86 us (2%)
    ppermute x8, starting transfers between devices, swap(): lax.ppermute(x, axis, [(i, i ^ mask) for i in range(lax.axis_size(axis))])  12.2 us
    all_to_all x1, blocking collectives, total_of_halves(): parts = lax.all_to_all(parts, ('gr', 'gc'), 0, 0, axis_index_groups=groups)  11.7 us
    all_to_all x1, blocking collectives, total_at_once(): lax.all_to_all(jnp.broadcast_to(x[None], (size,) + x.shape), axis, 0, 0)  8.94 us
    ppermute x8, waiting for transfers between devices, swap(): lax.ppermute(x, axis, [(i, i ^ mask) for i in range(lax.axis_size(axis))])  3.5 us
    pallas_call x1, Pallas kernels, shards(): pl.pallas_call(expand_kernel, out_shape=(jax.ShapeDtypeStruct(weights.sha...  1.35 us
    pallas_call x1, Pallas kernels, shards(): pl.pallas_call(pack_kernel, out_shape=(jax.ShapeDtypeStruct((1, SLOTS * s...  1.05 us
  transfers between devices with their start and end apart: 8, of which 3 were waited for; matrix products, arithmetic and copies ran while one was open for 0% of the time, Pallas kernels for 0%

profile of v3, /device:TPU:0, one launch (start us, length us, event | category | flops | bytes accessed | tf_op | source)
XLA Modules:
  0.0 40.7 jit_solution(11792659776046742774)
XLA Ops:
  0.0 1.1 %pack.1 = (bf16[1,528,128]{2,1,0:T(8,128)(2,1)S(1)}, f32[1,512]{1,0:T(1,128)S(1)}) custom-call(s32[2,4]{1,0:T(2,128)} %flags_hbm.2, bf16[256,512]{1,0:T(8,128)(2,1)} %weights_hbm.1), custom_call_target="tpu_custom_call" | custom-call | tf_op jit(solution)/shard_map/pack/pallas_call | solution.py:170
  1.1 4.1 %collective-permute-start = (bf16[1,528,128]{2,1,0:T(8,128)(2,1)S(1)}, bf16[1,528,128]{2,1,0:T(8,128)(2,1)S(1)}, u32[]{:S(2)}, u32[]{:S(2)}) collective-permute-start(bf16[1,528,128]{2,1,0:T(8,128)(2,1)S(1)} %get-tuple-element.17.refs_1_.refs_0_), channel_id=1, source_target_pairs={{0,4},{1,5},{2,6},{3,7},{4,0},{5,1},{6,2},{7,3},{8,12},{9,13},{10,... | collective-permute-start | bytes 405512 | tf_op jit(solution)/shard_map/ppermute | solution.py:23
  5.2 1.6 %collective-permute-start.1 = (bf16[1,528,128]{2,1,0:T(8,128)(2,1)S(1)}, bf16[1,528,128]{2,1,0:T(8,128)(2,1)S(1)}, u32[]{:S(2)}, u32[]{:S(2)}) collective-permute-start(bf16[1,528,128]{2,1,0:T(8,128)(2,1)S(1)} %get-tuple-element.17.refs_1_.refs_0_), channel_id=1, source_target_pairs={{0,2},{1,3},{2,0},{3,1},{4,6},{5,7},{6,4},{7,5},{8,10},{9,11},{10,... | collective-permute-start | bytes 405512 | tf_op jit(solution)/shard_map/ppermute | solution.py:23
  6.7 1.5 %collective-permute-start.2 = (bf16[1,528,128]{2,1,0:T(8,128)(2,1)S(1)}, bf16[1,528,128]{2,1,0:T(8,128)(2,1)S(1)}, u32[]{:S(2)}, u32[]{:S(2)}) collective-permute-start(bf16[1,528,128]{2,1,0:T(8,128)(2,1)S(1)} %get-tuple-element.17.refs_1_.refs_0_), channel_id=1, source_target_pairs={{0,1},{1,0},{2,3},{3,2},{4,5},{5,4},{6,7},{7,6},{8,9},{9,8},{10,11... | collective-permute-start | bytes 405512 | tf_op jit(solution)/shard_map/ppermute | solution.py:23
  8.2 1.5 %collective-permute-start.3 = (bf16[1,528,128]{2,1,0:T(8,128)(2,1)S(1)}, bf16[1,528,128]{2,1,0:T(8,128)(2,1)S(1)}, u32[]{:S(2)}, u32[]{:S(2)}) collective-permute-start(bf16[1,528,128]{2,1,0:T(8,128)(2,1)S(1)} %get-tuple-element.17.refs_1_.refs_0_), channel_id=1, source_target_pairs={{0,16},{8,24},{16,0},{24,8},{1,17},{9,25},{17,1},{25,9},{2,18},{10... | collective-permute-start | bytes 405512 | tf_op jit(solution)/shard_map/ppermute | solution.py:23
  9.8 2.0 %collective-permute-done.refs_2_.refs_1_ = bf16[1,528,128]{2,1,0:T(8,128)(2,1)S(1)} collective-permute-done((bf16[1,528,128]{2,1,0:T(8,128)(2,1)S(1)}, bf16[1,528,128]{2,1,0:T(8,128)(2,1)S(1)}, u32[]{:S(2)}, u32[]{:S(2)}) %collective-permute-start) | collective-permute-done | bytes 135200 | tf_op jit(solution)/shard_map/ppermute | solution.py:23
  11.8 0.2 collective-permute-done.1.refs_3_.refs_2_
  11.9 0.0 collective-permute-done.2.refs_4_.refs_3_
  11.9 1.3 %collective-permute-done.3.refs_5_.refs_4_ = bf16[1,528,128]{2,1,0:T(8,128)(2,1)S(1)} collective-permute-done((bf16[1,528,128]{2,1,0:T(8,128)(2,1)S(1)}, bf16[1,528,128]{2,1,0:T(8,128)(2,1)S(1)}, u32[]{:S(2)}, u32[]{:S(2)}) %collective-permute-start.3) | collective-permute-done | bytes 135200 | tf_op jit(solution)/shard_map/ppermute | solution.py:23
  13.2 0.2 relay.1
  13.5 0.6 %collective-permute-start.4 = (bf16[2,528,128]{2,1,0:T(8,128)(2,1)S(1)}, bf16[2,528,128]{2,1,0:T(8,128)(2,1)S(1)}, u32[]{:S(2)}, u32[]{:S(2)}) collective-permute-start(bf16[2,528,128]{2,1,0:T(8,128)(2,1)S(1)} %get-tuple-element.19), channel_id=1, source_target_pairs={{0,1},{1,0},{2,3},{3,2},{4,5},{5,4},{6,7},{7,6},{8,9},{9,8},{10,11... | collective-permute-start | bytes 811016 | tf_op jit(solution)/shard_map/ppermute | solution.py:23
  14.1 0.0 collective-permute-start.7
  14.1 1.1 %collective-permute-start.5 = (bf16[1,528,128]{2,1,0:T(8,128)(2,1)S(1)}, bf16[1,528,128]{2,1,0:T(8,128)(2,1)S(1)}, u32[]{:S(2)}, u32[]{:S(2)}) collective-permute-start(bf16[1,528,128]{2,1,0:T(8,128)(2,1)S(1)} %get-tuple-element.20), channel_id=1, source_target_pairs={{0,2},{1,3},{2,0},{3,1},{4,6},{5,7},{6,4},{7,5},{8,10},{9,11},{10,... | collective-permute-start | bytes 405512 | tf_op jit(solution)/shard_map/ppermute | solution.py:23
  15.2 1.8 %collective-permute-start.6 = (bf16[1,528,128]{2,1,0:T(8,128)(2,1)S(1)}, bf16[1,528,128]{2,1,0:T(8,128)(2,1)S(1)}, u32[]{:S(2)}, u32[]{:S(2)}) collective-permute-start(bf16[1,528,128]{2,1,0:T(8,128)(2,1)S(1)} %get-tuple-element.21), channel_id=1, source_target_pairs={{0,6},{1,7},{2,4},{3,5},{4,2},{5,3},{6,0},{7,1},{8,14},{9,15},{10,... | collective-permute-start | bytes 405512 | tf_op jit(solution)/shard_map/ppermute | solution.py:23
  17.0 11.7 %all_to_all.10 = f32[8,1,512]{2,1,0:T(1,128)S(1)} all-to-all(f32[8,1,512]{2,1,0:T(1,128)S(1)} %broadcast_in_dim.17), channel_id=1, replica_groups={{0,7,8,15,16,23,24,31},{1,6,9,14,17,22,25,30},{2,5,10,13,18,21,26,29},{..., dimensions={0} | all-to-all | bytes 32768 | tf_op jit(solution)/shard_map/all_to_all | solution.py:108
  28.8 0.0 collective-permute-done.5.refs_6_
  28.8 0.0 collective-permute-done.6.refs_7_
  28.8 0.0 collective-permute-done.4.refs_5_
  28.8 0.0 collective-permute-done.7.refs_8_
  28.9 0.8 %spread.1 = (bf16[256,2048]{1,0:T(8,128)(2,1)S(1)}, bf16[2048,512]{1,0:T(8,128)(2,1)S(1)}) custom-call(bf16[1,528,128]{2,1,0:T(8,128)(2,1)S(1)} %get-tuple-element.17.refs_1_.refs_0_, bf16[1,528,128]{2,1,0:T(8,128)(2,1)S(1)} %collective-permute-done.refs_2_.refs_1_, bf16[1,528,128]{2,1,0:T(8,128)(2,1)S(1)} %collective-permute-done.1.refs_3_.refs_2_, ...), custom_call_target="tpu_custom_call" | custom-call | tf_op jit(solution)/shard_map/spread/pallas_call | solution.py:216
  29.6 1.3 %expand.1 = (f32[256,512]{1,0:T(8,128)S(1)}, f32[1,512]{1,0:T(1,128)S(1)}) custom-call(s32[2,4]{1,0:T(2,128)} %flags_hbm.3, f32[4,512]{1,0:T(4,128)S(1)} %reduce_sum.18.totals_ref, bf16[256,2048]{1,0:T(8,128)(2,1)S(1)} %get-tuple-element.23.left, bf16[2048,512]{1,0:T(8,128)(2,1)S(1)} %get-tuple-element.24.right), custom_call_target="tpu_custom_call" | custom-call | tf_op jit(solution)/shard_map/expand/pallas_call | solution.py:227
  31.0 8.9 %all_to_all.11 = f32[8,1,512]{2,1,0:T(1,128)S(1)} all-to-all(f32[8,1,512]{2,1,0:T(1,128)S(1)} %broadcast_in_dim.19), channel_id=1, replica_groups=mesh['gr'=4,'gc'=8] {'gc'}, dimensions={0} | all-to-all | bytes 32768 | tf_op jit(solution)/shard_map/all_to_all | solution.py:41
  40.0 0.8 %multiply_convert_fusion = bf16[256,512]{1,0:T(8,128)(2,1)} fusion(f32[256,512]{1,0:T(8,128)S(1)} %get-tuple-element.25, f32[512]{0:T(512)S(1)} %reduce_sum.19), kind=kLoop, calls=%fused_computation | loop fusion | flops 393216 | bytes 788480 | tf_op jit(solution)/shard_map/convert_element_type | solution.py:241
  (6 shorter events, 0.1 us)
Async XLA Ops:
  1.1 10.7 %collective-permute-start = (bf16[1,528,128]{2,1,0:T(8,128)(2,1)S(1)}, bf16[1,528,128]{2,1,0:T(8,128)(2,1)S(1)}, u32[]{:S(2)}, u32[]{:S(2)}) collective-permute-start(bf16[1,528,128]{2,1,0:T(8,128)(2,1)S(1)} %get-tuple-element.17.refs_1_.refs_0_), channel_id=1, source_target_pairs={{0,4},{1,5},{2,6},{3,7},{4,0},{5,1},{6,2},{7,3},{8,12},{9,13},{10,... | collective-permute-start | bytes 405512 | tf_op jit(solution)/shard_map/ppermute | solution.py:23
  5.2 6.8 %collective-permute-start.1 = (bf16[1,528,128]{2,1,0:T(8,128)(2,1)S(1)}, bf16[1,528,128]{2,1,0:T(8,128)(2,1)S(1)}, u32[]{:S(2)}, u32[]{:S(2)}) collective-permute-start(bf16[1,528,128]{2,1,0:T(8,128)(2,1)S(1)} %get-tuple-element.17.refs_1_.refs_0_), channel_id=1, source_target_pairs={{0,2},{1,3},{2,0},{3,1},{4,6},{5,7},{6,4},{7,5},{8,10},{9,11},{10,... | collective-permute-start | bytes 405512 | tf_op jit(solution)/shard_map/ppermute | solution.py:23
  6.7 5.2 %collective-permute-start.2 = (bf16[1,528,128]{2,1,0:T(8,128)(2,1)S(1)}, bf16[1,528,128]{2,1,0:T(8,128)(2,1)S(1)}, u32[]{:S(2)}, u32[]{:S(2)}) collective-permute-start(bf16[1,528,128]{2,1,0:T(8,128)(2,1)S(1)} %get-tuple-element.17.refs_1_.refs_0_), channel_id=1, source_target_pairs={{0,1},{1,0},{2,3},{3,2},{4,5},{5,4},{6,7},{7,6},{8,9},{9,8},{10,11... | collective-permute-start | bytes 405512 | tf_op jit(solution)/shard_map/ppermute | solution.py:23
  8.2 5.0 %collective-permute-start.3 = (bf16[1,528,128]{2,1,0:T(8,128)(2,1)S(1)}, bf16[1,528,128]{2,1,0:T(8,128)(2,1)S(1)}, u32[]{:S(2)}, u32[]{:S(2)}) collective-permute-start(bf16[1,528,128]{2,1,0:T(8,128)(2,1)S(1)} %get-tuple-element.17.refs_1_.refs_0_), channel_id=1, source_target_pairs={{0,16},{8,24},{16,0},{24,8},{1,17},{9,25},{17,1},{25,9},{2,18},{10... | collective-permute-start | bytes 405512 | tf_op jit(solution)/shard_map/ppermute | solution.py:23
  13.5 15.4 %collective-permute-start.4 = (bf16[2,528,128]{2,1,0:T(8,128)(2,1)S(1)}, bf16[2,528,128]{2,1,0:T(8,128)(2,1)S(1)}, u32[]{:S(2)}, u32[]{:S(2)}) collective-permute-start(bf16[2,528,128]{2,1,0:T(8,128)(2,1)S(1)} %get-tuple-element.19), channel_id=1, source_target_pairs={{0,1},{1,0},{2,3},{3,2},{4,5},{5,4},{6,7},{7,6},{8,9},{9,8},{10,11... | collective-permute-start | bytes 811016 | tf_op jit(solution)/shard_map/ppermute | solution.py:23
  14.1 14.8 %collective-permute-start.7 = (bf16[2,528,128]{2,1,0:T(8,128)(2,1)S(1)}, bf16[2,528,128]{2,1,0:T(8,128)(2,1)S(1)}, u32[]{:S(2)}, u32[]{:S(2)}) collective-permute-start(bf16[2,528,128]{2,1,0:T(8,128)(2,1)S(1)} %get-tuple-element.22), channel_id=1, source_target_pairs={{0,8},{8,0},{16,24},{24,16},{1,9},{9,1},{17,25},{25,17},{2,10},{10... | collective-permute-start | bytes 811016 | tf_op jit(solution)/shard_map/ppermute | solution.py:23
  14.1 14.7 %collective-permute-start.5 = (bf16[1,528,128]{2,1,0:T(8,128)(2,1)S(1)}, bf16[1,528,128]{2,1,0:T(8,128)(2,1)S(1)}, u32[]{:S(2)}, u32[]{:S(2)}) collective-permute-start(bf16[1,528,128]{2,1,0:T(8,128)(2,1)S(1)} %get-tuple-element.20), channel_id=1, source_target_pairs={{0,2},{1,3},{2,0},{3,1},{4,6},{5,7},{6,4},{7,5},{8,10},{9,11},{10,... | collective-permute-start | bytes 405512 | tf_op jit(solution)/shard_map/ppermute | solution.py:23
  15.2 13.6 %collective-permute-start.6 = (bf16[1,528,128]{2,1,0:T(8,128)(2,1)S(1)}, bf16[1,528,128]{2,1,0:T(8,128)(2,1)S(1)}, u32[]{:S(2)}, u32[]{:S(2)}) collective-permute-start(bf16[1,528,128]{2,1,0:T(8,128)(2,1)S(1)} %get-tuple-element.21), channel_id=1, source_target_pairs={{0,6},{1,7},{2,4},{3,5},{4,2},{5,3},{6,0},{7,1},{8,14},{9,15},{10,... | collective-permute-start | bytes 405512 | tf_op jit(solution)/shard_map/ppermute | solution.py:23

commit v4 on v3

v4 whole, which is shorter than its diff:
```python
import functools

import jax
import jax.numpy as jnp
from jax import lax
from jax.experimental import pallas as pl
from jax.experimental.pallas import tpu as pltpu
from jax.sharding import PartitionSpec as P

SLOTS = 4
META = 16
VMEM = pl.BlockSpec(memory_space=pltpu.VMEM)
HBM = pl.BlockSpec(memory_space=pltpu.HBM)
PARAMS = pltpu.CompilerParams(vmem_limit_bytes=16 << 20)
LONG = pl.CostEstimate(flops=10**10, bytes_accessed=0, transcendentals=0)


def in_hbm(x):
    return pltpu.with_memory_space_constraint(x, pltpu.HBM)


def bits_of(size):
    return [1 << b for b in reversed(range(size.bit_length() - 1))]


def swap(x, axis, mask):
    return lax.ppermute(x, axis, [(i, i ^ mask) for i in range(lax.axis_size(axis))])


def way_to(mask, axis):
    full = lax.axis_size(axis) - 1
    if mask == full and mask.bit_count() > 2:
        return 1, mask ^ 1
    bits = [bit for bit in bits_of(full + 1) if mask & bit]
    last = bits[min(1, len(bits) - 1)]
    return mask ^ last, last


def total_at_once(x, axis):
    size = lax.axis_size(axis)
    parts = lax.all_to_all(jnp.broadcast_to(x[None], (size,) + x.shape), axis, 0, 0)
    return jnp.sum(parts, axis=0)


def places_in(packet, size):
    meta = packet[pl.ds(SLOTS * size, META), :].astype(jnp.float32)
    return [jnp.max(meta[s : s + 1, :]).astype(jnp.int32) for s in range(SLOTS)]


def pack_kernel(flags_hbm, weights_hbm, packet_ref, sums_ref, flags_ref, weights_ref, sems):
    copies = [
        pltpu.make_async_copy(flags_hbm, flags_ref, sems.at[0]),
        pltpu.make_async_copy(weights_hbm, weights_ref, sems.at[1]),
    ]
    for copy in copies:
        copy.start()
    for copy in copies:
        copy.wait()
    blk_rows, blk_cols = flags_ref.shape
    size = weights_ref.shape[0] // blk_rows
    blocks = blk_rows * blk_cols
    flags = [flags_ref[b // blk_cols, b % blk_cols] for b in range(blocks)]
    count = sum(flags)
    ones, zeros, slots = 0, 0, []
    for b in range(blocks):
        slots.append(jnp.where(flags[b] == 1, ones, count + zeros))
        ones, zeros = ones + flags[b], zeros + (1 - flags[b])
    sums_ref[...] = jnp.zeros_like(sums_ref)
    row_ids = lax.broadcasted_iota(jnp.int32, (META, size), 0)
    meta = jnp.zeros((META, size), jnp.float32)
    for s in range(SLOTS):
        place = sum(jnp.where(slots[b] == s, b, 0) for b in range(blocks))
        row = pl.multiple_of(place // blk_cols * size, size)
        col = pl.multiple_of(place % blk_cols * size, size)
        block = weights_ref[pl.ds(row, size), pl.ds(col, size)]
        block = jnp.where(s < count, block, jnp.zeros_like(block))
        packet_ref[pl.ds(s * size, size), :] = block
        sums_ref[:, pl.ds(col, size)] += jnp.sum(block.astype(jnp.float32), axis=0, keepdims=True)
        meta = jnp.where(row_ids == s, place.astype(jnp.float32), meta)
    packet_ref[pl.ds(SLOTS * size, META), :] = meta.astype(packet_ref.dtype)


def rows_of(sums_ref):
    size = 128
    parts = [
        sums_ref[r : r + 1, at : at + size]
        for r in range(sums_ref.shape[0])
        for at in range(0, sums_ref.shape[1], size)
    ]
    return jnp.concatenate(parts, axis=0)


def split(x):
    high = x.astype(jnp.bfloat16)
    return high, (x - high.astype(jnp.float32)).astype(jnp.bfloat16)


def add_kernel(one_ref, other_ref, out_ref):
    out_ref[...] = one_ref[...] + other_ref[...]


def relay_kernel(routes, riding, sums_ref, *refs):
    packet_refs, sent_refs = refs[: -len(routes)], refs[-len(routes) :]
    rows = packet_refs[0].shape[0]
    if riding:
        high, low = split(rows_of(sums_ref))
    for sent_ref, (route, rider) in zip(sent_refs, routes):
        for at, source in enumerate(route):
            sent_ref[pl.ds(at * rows, rows), :] = packet_refs[source][...]
        if rider:
            first = len(route) * rows
            sent_ref[pl.ds(first, high.shape[0]), :] = high
            sent_ref[pl.ds(first + high.shape[0], high.shape[0]), :] = low


def spread(blk_rows, blk_cols, size, packets, right):
    my_row = lax.axis_index("gc")
    for m, packet in packets.items():
        base = (my_row ^ m) * blk_rows
        for s, place in enumerate(places_in(packet, size)):
            row = pl.multiple_of((base + place // blk_cols) * size, size)
            col = pl.multiple_of(place % blk_cols * size, size)
            right[pl.ds(row, size), pl.ds(col, size)] = packet[pl.ds(s * size, size), :]


def packets_in(refs, table, rows):
    return {m: refs[n].at[pl.ds(at * rows, rows), :] for m, (n, at) in table.items()}


def spread_kernel(blk_rows, blk_cols, evens, right_at, lefts_ref, *refs):
    *refs, right, left = refs
    rows, size = refs[0].shape
    right[...] = jnp.zeros_like(right)
    left[...] = jnp.zeros_like(left)
    spread(blk_rows, blk_cols, size, packets_in(refs, right_at, rows), right)
    my_col = lax.axis_index("gr")
    for n in range(lefts_ref.shape[0] // rows):
        packet = lefts_ref.at[pl.ds(n * rows, rows), :]
        gr = my_col // 2 * 2 + n // len(evens) ^ evens[n % len(evens)]
        for s, place in enumerate(places_in(packet, size)):
            row = pl.multiple_of(place // blk_cols * size, size)
            at = pl.multiple_of((gr * blk_cols + place % blk_cols) * size, size)
            left[pl.ds(row, size), pl.ds(at, size)] = packet[pl.ds(s * size, size), :]


def expand_kernel(right_at, riders, flags_hbm, sums_ref, left, *refs):
    *refs, _, inflated_ref, total_ref, right, flags_ref, scaled, sem = refs
    copy = pltpu.make_async_copy(flags_hbm, flags_ref, sem)
    copy.start()
    blk_rows, blk_cols = flags_ref.shape
    rows, size = refs[0].shape
    spread(blk_rows, blk_cols, size, packets_in(refs, right_at, rows), right)
    sums = rows_of(sums_ref)
    for n, at in riders:
        high = refs[n][pl.ds(at * rows, sums.shape[0]), :].astype(jnp.float32)
        low = refs[n][pl.ds(at * rows + sums.shape[0], sums.shape[0]), :].astype(jnp.float32)
        sums = sums + (high + low)
    inverse = 1.0 / sums
    for n in range(sums.shape[0]):
        at = slice(n * size, (n + 1) * size)
        scaled[:, at] = (left[:, at].astype(jnp.float32) * inverse[n : n + 1]).astype(scaled.dtype)
    product = jnp.dot(scaled[...], right[...], preferred_element_type=jnp.float32)
    copy.wait()
    my_col = lax.axis_index("gr")
    for j in range(blk_cols):
        at = slice(j * size, (j + 1) * size)
        own = inverse[j : j + 1]
        for r in range(1, sums.shape[0] // blk_cols):
            own = jnp.where(my_col == r, inverse[r * blk_cols + j : r * blk_cols + j + 1], own)
        total = jnp.zeros((1, size), jnp.float32)
        for i in range(blk_rows):
            rows_at = slice(i * size, (i + 1) * size)
            kept = product[rows_at, at] * own
            kept = kept * flags_ref[i, j].astype(jnp.float32)
            squared = kept * kept
            inflated_ref[rows_at, at] = squared
            total = total + jnp.sum(squared, axis=0, keepdims=True)
        total_ref[:, at] = total


def shards(weights, in_pattern, out_pattern):
    blk_rows, blk_cols = in_pattern.shape
    local_rows, local_cols = weights.shape
    size = local_rows // blk_rows
    gr_size, gc_size = lax.axis_size("gr"), lax.axis_size("gc")
    order_size = local_rows * gc_size
    sums_shape = jax.ShapeDtypeStruct((1, local_cols), jnp.float32)
    rows = SLOTS * size + META
    packet, sums = pl.pallas_call(
        pack_kernel,
        out_shape=(jax.ShapeDtypeStruct((rows, size), weights.dtype), sums_shape),
        in_specs=[HBM, HBM],
        out_specs=(VMEM, VMEM),
        scratch_shapes=[
            pltpu.SMEM(in_pattern.shape, in_pattern.dtype),
            pltpu.VMEM(weights.shape, weights.dtype),
            pltpu.SemaphoreType.DMA((2,)),
        ],
        compiler_params=PARAMS,
        name="pack",
    )(in_hbm(in_pattern), in_hbm(weights))

    arrays, right_at, evens = [packet], {0: (0, 0)}, {0: 0}

    def keep(array, masks):
        arrays.append(array)
        right_at.update({m: (len(arrays) - 1, at) for at, m in enumerate(masks)})

    riding = gc_size == 8
    if riding:
        sums = pl.pallas_call(
            add_kernel,
            out_shape=sums_shape,
            in_specs=[VMEM] * 2,
            out_specs=VMEM,
            compiler_params=PARAMS,
            cost_estimate=LONG,
            name="add",
        )(sums, swap(sums, "gc", 5))
    else:
        sums = lax.psum(sums, "gc")
    for bit in reversed(bits_of(gc_size)):
        keep(swap(packet, "gc", bit), [bit])
    for bit in bits_of(gr_size)[:-1]:
        for m, n in list(evens.items()):
            arrays.append(swap(arrays[n], "gr", bit))
            evens[m | bit] = len(arrays) - 1
    sums = lax.all_gather(sums, "gr", tiled=True)

    hops = {}
    for mask in range(gc_size):
        if mask not in right_at and min(mask.bit_count(), max(2, gc_size.bit_length() - 2)) == 2:
            parent, hop = way_to(mask, "gc")
            hops.setdefault(hop, []).append((mask, parent))
    routes = [([right_at[parent][0] for _, parent in hop], riding) for hop in hops.values()]
    routes.append((list(evens.values()), False))
    extra = 2 * gr_size * blk_cols
    sent = pl.pallas_call(
        functools.partial(relay_kernel, routes, riding),
        out_shape=[
            jax.ShapeDtypeStruct((len(route) * rows + extra * rider, size), packet.dtype)
            for route, rider in routes
        ],
        in_specs=[VMEM] * (1 + len(arrays)),
        out_specs=[VMEM] * len(routes),
        compiler_params=PARAMS,
        name="relay",
    )(sums, *arrays)
    cores = [[i, i + 1] for i in range(0, gr_size, 2)]
    lefts = lax.all_gather(sent[-1], "gr", axis_index_groups=cores, tiled=True)
    right, left = pl.pallas_call(
        functools.partial(spread_kernel, blk_rows, blk_cols, list(evens), dict(right_at)),
        out_shape=(
            jax.ShapeDtypeStruct((order_size, local_cols), weights.dtype),
            jax.ShapeDtypeStruct((local_rows, order_size), weights.dtype),
        ),
        in_specs=[VMEM] * (1 + len(arrays)),
        out_specs=(VMEM, VMEM),
        compiler_params=PARAMS,
        name="spread",
    )(lefts, *arrays)
    early, riders = set(right_at), []
    for (hop, masks), buffer in zip(hops.items(), sent):
        keep(swap(buffer, "gc", hop), [m for m, _ in masks])
        if riding:
            riders.append((len(arrays) - 1, len(masks)))
    for mask in sorted(set(range(gc_size)) - set(right_at), key=lambda m: m.bit_count()):
        parent, hop = way_to(mask, "gc")
        n, at = right_at[parent]
        keep(swap(arrays[n][at * rows : (at + 1) * rows], "gc", hop), [mask])
    late_at = {m: at for m, at in right_at.items() if m not in early}
    inflated, sums, _ = pl.pallas_call(
        functools.partial(expand_kernel, late_at, riders),
        out_shape=(jax.ShapeDtypeStruct(weights.shape, jnp.float32), sums_shape, right),
        in_specs=[HBM] + [VMEM] * (3 + len(arrays)),
        out_specs=(VMEM, VMEM, VMEM),
        input_output_aliases={3 + len(arrays): 2},
        scratch_shapes=[
            pltpu.SMEM(out_pattern.shape, out_pattern.dtype),
            pltpu.VMEM((local_rows, order_size), weights.dtype),
            pltpu.SemaphoreType.DMA,
        ],
        compiler_params=PARAMS,
        name="expand",
    )(in_hbm(out_pattern), sums, left, *arrays, right)
    output_total = total_at_once(sums, "gc")
    return (inflated / output_total * float(order_size)).astype(jnp.bfloat16)


def solution(mesh):
    in_specs = (P("gc", "gr"), P("gc", "gr"), P("gc", "gr"))
    out_specs = P("gc", "gr")
    return jax.shard_map(shards, mesh=mesh, in_specs=in_specs, out_specs=out_specs, check_vma=False)
```

time: 40.9 us -> 39.3 us (0.961)
  blocking collectives: 20.7 us -> 16.3 us
  waiting for transfers between devices: 3.5 us -> 4.96 us
  starting transfers between devices: 12.2 us -> 13.6 us
    all_to_all x1 -> x0, blocking collectives: 11.7 us -> none  [total_of_halves(): parts = lax.all_to_all(parts, ('gr', 'gc'), 0, 0, axis_index_groups=groups)]
    all_gather x0 -> x2, blocking collectives: none -> 7.33 us  [the longest x1 5.15 us: shards(): sums = lax.all_gather(sums, 'gr', tiled=True)]
    ppermute x8, waiting for transfers between devices: 3.5 us -> 4.96 us  [swap(): lax.ppermute(x, axis, [(i, i ^ mask) for i in range(lax.axis_size(axis))])]
    ppermute x8, starting transfers between devices: 12.2 us -> 13.6 us  [swap(): lax.ppermute(x, axis, [(i, i ^ mask) for i in range(lax.axis_size(axis))])]
    pallas_call x4 -> x5, Pallas kernels: 3.37 us -> 3.33 us  [the longest x1 1.62 us: shards(): pl.pallas_call(functools.partial(expand_kernel, late_at, riders), out_sha...]
  transfers between devices with their start and end apart: 8 -> 8, of which waited for: 3 -> 2; matrix products, arithmetic and copies ran while one was open for 0% -> 0% of each run, Pallas kernels for 0% -> 1%
where the time goes in v4:
time: 39.3 us; the launch traced here: 39.1 us
  blocking collectives  16.3 us (41%)
  starting transfers between devices  13.6 us (35%)
  waiting for transfers between devices  4.96 us (13%)
  Pallas kernels  3.33 us (8%)
  other arithmetic  0.79 us (2%)
    ppermute x8, starting transfers between devices, swap(): lax.ppermute(x, axis, [(i, i ^ mask) for i in range(lax.axis_size(axis))])  13.6 us
    all_to_all x1, blocking collectives, total_at_once(): lax.all_to_all(jnp.broadcast_to(x[None], (size,) + x.shape), axis, 0, 0)  8.94 us
    all_gather x1, blocking collectives, shards(): sums = lax.all_gather(sums, 'gr', tiled=True)  5.15 us
    ppermute x8, waiting for transfers between devices, swap(): lax.ppermute(x, axis, [(i, i ^ mask) for i in range(lax.axis_size(axis))])  4.96 us
    all_gather x1, blocking collectives, shards(): lefts = lax.all_gather(sent[-1], 'gr', axis_index_groups=cores, tiled=True)  2.18 us
    pallas_call x1, Pallas kernels, shards(): pl.pallas_call(functools.partial(expand_kernel, late_at, riders), out_sha...  1.62 us
    pallas_call x1, Pallas kernels, shards(): pl.pallas_call(pack_kernel, out_shape=(jax.ShapeDtypeStruct((rows, size),...  1.05 us
  transfers between devices with their start and end apart: 8, of which 2 were waited for; matrix products, arithmetic and copies ran while one was open for 0% of the time, Pallas kernels for 1%

profile of v4, /device:TPU:0, one launch (start us, length us, event | category | flops | bytes accessed | tf_op | source)
XLA Modules:
  0.0 39.1 jit_solution(8606773330830904846)
XLA Ops:
  0.0 1.1 %pack.1 = (bf16[528,128]{1,0:T(8,128)(2,1)S(1)}, f32[1,512]{1,0:T(1,128)S(1)}) custom-call(s32[2,4]{1,0:T(2,128)} %flags_hbm.2, bf16[256,512]{1,0:T(8,128)(2,1)} %weights_hbm.1), custom_call_target="tpu_custom_call" | custom-call | tf_op jit(solution)/shard_map/pack/pallas_call | solution.py:189
  1.1 5.0 %collective-permute-start = (f32[1,512]{1,0:T(1,128)S(1)}, f32[1,512]{1,0:T(1,128)S(1)}, u32[]{:S(2)}, u32[]{:S(2)}) collective-permute-start(f32[1,512]{1,0:T(1,128)S(1)} %get-tuple-element.15.one_ref), channel_id=1, source_target_pairs={{0,5},{1,4},{2,7},{3,6},{4,1},{5,0},{6,3},{7,2},{8,13},{9,12},{10,... | collective-permute-start | bytes 6152 | tf_op jit(solution)/shard_map/ppermute | solution.py:27
  6.1 1.5 %collective-permute-start.4 = (bf16[528,128]{1,0:T(8,128)(2,1)S(1)}, bf16[528,128]{1,0:T(8,128)(2,1)S(1)}, u32[]{:S(2)}, u32[]{:S(2)}) collective-permute-start(bf16[528,128]{1,0:T(8,128)(2,1)S(1)} %get-tuple-element.16.refs_0_), channel_id=1, source_target_pairs={{0,16},{8,24},{16,0},{24,8},{1,17},{9,25},{17,1},{25,9},{2,18},{10... | collective-permute-start | bytes 405512 | tf_op jit(solution)/shard_map/ppermute | solution.py:27
  7.6 0.3 collective-permute-start.3
  7.9 1.6 %collective-permute-start.2 = (bf16[528,128]{1,0:T(8,128)(2,1)S(1)}, bf16[528,128]{1,0:T(8,128)(2,1)S(1)}, u32[]{:S(2)}, u32[]{:S(2)}) collective-permute-start(bf16[528,128]{1,0:T(8,128)(2,1)S(1)} %get-tuple-element.16.refs_0_), channel_id=1, source_target_pairs={{0,2},{1,3},{2,0},{3,1},{4,6},{5,7},{6,4},{7,5},{8,10},{9,11},{10,... | collective-permute-start | bytes 405512 | tf_op jit(solution)/shard_map/ppermute | solution.py:27
  9.5 0.5 %collective-permute-start.1 = (bf16[528,128]{1,0:T(8,128)(2,1)S(1)}, bf16[528,128]{1,0:T(8,128)(2,1)S(1)}, u32[]{:S(2)}, u32[]{:S(2)}) collective-permute-start(bf16[528,128]{1,0:T(8,128)(2,1)S(1)} %get-tuple-element.16.refs_0_), channel_id=1, source_target_pairs={{0,1},{1,0},{2,3},{3,2},{4,5},{5,4},{6,7},{7,6},{8,9},{9,8},{10,11... | collective-permute-start | bytes 405512 | tf_op jit(solution)/shard_map/ppermute | solution.py:27
  10.1 0.0 collective-permute-done.other_ref
  10.1 5.2 %all-gather = f32[4,1,512]{2,1,0:T(1,128)S(1)} all-gather(f32[1,1,512]{2,1,0:T(1,128)S(1)} %bitcast.8), channel_id=1, replica_groups=mesh['gr'=4,'gc'=8] {'gr'}, dimensions={0}, use_global_device_ids=true | all-gather | bytes 10240 | tf_op jit(solution)/shard_map/all_gather | solution.py:228
  15.2 0.0 collective-permute-done.4.refs_4_
  15.2 1.0 %collective-permute-done.3.refs_3_ = bf16[528,128]{1,0:T(8,128)(2,1)S(1)} collective-permute-done((bf16[528,128]{1,0:T(8,128)(2,1)S(1)}, bf16[528,128]{1,0:T(8,128)(2,1)S(1)}, u32[]{:S(2)}, u32[]{:S(2)}) %collective-permute-start.3) | collective-permute-done | bytes 135200 | tf_op jit(solution)/shard_map/ppermute | solution.py:27
  16.2 0.0 collective-permute-done.2.refs_2_
  16.2 0.0 collective-permute-done.1.refs_1_
  16.2 0.1 relay.1
  16.3 0.6 %collective-permute-start.5 = (bf16[1088,128]{1,0:T(8,128)(2,1)S(1)}, bf16[1088,128]{1,0:T(8,128)(2,1)S(1)}, u32[]{:S(2)}, u32[]{:S(2)}) collective-permute-start(bf16[1088,128]{1,0:T(8,128)(2,1)S(1)} %get-tuple-element.19), channel_id=1, source_target_pairs={{0,1},{1,0},{2,3},{3,2},{4,5},{5,4},{6,7},{7,6},{8,9},{9,8},{10,11... | collective-permute-start | bytes 835592 | tf_op jit(solution)/shard_map/ppermute | solution.py:27
  16.9 0.4 %collective-permute-start.6 = (bf16[560,128]{1,0:T(8,128)(2,1)S(1)}, bf16[560,128]{1,0:T(8,128)(2,1)S(1)}, u32[]{:S(2)}, u32[]{:S(2)}) collective-permute-start(bf16[560,128]{1,0:T(8,128)(2,1)S(1)} %get-tuple-element.20), channel_id=1, source_target_pairs={{0,2},{1,3},{2,0},{3,1},{4,6},{5,7},{6,4},{7,5},{8,10},{9,11},{10,... | collective-permute-start | bytes 430088 | tf_op jit(solution)/shard_map/ppermute | solution.py:27
  17.3 3.6 %collective-permute-start.7 = (bf16[560,128]{1,0:T(8,128)(2,1)S(1)}, bf16[560,128]{1,0:T(8,128)(2,1)S(1)}, u32[]{:S(2)}, u32[]{:S(2)}) collective-permute-start(bf16[560,128]{1,0:T(8,128)(2,1)S(1)} %get-tuple-element.21), channel_id=1, source_target_pairs={{0,6},{1,7},{2,4},{3,5},{4,2},{5,3},{6,0},{7,1},{8,14},{9,15},{10,... | collective-permute-start | bytes 430088 | tf_op jit(solution)/shard_map/ppermute | solution.py:27
  20.9 2.2 %all_gather.7.lefts_ref = bf16[2112,128]{1,0:T(8,128)(2,1)S(1)} all-gather(bf16[1056,128]{1,0:T(8,128)(2,1)S(1)} %get-tuple-element.17), channel_id=1, replica_groups={{0,8},{16,24},{1,9},{17,25},{2,10},{18,26},{3,11},{19,27},{4,12},{20,28..., dimensions={0}, use_global_device_ids=true | all-gather | bytes 811008 | tf_op jit(solution)/shard_map/all_gather | solution.py:250
  23.1 0.6 %spread.1 = (bf16[2048,512]{1,0:T(8,128)(2,1)S(1)}, bf16[256,2048]{1,0:T(8,128)(2,1)S(1)}) custom-call(bf16[2112,128]{1,0:T(8,128)(2,1)S(1)} %all_gather.7.lefts_ref, bf16[528,128]{1,0:T(8,128)(2,1)S(1)} %get-tuple-element.16.refs_0_, bf16[528,128]{1,0:T(8,128)(2,1)S(1)} %collective-permute-done.1.refs_1_, ...), custom_call_target="tpu_custom_call" | custom-call | tf_op jit(solution)/shard_map/spread/pallas_call | solution.py:251
  23.7 0.0 collective-permute-done.6.refs_6_
  23.7 4.0 %collective-permute-done.7.refs_7_ = bf16[560,128]{1,0:T(8,128)(2,1)S(1)} collective-permute-done((bf16[560,128]{1,0:T(8,128)(2,1)S(1)}, bf16[560,128]{1,0:T(8,128)(2,1)S(1)}, u32[]{:S(2)}, u32[]{:S(2)}) %collective-permute-start.7) | collective-permute-done | bytes 143392 | tf_op jit(solution)/shard_map/ppermute | solution.py:27
  27.7 0.0 collective-permute-done.5.refs_5_
  27.7 1.6 %expand.1 = (f32[256,512]{1,0:T(8,128)S(1)}, f32[1,512]{1,0:T(1,128)S(1)}, bf16[2048,512]{1,0:T(8,128)(2,1)S(1)}) custom-call(s32[2,4]{1,0:T(2,128)} %flags_hbm.3, f32[4,512]{1,0:T(4,128)S(1)} %bitcast.6, bf16[256,2048]{1,0:T(8,128)(2,1)S(1)} %get-tuple-element.18.left, ...), custom_call_target="tpu_custom_call", output_to_operand_aliasing={{2}: (11, {})} | custom-call | tf_op jit(solution)/shard_map/expand/pallas_call | solution.py:272
  29.3 8.9 %all_to_all.5 = f32[8,1,512]{2,1,0:T(1,128)S(1)} all-to-all(f32[8,1,512]{2,1,0:T(1,128)S(1)} %broadcast_in_dim.9), channel_id=1, replica_groups=mesh['gr'=4,'gc'=8] {'gc'}, dimensions={0} | all-to-all | bytes 32768 | tf_op jit(solution)/shard_map/all_to_all | solution.py:41
  38.3 0.8 %multiply_convert_fusion = bf16[256,512]{1,0:T(8,128)(2,1)} fusion(f32[256,512]{1,0:T(8,128)S(1)} %get-tuple-element.23, f32[512]{0:T(512)S(1)} %reduce_sum.9), kind=kLoop, calls=%fused_computation | loop fusion | flops 393216 | bytes 788480 | tf_op jit(solution)/shard_map/convert_element_type | solution.py:287
  (4 shorter events, 0.0 us)
Async XLA Ops:
  1.1 9.0 %collective-permute-start = (f32[1,512]{1,0:T(1,128)S(1)}, f32[1,512]{1,0:T(1,128)S(1)}, u32[]{:S(2)}, u32[]{:S(2)}) collective-permute-start(f32[1,512]{1,0:T(1,128)S(1)} %get-tuple-element.15.one_ref), channel_id=1, source_target_pairs={{0,5},{1,4},{2,7},{3,6},{4,1},{5,0},{6,3},{7,2},{8,13},{9,12},{10,... | collective-permute-start | bytes 6152 | tf_op jit(solution)/shard_map/ppermute | solution.py:27
  6.1 9.1 %collective-permute-start.4 = (bf16[528,128]{1,0:T(8,128)(2,1)S(1)}, bf16[528,128]{1,0:T(8,128)(2,1)S(1)}, u32[]{:S(2)}, u32[]{:S(2)}) collective-permute-start(bf16[528,128]{1,0:T(8,128)(2,1)S(1)} %get-tuple-element.16.refs_0_), channel_id=1, source_target_pairs={{0,16},{8,24},{16,0},{24,8},{1,17},{9,25},{17,1},{25,9},{2,18},{10... | collective-permute-start | bytes 405512 | tf_op jit(solution)/shard_map/ppermute | solution.py:27
  7.6 8.6 %collective-permute-start.3 = (bf16[528,128]{1,0:T(8,128)(2,1)S(1)}, bf16[528,128]{1,0:T(8,128)(2,1)S(1)}, u32[]{:S(2)}, u32[]{:S(2)}) collective-permute-start(bf16[528,128]{1,0:T(8,128)(2,1)S(1)} %get-tuple-element.16.refs_0_), channel_id=1, source_target_pairs={{0,4},{1,5},{2,6},{3,7},{4,0},{5,1},{6,2},{7,3},{8,12},{9,13},{10,... | collective-permute-start | bytes 405512 | tf_op jit(solution)/shard_map/ppermute | solution.py:27
  7.9 8.3 %collective-permute-start.2 = (bf16[528,128]{1,0:T(8,128)(2,1)S(1)}, bf16[528,128]{1,0:T(8,128)(2,1)S(1)}, u32[]{:S(2)}, u32[]{:S(2)}) collective-permute-start(bf16[528,128]{1,0:T(8,128)(2,1)S(1)} %get-tuple-element.16.refs_0_), channel_id=1, source_target_pairs={{0,2},{1,3},{2,0},{3,1},{4,6},{5,7},{6,4},{7,5},{8,10},{9,11},{10,... | collective-permute-start | bytes 405512 | tf_op jit(solution)/shard_map/ppermute | solution.py:27
  9.5 6.7 %collective-permute-start.1 = (bf16[528,128]{1,0:T(8,128)(2,1)S(1)}, bf16[528,128]{1,0:T(8,128)(2,1)S(1)}, u32[]{:S(2)}, u32[]{:S(2)}) collective-permute-start(bf16[528,128]{1,0:T(8,128)(2,1)S(1)} %get-tuple-element.16.refs_0_), channel_id=1, source_target_pairs={{0,1},{1,0},{2,3},{3,2},{4,5},{5,4},{6,7},{7,6},{8,9},{9,8},{10,11... | collective-permute-start | bytes 405512 | tf_op jit(solution)/shard_map/ppermute | solution.py:27
  16.3 11.4 %collective-permute-start.5 = (bf16[1088,128]{1,0:T(8,128)(2,1)S(1)}, bf16[1088,128]{1,0:T(8,128)(2,1)S(1)}, u32[]{:S(2)}, u32[]{:S(2)}) collective-permute-start(bf16[1088,128]{1,0:T(8,128)(2,1)S(1)} %get-tuple-element.19), channel_id=1, source_target_pairs={{0,1},{1,0},{2,3},{3,2},{4,5},{5,4},{6,7},{7,6},{8,9},{9,8},{10,11... | collective-permute-start | bytes 835592 | tf_op jit(solution)/shard_map/ppermute | solution.py:27
  16.9 6.8 %collective-permute-start.6 = (bf16[560,128]{1,0:T(8,128)(2,1)S(1)}, bf16[560,128]{1,0:T(8,128)(2,1)S(1)}, u32[]{:S(2)}, u32[]{:S(2)}) collective-permute-start(bf16[560,128]{1,0:T(8,128)(2,1)S(1)} %get-tuple-element.20), channel_id=1, source_target_pairs={{0,2},{1,3},{2,0},{3,1},{4,6},{5,7},{6,4},{7,5},{8,10},{9,11},{10,... | collective-permute-start | bytes 430088 | tf_op jit(solution)/shard_map/ppermute | solution.py:27
  17.3 10.3 %collective-permute-start.7 = (bf16[560,128]{1,0:T(8,128)(2,1)S(1)}, bf16[560,128]{1,0:T(8,128)(2,1)S(1)}, u32[]{:S(2)}, u32[]{:S(2)}) collective-permute-start(bf16[560,128]{1,0:T(8,128)(2,1)S(1)} %get-tuple-element.21), channel_id=1, source_target_pairs={{0,6},{1,7},{2,4},{3,5},{4,2},{5,3},{6,0},{7,1},{8,14},{9,15},{10,... | collective-permute-start | bytes 430088 | tf_op jit(solution)/shard_map/ppermute | solution.py:27

commit v5 on v4

--- a/solution.py
+++ b/solution.py
@@ -25,6 +25,10 @@
 
 def swap(x, axis, mask):
     return lax.ppermute(x, axis, [(i, i ^ mask) for i in range(lax.axis_size(axis))])
+
+
+def with_partner(x, axis, mask):
+    return jnp.concatenate([x, swap(x, axis, mask)], axis=0)
 
 
 def way_to(mask, axis):
@@ -36,21 +40,16 @@
     return mask ^ last, last
 
 
-def total_at_once(x, axis):
-    size = lax.axis_size(axis)
-    parts = lax.all_to_all(jnp.broadcast_to(x[None], (size,) + x.shape), axis, 0, 0)
-    return jnp.sum(parts, axis=0)
-
-
 def places_in(packet, size):
     meta = packet[pl.ds(SLOTS * size, META), :].astype(jnp.float32)
     return [jnp.max(meta[s : s + 1, :]).astype(jnp.int32) for s in range(SLOTS)]
 
 
-def pack_kernel(flags_hbm, weights_hbm, packet_ref, sums_ref, flags_ref, weights_ref, sems):
+def pack_kernel(flags_hbm, kept_hbm, weights_hbm, packet_ref, sums_ref, flags_ref, kept_ref, weights_ref, sems):
     copies = [
         pltpu.make_async_copy(flags_hbm, flags_ref, sems.at[0]),
-        pltpu.make_async_copy(weights_hbm, weights_ref, sems.at[1]),
+        pltpu.make_async_copy(kept_hbm, kept_ref, sems.at[1]),
+        pltpu.make_async_copy(weights_hbm, weights_ref, sems.at[2]),
     ]
     for copy in copies:
         copy.start()
@@ -77,6 +76,9 @@
         packet_ref[pl.ds(s * size, size), :] = block
         sums_ref[:, pl.ds(col, size)] += jnp.sum(block.astype(jnp.float32), axis=0, keepdims=True)
         meta = jnp.where(row_ids == s, place.astype(jnp.float32), meta)
+    for b in range(blocks):
+        kept = kept_ref[b // blk_cols, b % blk_cols].astype(jnp.float32)
+        meta = jnp.where(row_ids == SLOTS + b, kept, meta)
     packet_ref[pl.ds(SLOTS * size, META), :] = meta.astype(packet_ref.dtype)
 
 
@@ -127,28 +129,19 @@
     return {m: refs[n].at[pl.ds(at * rows, rows), :] for m, (n, at) in table.items()}
 
 
-def spread_kernel(blk_rows, blk_cols, evens, right_at, lefts_ref, *refs):
+def spread_kernel(blk_rows, blk_cols, right_at, *refs):
     *refs, right, left = refs
     rows, size = refs[0].shape
     right[...] = jnp.zeros_like(right)
     left[...] = jnp.zeros_like(left)
     spread(blk_rows, blk_cols, size, packets_in(refs, right_at, rows), right)
-    my_col = lax.axis_index("gr")
-    for n in range(lefts_ref.shape[0] // rows):
-        packet = lefts_ref.at[pl.ds(n * rows, rows), :]
-        gr = my_col // 2 * 2 + n // len(evens) ^ evens[n % len(evens)]
-        for s, place in enumerate(places_in(packet, size)):
-            row = pl.multiple_of(place // blk_cols * size, size)
-            at = pl.multiple_of((gr * blk_cols + place % blk_cols) * size, size)
-            left[pl.ds(row, size), pl.ds(at, size)] = packet[pl.ds(s * size, size), :]
-
-
-def expand_kernel(right_at, riders, flags_hbm, sums_ref, left, *refs):
-    *refs, _, inflated_ref, total_ref, right, flags_ref, scaled, sem = refs
-    copy = pltpu.make_async_copy(flags_hbm, flags_ref, sem)
-    copy.start()
-    blk_rows, blk_cols = flags_ref.shape
+
+
+def expand_kernel(right_at, riders, evens, blk_cols, sums_ref, *refs):
+    *halves, _, _, inflated_ref, total_ref, right, left = refs[:2] + refs[-6:]
+    refs = refs[2:-6]
     rows, size = refs[0].shape
+    blk_rows = inflated_ref.shape[0] // size
     spread(blk_rows, blk_cols, size, packets_in(refs, right_at, rows), right)
     sums = rows_of(sums_ref)
     for n, at in riders:
@@ -156,24 +149,41 @@
         low = refs[n][pl.ds(at * rows + sums.shape[0], sums.shape[0]), :].astype(jnp.float32)
         sums = sums + (high + low)
     inverse = 1.0 / sums
-    for n in range(sums.shape[0]):
-        at = slice(n * size, (n + 1) * size)
-        scaled[:, at] = (left[:, at].astype(jnp.float32) * inverse[n : n + 1]).astype(scaled.dtype)
-    product = jnp.dot(scaled[...], right[...], preferred_element_type=jnp.float32)
-    copy.wait()
     my_col = lax.axis_index("gr")
+    for n in range(2 * len(evens)):
+        gr = my_col // 2 * 2 + n // len(evens) ^ evens[n % len(evens)]
+        scales = []
+        for j in range(blk_cols):
+            scale = inverse[j : j + 1]
+            for m in range(1, 2 * len(evens)):
+                there = inverse[m * blk_cols + j : m * blk_cols + j + 1]
+                scale = jnp.where(my_col ^ m == gr, there, scale)
+            scales.append(scale)
+        for part, half in enumerate(halves):
+            packet = half.at[pl.ds(n * rows, rows), :]
+            for s, place in enumerate(places_in(packet, size)):
+                row = pl.multiple_of((part * blk_rows + place // blk_cols) * size, size)
+                col = place % blk_cols
+                scale = scales[0]
+                for j in range(1, blk_cols):
+                    scale = jnp.where(col == j, scales[j], scale)
+                block = packet[pl.ds(s * size, size), :].astype(jnp.float32) * scale
+                at = pl.multiple_of((gr * blk_cols + col) * size, size)
+                left[pl.ds(row, size), pl.ds(at, size)] = block.astype(left.dtype)
+    product = jnp.dot(left[...], right[...], preferred_element_type=jnp.float32)
+    first = SLOTS * size
+    flags = [ref[pl.ds(first, META), :].astype(jnp.float32) for ref in (refs[0], refs[1])]
     for j in range(blk_cols):
         at = slice(j * size, (j + 1) * size)
         own = inverse[j : j + 1]
-        for r in range(1, sums.shape[0] // blk_cols):
-            own = jnp.where(my_col == r, inverse[r * blk_cols + j : r * blk_cols + j + 1], own)
         total = jnp.zeros((1, size), jnp.float32)
-        for i in range(blk_rows):
-            rows_at = slice(i * size, (i + 1) * size)
-            kept = product[rows_at, at] * own
-            kept = kept * flags_ref[i, j].astype(jnp.float32)
+        for i in range(2 * blk_rows):
+            part, flag = i // blk_rows, SLOTS + i % blk_rows * blk_cols + j
+            kept = product[i * size : (i + 1) * size, at] * own
+            kept = kept * flags[part][flag : flag + 1]
             squared = kept * kept
-            inflated_ref[rows_at, at] = squared
+            if part == 0:
+                inflated_ref[i * size : (i + 1) * size, at] = squared
             total = total + jnp.sum(squared, axis=0, keepdims=True)
         total_ref[:, at] = total
 
@@ -189,16 +199,17 @@
     packet, sums = pl.pallas_call(
         pack_kernel,
         out_shape=(jax.ShapeDtypeStruct((rows, size), weights.dtype), sums_shape),
-        in_specs=[HBM, HBM],
+        in_specs=[HBM] * 3,
         out_specs=(VMEM, VMEM),
         scratch_shapes=[
             pltpu.SMEM(in_pattern.shape, in_pattern.dtype),
+            pltpu.SMEM(out_pattern.shape, out_pattern.dtype),
             pltpu.VMEM(weights.shape, weights.dtype),
-            pltpu.SemaphoreType.DMA((2,)),
+            pltpu.SemaphoreType.DMA((3,)),
         ],
         compiler_params=PARAMS,
         name="pack",
-    )(in_hbm(in_pattern), in_hbm(weights))
+    )(in_hbm(in_pattern), in_hbm(out_pattern), in_hbm(weights))
 
     arrays, right_at, evens = [packet], {0: (0, 0)}, {0: 0}
 
@@ -207,10 +218,11 @@
         right_at.update({m: (len(arrays) - 1, at) for at, m in enumerate(masks)})
 
     riding = gc_size == 8
+    sums = with_partner(sums, "gr", 1)
     if riding:
         sums = pl.pallas_call(
             add_kernel,
-            out_shape=sums_shape,
+            out_shape=jax.ShapeDtypeStruct(sums.shape, sums.dtype),
             in_specs=[VMEM] * 2,
             out_specs=VMEM,
             compiler_params=PARAMS,
@@ -219,13 +231,19 @@
         )(sums, swap(sums, "gc", 5))
     else:
         sums = lax.psum(sums, "gc")
-    for bit in reversed(bits_of(gc_size)):
-        keep(swap(packet, "gc", bit), [bit])
+    keep(swap(packet, "gc", 1), [1])
     for bit in bits_of(gr_size)[:-1]:
         for m, n in list(evens.items()):
             arrays.append(swap(arrays[n], "gr", bit))
             evens[m | bit] = len(arrays) - 1
-    sums = lax.all_gather(sums, "gr", tiled=True)
+    for bit in reversed(bits_of(gc_size)[:-1]):
+        keep(swap(packet, "gc", bit), [bit])
+    others = {0: right_at[1][0]}
+    for m in list(evens)[1:]:
+        arrays.append(swap(arrays[evens[m]], "gc", 1))
+        others[m] = len(arrays) - 1
+    for bit in reversed(bits_of(gr_size)[:-1]):
+        sums = with_partner(sums, "gr", bit)
 
     hops = {}
     for mask in range(gc_size):
@@ -234,6 +252,7 @@
             hops.setdefault(hop, []).append((mask, parent))
     routes = [([right_at[parent][0] for _, parent in hop], riding) for hop in hops.values()]
     routes.append((list(evens.values()), False))
+    routes.append((list(others.values()), False))
     extra = 2 * gr_size * blk_cols
     sent = pl.pallas_call(
         functools.partial(relay_kernel, routes, riding),
@@ -247,18 +266,20 @@
         name="relay",
     )(sums, *arrays)
     cores = [[i, i + 1] for i in range(0, gr_size, 2)]
-    lefts = lax.all_gather(sent[-1], "gr", axis_index_groups=cores, tiled=True)
+    lefts = [
+        lax.all_gather(half, "gr", axis_index_groups=cores, tiled=True) for half in sent[-2:]
+    ]
     right, left = pl.pallas_call(
-        functools.partial(spread_kernel, blk_rows, blk_cols, list(evens), dict(right_at)),
+        functools.partial(spread_kernel, blk_rows, blk_cols, dict(right_at)),
         out_shape=(
             jax.ShapeDtypeStruct((order_size, local_cols), weights.dtype),
-            jax.ShapeDtypeStruct((local_rows, order_size), weights.dtype),
+            jax.ShapeDtypeStruct((2 * local_rows, order_size), weights.dtype),
         ),
-        in_specs=[VMEM] * (1 + len(arrays)),
+        in_specs=[VMEM] * len(arrays),
         out_specs=(VMEM, VMEM),
         compiler_params=PARAMS,
         name="spread",
-    )(lefts, *arrays)
+    )(*arrays)
     early, riders = set(right_at), []
     for (hop, masks), buffer in zip(hops.items(), sent):
         keep(swap(buffer, "gc", hop), [m for m, _ in masks])
@@ -269,21 +290,18 @@
         n, at = right_at[parent]
         keep(swap(arrays[n][at * rows : (at + 1) * rows], "gc", hop), [mask])
     late_at = {m: at for m, at in right_at.items() if m not in early}
-    inflated, sums, _ = pl.pallas_call(
-        functools.partial(expand_kernel, late_at, riders),
-        out_shape=(jax.ShapeDtypeStruct(weights.shape, jnp.float32), sums_shape, right),
-        in_specs=[HBM] + [VMEM] * (3 + len(arrays)),
-        out_specs=(VMEM, VMEM, VMEM),
-        input_output_aliases={3 + len(arrays): 2},
-        scratch_shapes=[
-            pltpu.SMEM(out_pattern.shape, out_pattern.dtype),
-            pltpu.VMEM((local_rows, order_size), weights.dtype),
-            pltpu.SemaphoreType.DMA,
-        ],
+    inflated, sums, *_ = pl.pallas_call(
+        functools.partial(expand_kernel, late_at, riders, list(evens), blk_cols),
+        out_shape=(jax.ShapeDtypeStruct(weights.shape, jnp.float32), sums_shape, right, left),
+        in_specs=[VMEM] * (5 + len(arrays)),
+        out_specs=[VMEM] * 4,
+        input_output_aliases={3 + len(arrays): 2, 4 + len(arrays): 3},
         compiler_params=PARAMS,
         name="expand",
-    )(in_hbm(out_pattern), sums, left, *arrays, right)
-    output_total = total_at_once(sums, "gc")
+    )(sums, *lefts, *arrays, right, left)
+    output_total = sums
+    for mask in range(2, gc_size, 2):
+        output_total = output_total + swap(sums, "gc", mask)
     return (inflated / output_total * float(order_size)).astype(jnp.bfloat16)
 
 

time: 39.3 us -> 37.9 us (0.964)
  blocking collectives: 16.3 us -> 4.37 us
  starting transfers between devices: 13.6 us -> 20.2 us
  waiting for transfers between devices: 4.96 us -> 8.49 us
  Pallas kernels: 3.33 us -> 3.83 us
    all_to_all x1 -> x0, blocking collectives: 8.94 us -> none  [total_at_once(): lax.all_to_all(jnp.broadcast_to(x[None], (size,) + x.shape), axis, 0, 0)]
    ppermute x8 -> x14, starting transfers between devices: 13.6 us -> 20.2 us  [swap(): lax.ppermute(x, axis, [(i, i ^ mask) for i in range(lax.axis_size(axis))])]
    ppermute x8 -> x14, waiting for transfers between devices: 4.96 us -> 8.49 us  [swap(): lax.ppermute(x, axis, [(i, i ^ mask) for i in range(lax.axis_size(axis))])]
    all_gather x2, blocking collectives: 7.33 us -> 4.37 us  [shards(): lax.all_gather(half, 'gr', axis_index_groups=cores, tiled=True)]
    pallas_call x3, Pallas kernels: 2.2 us -> 2.65 us  [the longest x1 2.19 us: shards(): pl.pallas_call(functools.partial(expand_kernel, late_at, riders, list(eve...]
  transfers between devices with their start and end apart: 8 -> 14, of which waited for: 2 -> 6; matrix products, arithmetic and copies ran while one was open for 0% -> 0% of each run, Pallas kernels for 1% -> 1%
where the time goes in v5:
time: 37.9 us; the launch traced here: 37.7 us
  starting transfers between devices  20.2 us (53%)
  waiting for transfers between devices  8.49 us (22%)
  blocking collectives  4.37 us (12%)
  Pallas kernels  3.83 us (10%)
  other arithmetic  0.78 us (2%)
    ppermute x14, starting transfers between devices, swap(): lax.ppermute(x, axis, [(i, i ^ mask) for i in range(lax.axis_size(axis))])  20.2 us
    ppermute x14, waiting for transfers between devices, swap(): lax.ppermute(x, axis, [(i, i ^ mask) for i in range(lax.axis_size(axis))])  8.49 us
    all_gather x2, blocking collectives, shards(): lax.all_gather(half, 'gr', axis_index_groups=cores, tiled=True)  4.37 us
    pallas_call x1, Pallas kernels, shards(): pl.pallas_call(functools.partial(expand_kernel, late_at, riders, list(eve...  2.19 us
    pallas_call x1, Pallas kernels, shards(): pl.pallas_call(pack_kernel, out_shape=(jax.ShapeDtypeStruct((rows, size),...  1.06 us
    convert_element_type x1, other arithmetic, shards(): return (inflated / output_total * float(order_size)).astype(jnp.bfloat16)  0.76 us
  transfers between devices with their start and end apart: 14, of which 6 were waited for; matrix products, arithmetic and copies ran while one was open for 0% of the time, Pallas kernels for 1%

profile of v5, /device:TPU:0, one launch (start us, length us, event | category | flops | bytes accessed | tf_op | source)
XLA Modules:
  0.0 37.7 jit_solution(12248851602647708508)
XLA Ops:
  0.0 1.1 %pack.1 = (bf16[528,128]{1,0:T(8,128)(2,1)S(1)}, f32[1,512]{1,0:T(1,128)S(1)}) custom-call(s32[2,4]{1,0:T(2,128)} %flags_hbm.1, s32[2,4]{1,0:T(2,128)} %kept_hbm.1, bf16[256,512]{1,0:T(8,128)(2,1)} %weights_hbm.1), custom_call_target="tpu_custom_call" | custom-call | tf_op jit(solution)/shard_map/pack/pallas_call | solution.py:199
  1.1 3.0 %collective-permute-start.4 = (bf16[528,128]{1,0:T(8,128)(2,1)S(1)}, bf16[528,128]{1,0:T(8,128)(2,1)S(1)}, u32[]{:S(2)}, u32[]{:S(2)}) collective-permute-start(bf16[528,128]{1,0:T(8,128)(2,1)S(1)} %get-tuple-element.17.refs_0_.refs_2_), channel_id=1, source_target_pairs={{0,16},{8,24},{16,0},{24,8},{1,17},{9,25},{17,1},{25,9},{2,18},{10... | collective-permute-start | bytes 405512 | tf_op jit(solution)/shard_map/ppermute | solution.py:27
  4.1 1.2 %collective-permute-done = f32[1,512]{1,0:T(1,128)S(1)} collective-permute-done((f32[1,512]{1,0:T(1,128)S(1)}, f32[1,512]{1,0:T(1,128)S(1)}, u32[]{:S(2)}, u32[]{:S(2)}) %collective-permute-start) | collective-permute-done | bytes 2080 | tf_op jit(solution)/shard_map/ppermute | solution.py:27
  5.3 3.6 %collective-permute-start.1 = (f32[2,512]{1,0:T(2,128)S(1)}, f32[2,512]{1,0:T(2,128)S(1)}, u32[]{:S(2)}, u32[]{:S(2)}) collective-permute-start(f32[2,512]{1,0:T(2,128)S(1)} %pad_maximum_fusion.1.one_ref), channel_id=1, source_target_pairs={{0,5},{1,4},{2,7},{3,6},{4,1},{5,0},{6,3},{7,2},{8,13},{9,12},{10,... | collective-permute-start | bytes 12296 | tf_op jit(solution)/shard_map/ppermute | solution.py:27
  8.9 0.3 collective-permute-start.6
  9.2 1.6 %collective-permute-start.5 = (bf16[528,128]{1,0:T(8,128)(2,1)S(1)}, bf16[528,128]{1,0:T(8,128)(2,1)S(1)}, u32[]{:S(2)}, u32[]{:S(2)}) collective-permute-start(bf16[528,128]{1,0:T(8,128)(2,1)S(1)} %get-tuple-element.17.refs_0_.refs_2_), channel_id=1, source_target_pairs={{0,2},{1,3},{2,0},{3,1},{4,6},{5,7},{6,4},{7,5},{8,10},{9,11},{10,... | collective-permute-start | bytes 405512 | tf_op jit(solution)/shard_map/ppermute | solution.py:27
  10.8 0.5 %collective-permute-start.3 = (bf16[528,128]{1,0:T(8,128)(2,1)S(1)}, bf16[528,128]{1,0:T(8,128)(2,1)S(1)}, u32[]{:S(2)}, u32[]{:S(2)}) collective-permute-start(bf16[528,128]{1,0:T(8,128)(2,1)S(1)} %get-tuple-element.17.refs_0_.refs_2_), channel_id=1, source_target_pairs={{0,1},{1,0},{2,3},{3,2},{4,5},{5,4},{6,7},{7,6},{8,9},{9,8},{10,11... | collective-permute-start | bytes 405512 | tf_op jit(solution)/shard_map/ppermute | solution.py:27
  11.3 1.5 %collective-permute-start.7 = (bf16[528,128]{1,0:T(8,128)(2,1)S(1)}, bf16[528,128]{1,0:T(8,128)(2,1)S(1)}, u32[]{:S(2)}, u32[]{:S(2)}) collective-permute-start(bf16[528,128]{1,0:T(8,128)(2,1)S(1)} %collective-permute-done.4.refs_2_.refs_4_), channel_id=1, source_target_pairs={{0,1},{1,0},{2,3},{3,2},{4,5},{5,4},{6,7},{7,6},{8,9},{9,8},{10,11... | collective-permute-start | bytes 405512 | tf_op jit(solution)/shard_map/ppermute | solution.py:27
  12.8 0.5 %collective-permute-start.2 = (f32[2,512]{1,0:T(2,128)S(1)}, f32[2,512]{1,0:T(2,128)S(1)}, u32[]{:S(2)}, u32[]{:S(2)}) collective-permute-start(f32[2,512]{1,0:T(2,128)S(1)} %add.16), channel_id=1, source_target_pairs={{0,16},{8,24},{16,0},{24,8},{1,17},{9,25},{17,1},{25,9},{2,18},{10... | collective-permute-start | bytes 12296 | tf_op jit(solution)/shard_map/ppermute | solution.py:27
  13.3 3.1 %collective-permute-done.2 = f32[2,512]{1,0:T(2,128)S(1)} collective-permute-done((f32[2,512]{1,0:T(2,128)S(1)}, f32[2,512]{1,0:T(2,128)S(1)}, u32[]{:S(2)}, u32[]{:S(2)}) %collective-permute-start.2) | collective-permute-done | bytes 4128 | tf_op jit(solution)/shard_map/ppermute | solution.py:27
  16.4 1.6 %collective-permute-done.6.refs_4_.refs_6_ = bf16[528,128]{1,0:T(8,128)(2,1)S(1)} collective-permute-done((bf16[528,128]{1,0:T(8,128)(2,1)S(1)}, bf16[528,128]{1,0:T(8,128)(2,1)S(1)}, u32[]{:S(2)}, u32[]{:S(2)}) %collective-permute-start.6) | collective-permute-done | bytes 135200 | tf_op jit(solution)/shard_map/ppermute | solution.py:27
  18.0 0.4 %collective-permute-done.7.refs_5_.refs_7_ = bf16[528,128]{1,0:T(8,128)(2,1)S(1)} collective-permute-done((bf16[528,128]{1,0:T(8,128)(2,1)S(1)}, bf16[528,128]{1,0:T(8,128)(2,1)S(1)}, u32[]{:S(2)}, u32[]{:S(2)}) %collective-permute-start.7) | collective-permute-done | bytes 135200 | tf_op jit(solution)/shard_map/ppermute | solution.py:27
  18.6 0.7 %collective-permute-start.8 = (bf16[1088,128]{1,0:T(8,128)(2,1)S(1)}, bf16[1088,128]{1,0:T(8,128)(2,1)S(1)}, u32[]{:S(2)}, u32[]{:S(2)}) collective-permute-start(bf16[1088,128]{1,0:T(8,128)(2,1)S(1)} %get-tuple-element.20), channel_id=1, source_target_pairs={{0,1},{1,0},{2,3},{3,2},{4,5},{5,4},{6,7},{7,6},{8,9},{9,8},{10,11... | collective-permute-start | bytes 835592 | tf_op jit(solution)/shard_map/ppermute | solution.py:27
  19.2 0.5 %collective-permute-start.9 = (bf16[560,128]{1,0:T(8,128)(2,1)S(1)}, bf16[560,128]{1,0:T(8,128)(2,1)S(1)}, u32[]{:S(2)}, u32[]{:S(2)}) collective-permute-start(bf16[560,128]{1,0:T(8,128)(2,1)S(1)} %get-tuple-element.21), channel_id=1, source_target_pairs={{0,2},{1,3},{2,0},{3,1},{4,6},{5,7},{6,4},{7,5},{8,10},{9,11},{10,... | collective-permute-start | bytes 430088 | tf_op jit(solution)/shard_map/ppermute | solution.py:27
  19.7 3.5 %collective-permute-start.10 = (bf16[560,128]{1,0:T(8,128)(2,1)S(1)}, bf16[560,128]{1,0:T(8,128)(2,1)S(1)}, u32[]{:S(2)}, u32[]{:S(2)}) collective-permute-start(bf16[560,128]{1,0:T(8,128)(2,1)S(1)} %get-tuple-element.22), channel_id=1, source_target_pairs={{0,6},{1,7},{2,4},{3,5},{4,2},{5,3},{6,0},{7,1},{8,14},{9,15},{10,... | collective-permute-start | bytes 430088 | tf_op jit(solution)/shard_map/ppermute | solution.py:27
  23.2 2.2 %all_gather.6.refs_0_ = bf16[2112,128]{1,0:T(8,128)(2,1)S(1)} all-gather(bf16[1056,128]{1,0:T(8,128)(2,1)S(1)} %get-tuple-element.18), channel_id=1, replica_groups={{0,8},{16,24},{1,9},{17,25},{2,10},{18,26},{3,11},{19,27},{4,12},{20,28..., dimensions={0}, use_global_device_ids=true | all-gather | bytes 811008 | tf_op jit(solution)/shard_map/all_gather | solution.py:270
  25.4 0.5 %spread.1 = (bf16[2048,512]{1,0:T(8,128)(2,1)S(1)}, bf16[512,2048]{1,0:T(8,128)(2,1)S(1)}) custom-call(bf16[528,128]{1,0:T(8,128)(2,1)S(1)} %get-tuple-element.17.refs_0_.refs_2_, bf16[528,128]{1,0:T(8,128)(2,1)S(1)} %collective-permute-done.3.refs_1_.refs_3_, bf16[528,128]{1,0:T(8,128)(2,1)S(1)} %collective-permute-done.4.refs_2_.refs_4_, ...), custom_call_target="tpu_custom_call" | custom-call | tf_op jit(solution)/shard_map/spread/pallas_call | solution.py:272
  25.9 2.2 %all_gather.7.refs_1_ = bf16[2112,128]{1,0:T(8,128)(2,1)S(1)} all-gather(bf16[1056,128]{1,0:T(8,128)(2,1)S(1)} %get-tuple-element.19), channel_id=1, replica_groups={{0,8},{16,24},{1,9},{17,25},{2,10},{18,26},{3,11},{19,27},{4,12},{20,28..., dimensions={0}, use_global_device_ids=true | all-gather | bytes 811008 | tf_op jit(solution)/shard_map/all_gather | solution.py:270
  28.1 2.2 %expand.1 = (f32[256,512]{1,0:T(8,128)S(1)}, f32[1,512]{1,0:T(1,128)S(1)}, bf16[2048,512]{1,0:T(8,128)(2,1)S(1)}, bf16[512,2048]{1,0:T(8,128)(2,1)S(1)}) custom-call(f32[4,512]{1,0:T(4,128)S(1)} %pad_maximum_fusion.sums_ref, bf16[2112,128]{1,0:T(8,128)(2,1)S(1)} %all_gather.6.refs_0_, ...), custom_call_target="tpu_custom_call", output_to_operand_aliasing={{2}: (12, {}), {3}: (13, {})} | custom-call | tf_op jit(solution)/shard_map/expand/pallas_call | solution.py:293
  30.3 2.2 %collective-permute-start.13 = (f32[1,512]{1,0:T(1,128)S(1)}, f32[1,512]{1,0:T(1,128)S(1)}, u32[]{:S(2)}, u32[]{:S(2)}) collective-permute-start(f32[1,512]{1,0:T(1,128)S(1)} %get-tuple-element.26), channel_id=1, source_target_pairs={{0,6},{1,7},{2,4},{3,5},{4,2},{5,3},{6,0},{7,1},{8,14},{9,15},{10,... | collective-permute-start | bytes 6152 | tf_op jit(solution)/shard_map/ppermute | solution.py:27
  32.4 2.3 %collective-permute-start.11 = (f32[1,512]{1,0:T(1,128)S(1)}, f32[1,512]{1,0:T(1,128)S(1)}, u32[]{:S(2)}, u32[]{:S(2)}) collective-permute-start(f32[1,512]{1,0:T(1,128)S(1)} %get-tuple-element.26), channel_id=1, source_target_pairs={{0,2},{1,3},{2,0},{3,1},{4,6},{5,7},{6,4},{7,5},{8,10},{9,11},{10,... | collective-permute-start | bytes 6152 | tf_op jit(solution)/shard_map/ppermute | solution.py:27
  34.7 1.0 %collective-permute-done.13 = f32[1,512]{1,0:T(1,128)S(1)} collective-permute-done((f32[1,512]{1,0:T(1,128)S(1)}, f32[1,512]{1,0:T(1,128)S(1)}, u32[]{:S(2)}, u32[]{:S(2)}) %collective-permute-start.13) | collective-permute-done | bytes 2080 | tf_op jit(solution)/shard_map/ppermute | solution.py:27
  35.7 1.2 %collective-permute-done.12 = f32[1,512]{1,0:T(1,128)S(1)} collective-permute-done((f32[1,512]{1,0:T(1,128)S(1)}, f32[1,512]{1,0:T(1,128)S(1)}, u32[]{:S(2)}, u32[]{:S(2)}) %collective-permute-start.12) | collective-permute-done | bytes 2080 | tf_op jit(solution)/shard_map/ppermute | solution.py:27
  36.9 0.8 %multiply_convert_fusion = bf16[256,512]{1,0:T(8,128)(2,1)} fusion(f32[256,512]{1,0:T(8,128)S(1)} %get-tuple-element.25, f32[512]{0:T(512)S(1)} %bitcast.1), kind=kLoop, calls=%fused_computation | loop fusion | flops 393216 | bytes 788480 | tf_op jit(solution)/shard_map/convert_element_type | solution.py:305
  (15 shorter events, 0.2 us)
Async XLA Ops:
  1.1 10.2 %collective-permute-start.4 = (bf16[528,128]{1,0:T(8,128)(2,1)S(1)}, bf16[528,128]{1,0:T(8,128)(2,1)S(1)}, u32[]{:S(2)}, u32[]{:S(2)}) collective-permute-start(bf16[528,128]{1,0:T(8,128)(2,1)S(1)} %get-tuple-element.17.refs_0_.refs_2_), channel_id=1, source_target_pairs={{0,16},{8,24},{16,0},{24,8},{1,17},{9,25},{17,1},{25,9},{2,18},{10... | collective-permute-start | bytes 405512 | tf_op jit(solution)/shard_map/ppermute | solution.py:27
  4.1 1.2 %collective-permute-start = (f32[1,512]{1,0:T(1,128)S(1)}, f32[1,512]{1,0:T(1,128)S(1)}, u32[]{:S(2)}, u32[]{:S(2)}) collective-permute-start(f32[1,512]{1,0:T(1,128)S(1)} %get-tuple-element.16), channel_id=1, source_target_pairs={{0,8},{8,0},{16,24},{24,16},{1,9},{9,1},{17,25},{25,17},{2,10},{10... | collective-permute-start | bytes 6152 | tf_op jit(solution)/shard_map/ppermute | solution.py:27
  5.3 7.5 %collective-permute-start.1 = (f32[2,512]{1,0:T(2,128)S(1)}, f32[2,512]{1,0:T(2,128)S(1)}, u32[]{:S(2)}, u32[]{:S(2)}) collective-permute-start(f32[2,512]{1,0:T(2,128)S(1)} %pad_maximum_fusion.1.one_ref), channel_id=1, source_target_pairs={{0,5},{1,4},{2,7},{3,6},{4,1},{5,0},{6,3},{7,2},{8,13},{9,12},{10,... | collective-permute-start | bytes 12296 | tf_op jit(solution)/shard_map/ppermute | solution.py:27
  8.9 9.2 %collective-permute-start.6 = (bf16[528,128]{1,0:T(8,128)(2,1)S(1)}, bf16[528,128]{1,0:T(8,128)(2,1)S(1)}, u32[]{:S(2)}, u32[]{:S(2)}) collective-permute-start(bf16[528,128]{1,0:T(8,128)(2,1)S(1)} %get-tuple-element.17.refs_0_.refs_2_), channel_id=1, source_target_pairs={{0,4},{1,5},{2,6},{3,7},{4,0},{5,1},{6,2},{7,3},{8,12},{9,13},{10,... | collective-permute-start | bytes 405512 | tf_op jit(solution)/shard_map/ppermute | solution.py:27
  9.2 8.8 %collective-permute-start.5 = (bf16[528,128]{1,0:T(8,128)(2,1)S(1)}, bf16[528,128]{1,0:T(8,128)(2,1)S(1)}, u32[]{:S(2)}, u32[]{:S(2)}) collective-permute-start(bf16[528,128]{1,0:T(8,128)(2,1)S(1)} %get-tuple-element.17.refs_0_.refs_2_), channel_id=1, source_target_pairs={{0,2},{1,3},{2,0},{3,1},{4,6},{5,7},{6,4},{7,5},{8,10},{9,11},{10,... | collective-permute-start | bytes 405512 | tf_op jit(solution)/shard_map/ppermute | solution.py:27
  10.8 7.3 %collective-permute-start.3 = (bf16[528,128]{1,0:T(8,128)(2,1)S(1)}, bf16[528,128]{1,0:T(8,128)(2,1)S(1)}, u32[]{:S(2)}, u32[]{:S(2)}) collective-permute-start(bf16[528,128]{1,0:T(8,128)(2,1)S(1)} %get-tuple-element.17.refs_0_.refs_2_), channel_id=1, source_target_pairs={{0,1},{1,0},{2,3},{3,2},{4,5},{5,4},{6,7},{7,6},{8,9},{9,8},{10,11... | collective-permute-start | bytes 405512 | tf_op jit(solution)/shard_map/ppermute | solution.py:27
  11.3 7.1 %collective-permute-start.7 = (bf16[528,128]{1,0:T(8,128)(2,1)S(1)}, bf16[528,128]{1,0:T(8,128)(2,1)S(1)}, u32[]{:S(2)}, u32[]{:S(2)}) collective-permute-start(bf16[528,128]{1,0:T(8,128)(2,1)S(1)} %collective-permute-done.4.refs_2_.refs_4_), channel_id=1, source_target_pairs={{0,1},{1,0},{2,3},{3,2},{4,5},{5,4},{6,7},{7,6},{8,9},{9,8},{10,11... | collective-permute-start | bytes 405512 | tf_op jit(solution)/shard_map/ppermute | solution.py:27
  12.8 3.6 %collective-permute-start.2 = (f32[2,512]{1,0:T(2,128)S(1)}, f32[2,512]{1,0:T(2,128)S(1)}, u32[]{:S(2)}, u32[]{:S(2)}) collective-permute-start(f32[2,512]{1,0:T(2,128)S(1)} %add.16), channel_id=1, source_target_pairs={{0,16},{8,24},{16,0},{24,8},{1,17},{9,25},{17,1},{25,9},{2,18},{10... | collective-permute-start | bytes 12296 | tf_op jit(solution)/shard_map/ppermute | solution.py:27
  18.6 9.5 %collective-permute-start.8 = (bf16[1088,128]{1,0:T(8,128)(2,1)S(1)}, bf16[1088,128]{1,0:T(8,128)(2,1)S(1)}, u32[]{:S(2)}, u32[]{:S(2)}) collective-permute-start(bf16[1088,128]{1,0:T(8,128)(2,1)S(1)} %get-tuple-element.20), channel_id=1, source_target_pairs={{0,1},{1,0},{2,3},{3,2},{4,5},{5,4},{6,7},{7,6},{8,9},{9,8},{10,11... | collective-permute-start | bytes 835592 | tf_op jit(solution)/shard_map/ppermute | solution.py:27
  19.2 8.8 %collective-permute-start.9 = (bf16[560,128]{1,0:T(8,128)(2,1)S(1)}, bf16[560,128]{1,0:T(8,128)(2,1)S(1)}, u32[]{:S(2)}, u32[]{:S(2)}) collective-permute-start(bf16[560,128]{1,0:T(8,128)(2,1)S(1)} %get-tuple-element.21), channel_id=1, source_target_pairs={{0,2},{1,3},{2,0},{3,1},{4,6},{5,7},{6,4},{7,5},{8,10},{9,11},{10,... | collective-permute-start | bytes 430088 | tf_op jit(solution)/shard_map/ppermute | solution.py:27
  19.7 8.4 %collective-permute-start.10 = (bf16[560,128]{1,0:T(8,128)(2,1)S(1)}, bf16[560,128]{1,0:T(8,128)(2,1)S(1)}, u32[]{:S(2)}, u32[]{:S(2)}) collective-permute-start(bf16[560,128]{1,0:T(8,128)(2,1)S(1)} %get-tuple-element.22), channel_id=1, source_target_pairs={{0,6},{1,7},{2,4},{3,5},{4,2},{5,3},{6,0},{7,1},{8,14},{9,15},{10,... | collective-permute-start | bytes 430088 | tf_op jit(solution)/shard_map/ppermute | solution.py:27
  30.3 5.4 %collective-permute-start.13 = (f32[1,512]{1,0:T(1,128)S(1)}, f32[1,512]{1,0:T(1,128)S(1)}, u32[]{:S(2)}, u32[]{:S(2)}) collective-permute-start(f32[1,512]{1,0:T(1,128)S(1)} %get-tuple-element.26), channel_id=1, source_target_pairs={{0,6},{1,7},{2,4},{3,5},{4,2},{5,3},{6,0},{7,1},{8,14},{9,15},{10,... | collective-permute-start | bytes 6152 | tf_op jit(solution)/shard_map/ppermute | solution.py:27
  32.4 4.5 %collective-permute-start.12 = (f32[1,512]{1,0:T(1,128)S(1)}, f32[1,512]{1,0:T(1,128)S(1)}, u32[]{:S(2)}, u32[]{:S(2)}) collective-permute-start(f32[1,512]{1,0:T(1,128)S(1)} %get-tuple-element.26), channel_id=1, source_target_pairs={{0,4},{1,5},{2,6},{3,7},{4,0},{5,1},{6,2},{7,3},{8,12},{9,13},{10,... | collective-permute-start | bytes 6152 | tf_op jit(solution)/shard_map/ppermute | solution.py:27
  32.4 4.5 %collective-permute-start.11 = (f32[1,512]{1,0:T(1,128)S(1)}, f32[1,512]{1,0:T(1,128)S(1)}, u32[]{:S(2)}, u32[]{:S(2)}) collective-permute-start(f32[1,512]{1,0:T(1,128)S(1)} %get-tuple-element.26), channel_id=1, source_target_pairs={{0,2},{1,3},{2,0},{3,1},{4,6},{5,7},{6,4},{7,5},{8,10},{9,11},{10,... | collective-permute-start | bytes 6152 | tf_op jit(solution)/shard_map/ppermute | solution.py:27

commit v6 on v5

--- a/solution.py
+++ b/solution.py
@@ -25,10 +25,6 @@
 
 def swap(x, axis, mask):
     return lax.ppermute(x, axis, [(i, i ^ mask) for i in range(lax.axis_size(axis))])
-
-
-def with_partner(x, axis, mask):
-    return jnp.concatenate([x, swap(x, axis, mask)], axis=0)
 
 
 def way_to(mask, axis):
@@ -138,8 +134,8 @@
 
 
 def expand_kernel(right_at, riders, evens, blk_cols, sums_ref, *refs):
-    *halves, _, _, inflated_ref, total_ref, right, left = refs[:2] + refs[-6:]
-    refs = refs[2:-6]
+    *pairs, _, _, inflated_ref, total_ref, right, left = refs[: len(evens)] + refs[-6:]
+    refs = refs[len(evens) : -6]
     rows, size = refs[0].shape
     blk_rows = inflated_ref.shape[0] // size
     spread(blk_rows, blk_cols, size, packets_in(refs, right_at, rows), right)
@@ -151,16 +147,15 @@
     inverse = 1.0 / sums
     my_col = lax.axis_index("gr")
     for n in range(2 * len(evens)):
-        gr = my_col // 2 * 2 + n // len(evens) ^ evens[n % len(evens)]
+        gr = my_col // 2 * 2 + n % 2 ^ evens[n // 2]
         scales = []
         for j in range(blk_cols):
             scale = inverse[j : j + 1]
-            for m in range(1, 2 * len(evens)):
-                there = inverse[m * blk_cols + j : m * blk_cols + j + 1]
-                scale = jnp.where(my_col ^ m == gr, there, scale)
+            for r in range(1, 2 * len(evens)):
+                scale = jnp.where(gr == r, inverse[r * blk_cols + j : r * blk_cols + j + 1], scale)
             scales.append(scale)
-        for part, half in enumerate(halves):
-            packet = half.at[pl.ds(n * rows, rows), :]
+        for part in range(2):
+            packet = pairs[n // 2].at[pl.ds((n % 2 * 2 + part) * rows, rows), :]
             for s, place in enumerate(places_in(packet, size)):
                 row = pl.multiple_of((part * blk_rows + place // blk_cols) * size, size)
                 col = place % blk_cols
@@ -176,6 +171,8 @@
     for j in range(blk_cols):
         at = slice(j * size, (j + 1) * size)
         own = inverse[j : j + 1]
+        for r in range(1, 2 * len(evens)):
+            own = jnp.where(my_col == r, inverse[r * blk_cols + j : r * blk_cols + j + 1], own)
         total = jnp.zeros((1, size), jnp.float32)
         for i in range(2 * blk_rows):
             part, flag = i // blk_rows, SLOTS + i % blk_rows * blk_cols + j
@@ -211,18 +208,17 @@
         name="pack",
     )(in_hbm(in_pattern), in_hbm(out_pattern), in_hbm(weights))
 
-    arrays, right_at, evens = [packet], {0: (0, 0)}, {0: 0}
+    arrays, right_at = [packet], {0: (0, 0)}
 
     def keep(array, masks):
         arrays.append(array)
         right_at.update({m: (len(arrays) - 1, at) for at, m in enumerate(masks)})
 
     riding = gc_size == 8
-    sums = with_partner(sums, "gr", 1)
     if riding:
         sums = pl.pallas_call(
             add_kernel,
-            out_shape=jax.ShapeDtypeStruct(sums.shape, sums.dtype),
+            out_shape=sums_shape,
             in_specs=[VMEM] * 2,
             out_specs=VMEM,
             compiler_params=PARAMS,
@@ -231,19 +227,9 @@
         )(sums, swap(sums, "gc", 5))
     else:
         sums = lax.psum(sums, "gc")
-    keep(swap(packet, "gc", 1), [1])
-    for bit in bits_of(gr_size)[:-1]:
-        for m, n in list(evens.items()):
-            arrays.append(swap(arrays[n], "gr", bit))
-            evens[m | bit] = len(arrays) - 1
-    for bit in reversed(bits_of(gc_size)[:-1]):
+    for bit in reversed(bits_of(gc_size)):
         keep(swap(packet, "gc", bit), [bit])
-    others = {0: right_at[1][0]}
-    for m in list(evens)[1:]:
-        arrays.append(swap(arrays[evens[m]], "gc", 1))
-        others[m] = len(arrays) - 1
-    for bit in reversed(bits_of(gr_size)[:-1]):
-        sums = with_partner(sums, "gr", bit)
+    sums = lax.all_gather(sums, "gr", tiled=True)
 
     hops = {}
     for mask in range(gc_size):
@@ -251,8 +237,7 @@
             parent, hop = way_to(mask, "gc")
             hops.setdefault(hop, []).append((mask, parent))
     routes = [([right_at[parent][0] for _, parent in hop], riding) for hop in hops.values()]
-    routes.append((list(evens.values()), False))
-    routes.append((list(others.values()), False))
+    routes.append(([0, right_at[1][0]], False))
     extra = 2 * gr_size * blk_cols
     sent = pl.pallas_call(
         functools.partial(relay_kernel, routes, riding),
@@ -266,8 +251,11 @@
         name="relay",
     )(sums, *arrays)
     cores = [[i, i + 1] for i in range(0, gr_size, 2)]
+    pairs = {0: sent[-1]}
+    for bit in bits_of(gr_size)[:-1]:
+        pairs.update({m | bit: swap(pair, "gr", bit) for m, pair in list(pairs.items())})
     lefts = [
-        lax.all_gather(half, "gr", axis_index_groups=cores, tiled=True) for half in sent[-2:]
+        lax.all_gather(pair, "gr", axis_index_groups=cores, tiled=True) for pair in pairs.values()
     ]
     right, left = pl.pallas_call(
         functools.partial(spread_kernel, blk_rows, blk_cols, dict(right_at)),
@@ -291,11 +279,11 @@
         keep(swap(arrays[n][at * rows : (at + 1) * rows], "gc", hop), [mask])
     late_at = {m: at for m, at in right_at.items() if m not in early}
     inflated, sums, *_ = pl.pallas_call(
-        functools.partial(expand_kernel, late_at, riders, list(evens), blk_cols),
+        functools.partial(expand_kernel, late_at, riders, list(pairs), blk_cols),
         out_shape=(jax.ShapeDtypeStruct(weights.shape, jnp.float32), sums_shape, right, left),
-        in_specs=[VMEM] * (5 + len(arrays)),
+        in_specs=[VMEM] * (3 + len(lefts) + len(arrays)),
         out_specs=[VMEM] * 4,
-        input_output_aliases={3 + len(arrays): 2, 4 + len(arrays): 3},
+        input_output_aliases={1 + len(lefts) + len(arrays): 2, 2 + len(lefts) + len(arrays): 3},
         compiler_params=PARAMS,
         name="expand",
     )(sums, *lefts, *arrays, right, left)

time: 37.9 us -> 36.7 us (0.968)
  blocking collectives: 4.37 us -> 9.52 us
  waiting for transfers between devices: 8.49 us -> 4.55 us
  starting transfers between devices: 20.2 us -> 17.8 us
    all_gather x2 -> x3, blocking collectives: 4.37 us -> 9.52 us  [the longest x1 5.15 us: shards(): sums = lax.all_gather(sums, 'gr', tiled=True)]
    ppermute x14 -> x11, waiting for transfers between devices: 8.49 us -> 4.55 us  [swap(): lax.ppermute(x, axis, [(i, i ^ mask) for i in range(lax.axis_size(axis))])]
    ppermute x14 -> x11, starting transfers between devices: 20.2 us -> 17.8 us  [swap(): lax.ppermute(x, axis, [(i, i ^ mask) for i in range(lax.axis_size(axis))])]
  transfers between devices with their start and end apart: 14 -> 11, of which waited for: 6 -> 4; matrix products, arithmetic and copies ran while one was open for 0% -> 0% of each run, Pallas kernels for 1% -> 1%
where the time goes in v6:
time: 36.7 us; the launch traced here: 36.5 us
  starting transfers between devices  17.8 us (49%)
  blocking collectives  9.52 us (26%)
  waiting for transfers between devices  4.55 us (12%)
  Pallas kernels  3.81 us (10%)
  other arithmetic  0.77 us (2%)
    ppermute x11, starting transfers between devices, swap(): lax.ppermute(x, axis, [(i, i ^ mask) for i in range(lax.axis_size(axis))])  17.8 us
    all_gather x1, blocking collectives, shards(): sums = lax.all_gather(sums, 'gr', tiled=True)  5.15 us
    ppermute x11, waiting for transfers between devices, swap(): lax.ppermute(x, axis, [(i, i ^ mask) for i in range(lax.axis_size(axis))])  4.55 us
    all_gather x2, blocking collectives, shards(): lax.all_gather(pair, 'gr', axis_index_groups=cores, tiled=True)  4.37 us
    pallas_call x1, Pallas kernels, shards(): pl.pallas_call(functools.partial(expand_kernel, late_at, riders, list(pai...  2.19 us
    pallas_call x1, Pallas kernels, shards(): pl.pallas_call(pack_kernel, out_shape=(jax.ShapeDtypeStruct((rows, size),...  1.07 us
    convert_element_type x1, other arithmetic, shards(): return (inflated / output_total * float(order_size)).astype(jnp.bfloat16)  0.76 us
  transfers between devices with their start and end apart: 11, of which 4 were waited for; matrix products, arithmetic and copies ran while one was open for 0% of the time, Pallas kernels for 1%

profile of v6, /device:TPU:0, one launch (start us, length us, event | category | flops | bytes accessed | tf_op | source)
XLA Modules:
  0.0 36.5 jit_solution(4901471025076296517)
XLA Ops:
  0.0 1.1 %pack.1 = (bf16[528,128]{1,0:T(8,128)(2,1)S(1)}, f32[1,512]{1,0:T(1,128)S(1)}) custom-call(s32[2,4]{1,0:T(2,128)} %flags_hbm.1, s32[2,4]{1,0:T(2,128)} %kept_hbm.1, bf16[256,512]{1,0:T(8,128)(2,1)} %weights_hbm.1), custom_call_target="tpu_custom_call" | custom-call | tf_op jit(solution)/shard_map/pack/pallas_call | solution.py:196
  1.1 5.0 %collective-permute-start = (f32[1,512]{1,0:T(1,128)S(1)}, f32[1,512]{1,0:T(1,128)S(1)}, u32[]{:S(2)}, u32[]{:S(2)}) collective-permute-start(f32[1,512]{1,0:T(1,128)S(1)} %get-tuple-element.15.one_ref), channel_id=1, source_target_pairs={{0,5},{1,4},{2,7},{3,6},{4,1},{5,0},{6,3},{7,2},{8,13},{9,12},{10,... | collective-permute-start | bytes 6152 | tf_op jit(solution)/shard_map/ppermute | solution.py:27
  6.1 0.3 collective-permute-start.3
  6.4 1.6 %collective-permute-start.2 = (bf16[528,128]{1,0:T(8,128)(2,1)S(1)}, bf16[528,128]{1,0:T(8,128)(2,1)S(1)}, u32[]{:S(2)}, u32[]{:S(2)}) collective-permute-start(bf16[528,128]{1,0:T(8,128)(2,1)S(1)} %get-tuple-element.16.refs_0_.refs_2_), channel_id=1, source_target_pairs={{0,2},{1,3},{2,0},{3,1},{4,6},{5,7},{6,4},{7,5},{8,10},{9,11},{10,... | collective-permute-start | bytes 405512 | tf_op jit(solution)/shard_map/ppermute | solution.py:27
  8.0 0.5 %collective-permute-start.1 = (bf16[528,128]{1,0:T(8,128)(2,1)S(1)}, bf16[528,128]{1,0:T(8,128)(2,1)S(1)}, u32[]{:S(2)}, u32[]{:S(2)}) collective-permute-start(bf16[528,128]{1,0:T(8,128)(2,1)S(1)} %get-tuple-element.16.refs_0_.refs_2_), channel_id=1, source_target_pairs={{0,1},{1,0},{2,3},{3,2},{4,5},{5,4},{6,7},{7,6},{8,9},{9,8},{10,11... | collective-permute-start | bytes 405512 | tf_op jit(solution)/shard_map/ppermute | solution.py:27
  8.6 5.2 %all-gather = f32[4,1,512]{2,1,0:T(1,128)S(1)} all-gather(f32[1,1,512]{2,1,0:T(1,128)S(1)} %bitcast.7), channel_id=1, replica_groups=mesh['gr'=4,'gc'=8] {'gr'}, dimensions={0}, use_global_device_ids=true | all-gather | bytes 10240 | tf_op jit(solution)/shard_map/all_gather | solution.py:232
  13.7 1.3 %collective-permute-done.3.refs_3_.refs_5_ = bf16[528,128]{1,0:T(8,128)(2,1)S(1)} collective-permute-done((bf16[528,128]{1,0:T(8,128)(2,1)S(1)}, bf16[528,128]{1,0:T(8,128)(2,1)S(1)}, u32[]{:S(2)}, u32[]{:S(2)}) %collective-permute-start.3) | collective-permute-done | bytes 135200 | tf_op jit(solution)/shard_map/ppermute | solution.py:27
  15.0 0.1 relay.1
  15.1 1.6 %collective-permute-start.4 = (bf16[1056,128]{1,0:T(8,128)(2,1)S(1)}, bf16[1056,128]{1,0:T(8,128)(2,1)S(1)}, u32[]{:S(2)}, u32[]{:S(2)}) collective-permute-start(bf16[1056,128]{1,0:T(8,128)(2,1)S(1)} %get-tuple-element.17), channel_id=1, source_target_pairs={{0,16},{8,24},{16,0},{24,8},{1,17},{9,25},{17,1},{25,9},{2,18},{10... | collective-permute-start | bytes 811016 | tf_op jit(solution)/shard_map/ppermute | solution.py:27
  16.7 0.5 %collective-permute-start.5 = (bf16[1088,128]{1,0:T(8,128)(2,1)S(1)}, bf16[1088,128]{1,0:T(8,128)(2,1)S(1)}, u32[]{:S(2)}, u32[]{:S(2)}) collective-permute-start(bf16[1088,128]{1,0:T(8,128)(2,1)S(1)} %get-tuple-element.18), channel_id=1, source_target_pairs={{0,1},{1,0},{2,3},{3,2},{4,5},{5,4},{6,7},{7,6},{8,9},{9,8},{10,11... | collective-permute-start | bytes 835592 | tf_op jit(solution)/shard_map/ppermute | solution.py:27
  17.2 0.8 %collective-permute-start.6 = (bf16[560,128]{1,0:T(8,128)(2,1)S(1)}, bf16[560,128]{1,0:T(8,128)(2,1)S(1)}, u32[]{:S(2)}, u32[]{:S(2)}) collective-permute-start(bf16[560,128]{1,0:T(8,128)(2,1)S(1)} %get-tuple-element.19), channel_id=1, source_target_pairs={{0,2},{1,3},{2,0},{3,1},{4,6},{5,7},{6,4},{7,5},{8,10},{9,11},{10,... | collective-permute-start | bytes 430088 | tf_op jit(solution)/shard_map/ppermute | solution.py:27
  18.0 3.0 %collective-permute-start.7 = (bf16[560,128]{1,0:T(8,128)(2,1)S(1)}, bf16[560,128]{1,0:T(8,128)(2,1)S(1)}, u32[]{:S(2)}, u32[]{:S(2)}) collective-permute-start(bf16[560,128]{1,0:T(8,128)(2,1)S(1)} %get-tuple-element.20), channel_id=1, source_target_pairs={{0,6},{1,7},{2,4},{3,5},{4,2},{5,3},{6,0},{7,1},{8,14},{9,15},{10,... | collective-permute-start | bytes 430088 | tf_op jit(solution)/shard_map/ppermute | solution.py:27
  21.0 2.2 %all_gather.10.refs_0_ = bf16[2112,128]{1,0:T(8,128)(2,1)S(1)} all-gather(bf16[1056,128]{1,0:T(8,128)(2,1)S(1)} %get-tuple-element.17), channel_id=1, replica_groups={{0,8},{16,24},{1,9},{17,25},{2,10},{18,26},{3,11},{19,27},{4,12},{20,28..., dimensions={0}, use_global_device_ids=true | all-gather | bytes 811008 | tf_op jit(solution)/shard_map/all_gather | solution.py:258
  23.1 0.5 %spread.1 = (bf16[2048,512]{1,0:T(8,128)(2,1)S(1)}, bf16[512,2048]{1,0:T(8,128)(2,1)S(1)}) custom-call(bf16[528,128]{1,0:T(8,128)(2,1)S(1)} %get-tuple-element.16.refs_0_.refs_2_, bf16[528,128]{1,0:T(8,128)(2,1)S(1)} %collective-permute-done.1.refs_1_.refs_3_, bf16[528,128]{1,0:T(8,128)(2,1)S(1)} %collective-permute-done.2.refs_2_.refs_4_, ...), custom_call_target="tpu_custom_call" | custom-call | tf_op jit(solution)/shard_map/spread/pallas_call | solution.py:260
  23.6 2.2 %all_gather.11.refs_1_ = bf16[2112,128]{1,0:T(8,128)(2,1)S(1)} all-gather(bf16[1056,128]{1,0:T(8,128)(2,1)S(1)} %collective-permute-done.4), channel_id=1, replica_groups={{0,8},{16,24},{1,9},{17,25},{2,10},{18,26},{3,11},{19,27},{4,12},{20,28..., dimensions={0}, use_global_device_ids=true | all-gather | bytes 811008 | tf_op jit(solution)/shard_map/all_gather | solution.py:258
  25.8 1.7 %collective-permute-done.7.refs_8_ = bf16[560,128]{1,0:T(8,128)(2,1)S(1)} collective-permute-done((bf16[560,128]{1,0:T(8,128)(2,1)S(1)}, bf16[560,128]{1,0:T(8,128)(2,1)S(1)}, u32[]{:S(2)}, u32[]{:S(2)}) %collective-permute-start.7) | collective-permute-done | bytes 143392 | tf_op jit(solution)/shard_map/ppermute | solution.py:27
  27.5 2.2 %expand.1 = (f32[256,512]{1,0:T(8,128)S(1)}, f32[1,512]{1,0:T(1,128)S(1)}, bf16[2048,512]{1,0:T(8,128)(2,1)S(1)}, bf16[512,2048]{1,0:T(8,128)(2,1)S(1)}) custom-call(f32[4,512]{1,0:T(4,128)S(1)} %bitcast.6, bf16[2112,128]{1,0:T(8,128)(2,1)S(1)} %all_gather.10.refs_0_, ...), custom_call_target="tpu_custom_call", output_to_operand_aliasing={{2}: (10, {}), {3}: (11, {})} | custom-call | tf_op jit(solution)/shard_map/expand/pallas_call | solution.py:281
  29.7 1.5 %collective-permute-start.10 = (f32[1,512]{1,0:T(1,128)S(1)}, f32[1,512]{1,0:T(1,128)S(1)}, u32[]{:S(2)}, u32[]{:S(2)}) collective-permute-start(f32[1,512]{1,0:T(1,128)S(1)} %get-tuple-element.24), channel_id=1, source_target_pairs={{0,6},{1,7},{2,4},{3,5},{4,2},{5,3},{6,0},{7,1},{8,14},{9,15},{10,... | collective-permute-start | bytes 6152 | tf_op jit(solution)/shard_map/ppermute | solution.py:27
  31.2 0.4 collective-permute-start.9
  31.6 2.6 %collective-permute-start.8 = (f32[1,512]{1,0:T(1,128)S(1)}, f32[1,512]{1,0:T(1,128)S(1)}, u32[]{:S(2)}, u32[]{:S(2)}) collective-permute-start(f32[1,512]{1,0:T(1,128)S(1)} %get-tuple-element.24), channel_id=1, source_target_pairs={{0,2},{1,3},{2,0},{3,1},{4,6},{5,7},{6,4},{7,5},{8,10},{9,11},{10,... | collective-permute-start | bytes 6152 | tf_op jit(solution)/shard_map/ppermute | solution.py:27
  34.1 1.0 %collective-permute-done.10 = f32[1,512]{1,0:T(1,128)S(1)} collective-permute-done((f32[1,512]{1,0:T(1,128)S(1)}, f32[1,512]{1,0:T(1,128)S(1)}, u32[]{:S(2)}, u32[]{:S(2)}) %collective-permute-start.10) | collective-permute-done | bytes 2080 | tf_op jit(solution)/shard_map/ppermute | solution.py:27
  35.1 0.6 %collective-permute-done.9 = f32[1,512]{1,0:T(1,128)S(1)} collective-permute-done((f32[1,512]{1,0:T(1,128)S(1)}, f32[1,512]{1,0:T(1,128)S(1)}, u32[]{:S(2)}, u32[]{:S(2)}) %collective-permute-start.9) | collective-permute-done | bytes 2080 | tf_op jit(solution)/shard_map/ppermute | solution.py:27
  35.7 0.0 collective-permute-done.8
  35.7 0.8 %multiply_convert_fusion = bf16[256,512]{1,0:T(8,128)(2,1)} fusion(f32[256,512]{1,0:T(8,128)S(1)} %get-tuple-element.23, f32[512]{0:T(512)S(1)} %bitcast.8), kind=kLoop, calls=%fused_computation | loop fusion | flops 393216 | bytes 788480 | tf_op jit(solution)/shard_map/convert_element_type | solution.py:293
  (9 shorter events, 0.0 us)
Async XLA Ops:
  1.1 7.5 %collective-permute-start = (f32[1,512]{1,0:T(1,128)S(1)}, f32[1,512]{1,0:T(1,128)S(1)}, u32[]{:S(2)}, u32[]{:S(2)}) collective-permute-start(f32[1,512]{1,0:T(1,128)S(1)} %get-tuple-element.15.one_ref), channel_id=1, source_target_pairs={{0,5},{1,4},{2,7},{3,6},{4,1},{5,0},{6,3},{7,2},{8,13},{9,12},{10,... | collective-permute-start | bytes 6152 | tf_op jit(solution)/shard_map/ppermute | solution.py:27
  6.1 8.9 %collective-permute-start.3 = (bf16[528,128]{1,0:T(8,128)(2,1)S(1)}, bf16[528,128]{1,0:T(8,128)(2,1)S(1)}, u32[]{:S(2)}, u32[]{:S(2)}) collective-permute-start(bf16[528,128]{1,0:T(8,128)(2,1)S(1)} %get-tuple-element.16.refs_0_.refs_2_), channel_id=1, source_target_pairs={{0,4},{1,5},{2,6},{3,7},{4,0},{5,1},{6,2},{7,3},{8,12},{9,13},{10,... | collective-permute-start | bytes 405512 | tf_op jit(solution)/shard_map/ppermute | solution.py:27
  6.4 8.6 %collective-permute-start.2 = (bf16[528,128]{1,0:T(8,128)(2,1)S(1)}, bf16[528,128]{1,0:T(8,128)(2,1)S(1)}, u32[]{:S(2)}, u32[]{:S(2)}) collective-permute-start(bf16[528,128]{1,0:T(8,128)(2,1)S(1)} %get-tuple-element.16.refs_0_.refs_2_), channel_id=1, source_target_pairs={{0,2},{1,3},{2,0},{3,1},{4,6},{5,7},{6,4},{7,5},{8,10},{9,11},{10,... | collective-permute-start | bytes 405512 | tf_op jit(solution)/shard_map/ppermute | solution.py:27
  8.0 7.0 %collective-permute-start.1 = (bf16[528,128]{1,0:T(8,128)(2,1)S(1)}, bf16[528,128]{1,0:T(8,128)(2,1)S(1)}, u32[]{:S(2)}, u32[]{:S(2)}) collective-permute-start(bf16[528,128]{1,0:T(8,128)(2,1)S(1)} %get-tuple-element.16.refs_0_.refs_2_), channel_id=1, source_target_pairs={{0,1},{1,0},{2,3},{3,2},{4,5},{5,4},{6,7},{7,6},{8,9},{9,8},{10,11... | collective-permute-start | bytes 405512 | tf_op jit(solution)/shard_map/ppermute | solution.py:27
  15.1 8.5 %collective-permute-start.4 = (bf16[1056,128]{1,0:T(8,128)(2,1)S(1)}, bf16[1056,128]{1,0:T(8,128)(2,1)S(1)}, u32[]{:S(2)}, u32[]{:S(2)}) collective-permute-start(bf16[1056,128]{1,0:T(8,128)(2,1)S(1)} %get-tuple-element.17), channel_id=1, source_target_pairs={{0,16},{8,24},{16,0},{24,8},{1,17},{9,25},{17,1},{25,9},{2,18},{10... | collective-permute-start | bytes 811016 | tf_op jit(solution)/shard_map/ppermute | solution.py:27
  16.7 10.8 %collective-permute-start.5 = (bf16[1088,128]{1,0:T(8,128)(2,1)S(1)}, bf16[1088,128]{1,0:T(8,128)(2,1)S(1)}, u32[]{:S(2)}, u32[]{:S(2)}) collective-permute-start(bf16[1088,128]{1,0:T(8,128)(2,1)S(1)} %get-tuple-element.18), channel_id=1, source_target_pairs={{0,1},{1,0},{2,3},{3,2},{4,5},{5,4},{6,7},{7,6},{8,9},{9,8},{10,11... | collective-permute-start | bytes 835592 | tf_op jit(solution)/shard_map/ppermute | solution.py:27
  17.2 8.6 %collective-permute-start.6 = (bf16[560,128]{1,0:T(8,128)(2,1)S(1)}, bf16[560,128]{1,0:T(8,128)(2,1)S(1)}, u32[]{:S(2)}, u32[]{:S(2)}) collective-permute-start(bf16[560,128]{1,0:T(8,128)(2,1)S(1)} %get-tuple-element.19), channel_id=1, source_target_pairs={{0,2},{1,3},{2,0},{3,1},{4,6},{5,7},{6,4},{7,5},{8,10},{9,11},{10,... | collective-permute-start | bytes 430088 | tf_op jit(solution)/shard_map/ppermute | solution.py:27
  18.0 9.5 %collective-permute-start.7 = (bf16[560,128]{1,0:T(8,128)(2,1)S(1)}, bf16[560,128]{1,0:T(8,128)(2,1)S(1)}, u32[]{:S(2)}, u32[]{:S(2)}) collective-permute-start(bf16[560,128]{1,0:T(8,128)(2,1)S(1)} %get-tuple-element.20), channel_id=1, source_target_pairs={{0,6},{1,7},{2,4},{3,5},{4,2},{5,3},{6,0},{7,1},{8,14},{9,15},{10,... | collective-permute-start | bytes 430088 | tf_op jit(solution)/shard_map/ppermute | solution.py:27
  29.7 5.4 %collective-permute-start.10 = (f32[1,512]{1,0:T(1,128)S(1)}, f32[1,512]{1,0:T(1,128)S(1)}, u32[]{:S(2)}, u32[]{:S(2)}) collective-permute-start(f32[1,512]{1,0:T(1,128)S(1)} %get-tuple-element.24), channel_id=1, source_target_pairs={{0,6},{1,7},{2,4},{3,5},{4,2},{5,3},{6,0},{7,1},{8,14},{9,15},{10,... | collective-permute-start | bytes 6152 | tf_op jit(solution)/shard_map/ppermute | solution.py:27
  31.2 4.5 %collective-permute-start.9 = (f32[1,512]{1,0:T(1,128)S(1)}, f32[1,512]{1,0:T(1,128)S(1)}, u32[]{:S(2)}, u32[]{:S(2)}) collective-permute-start(f32[1,512]{1,0:T(1,128)S(1)} %get-tuple-element.24), channel_id=1, source_target_pairs={{0,4},{1,5},{2,6},{3,7},{4,0},{5,1},{6,2},{7,3},{8,12},{9,13},{10,... | collective-permute-start | bytes 6152 | tf_op jit(solution)/shard_map/ppermute | solution.py:27
  31.6 4.1 %collective-permute-start.8 = (f32[1,512]{1,0:T(1,128)S(1)}, f32[1,512]{1,0:T(1,128)S(1)}, u32[]{:S(2)}, u32[]{:S(2)}) collective-permute-start(f32[1,512]{1,0:T(1,128)S(1)} %get-tuple-element.24), channel_id=1, source_target_pairs={{0,2},{1,3},{2,0},{3,1},{4,6},{5,7},{6,4},{7,5},{8,10},{9,11},{10,... | collective-permute-start | bytes 6152 | tf_op jit(solution)/shard_map/ppermute | solution.py:27

commit v7 on v6

--- a/solution.py
+++ b/solution.py
@@ -151,8 +151,9 @@
         scales = []
         for j in range(blk_cols):
             scale = inverse[j : j + 1]
-            for r in range(1, 2 * len(evens)):
-                scale = jnp.where(gr == r, inverse[r * blk_cols + j : r * blk_cols + j + 1], scale)
+            for m in range(1, 2 * len(evens)):
+                there = inverse[m * blk_cols + j : m * blk_cols + j + 1]
+                scale = jnp.where(my_col ^ m == gr, there, scale)
             scales.append(scale)
         for part in range(2):
             packet = pairs[n // 2].at[pl.ds((n % 2 * 2 + part) * rows, rows), :]
@@ -171,8 +172,6 @@
     for j in range(blk_cols):
         at = slice(j * size, (j + 1) * size)
         own = inverse[j : j + 1]
-        for r in range(1, 2 * len(evens)):
-            own = jnp.where(my_col == r, inverse[r * blk_cols + j : r * blk_cols + j + 1], own)
         total = jnp.zeros((1, size), jnp.float32)
         for i in range(2 * blk_rows):
             part, flag = i // blk_rows, SLOTS + i % blk_rows * blk_cols + j
@@ -218,7 +217,7 @@
     if riding:
         sums = pl.pallas_call(
             add_kernel,
-            out_shape=sums_shape,
+            out_shape=jax.ShapeDtypeStruct(sums.shape, sums.dtype),
             in_specs=[VMEM] * 2,
             out_specs=VMEM,
             compiler_params=PARAMS,
@@ -229,7 +228,7 @@
         sums = lax.psum(sums, "gc")
     for bit in reversed(bits_of(gc_size)):
         keep(swap(packet, "gc", bit), [bit])
-    sums = lax.all_gather(sums, "gr", tiled=True)
+    sums = jnp.concatenate([sums] + [swap(sums, "gr", m) for m in range(1, gr_size)], axis=0)
 
     hops = {}
     for mask in range(gc_size):

time: 36.7 us -> 35.7 us (0.973)
  blocking collectives: 9.52 us -> 4.37 us
  waiting for transfers between devices: 4.55 us -> 7.68 us
  starting transfers between devices: 17.8 us -> 18.9 us
    all_gather x1 -> x0, blocking collectives: 5.15 us -> none  [shards(): sums = lax.all_gather(sums, 'gr', tiled=True)]
    ppermute x11 -> x14, waiting for transfers between devices: 4.55 us -> 7.68 us  [swap(): lax.ppermute(x, axis, [(i, i ^ mask) for i in range(lax.axis_size(axis))])]
    ppermute x11 -> x14, starting transfers between devices: 17.8 us -> 18.9 us  [swap(): lax.ppermute(x, axis, [(i, i ^ mask) for i in range(lax.axis_size(axis))])]
  transfers between devices with their start and end apart: 11 -> 14, of which waited for: 4 -> 7; matrix products, arithmetic and copies ran while one was open for 0% -> 0% of each run, Pallas kernels for 1% -> 1%
where the time goes in v7:
time: 35.7 us; the launch traced here: 35.6 us
  starting transfers between devices  18.9 us (53%)
  waiting for transfers between devices  7.68 us (22%)
  blocking collectives  4.37 us (12%)
  Pallas kernels  3.82 us (11%)
  other arithmetic  0.78 us (2%)
    ppermute x14, starting transfers between devices, swap(): lax.ppermute(x, axis, [(i, i ^ mask) for i in range(lax.axis_size(axis))])  18.9 us
    ppermute x14, waiting for transfers between devices, swap(): lax.ppermute(x, axis, [(i, i ^ mask) for i in range(lax.axis_size(axis))])  7.68 us
    all_gather x2, blocking collectives, shards(): lax.all_gather(pair, 'gr', axis_index_groups=cores, tiled=True)  4.37 us
    pallas_call x1, Pallas kernels, shards(): pl.pallas_call(functools.partial(expand_kernel, late_at, riders, list(pai...  2.2 us
    pallas_call x1, Pallas kernels, shards(): pl.pallas_call(pack_kernel, out_shape=(jax.ShapeDtypeStruct((rows, size),...  1.07 us
    convert_element_type x1, other arithmetic, shards(): return (inflated / output_total * float(order_size)).astype(jnp.bfloat16)  0.76 us
  transfers between devices with their start and end apart: 14, of which 7 were waited for; matrix products, arithmetic and copies ran while one was open for 0% of the time, Pallas kernels for 1%

profile of v7, /device:TPU:0, one launch (start us, length us, event | category | flops | bytes accessed | tf_op | source)
XLA Modules:
  0.0 35.6 jit_solution(15672855760798412891)
XLA Ops:
  0.0 1.1 %pack.1 = (bf16[528,128]{1,0:T(8,128)(2,1)S(1)}, f32[1,512]{1,0:T(1,128)S(1)}) custom-call(s32[2,4]{1,0:T(2,128)} %flags_hbm.1, s32[2,4]{1,0:T(2,128)} %kept_hbm.1, bf16[256,512]{1,0:T(8,128)(2,1)} %weights_hbm.1), custom_call_target="tpu_custom_call" | custom-call | tf_op jit(solution)/shard_map/pack/pallas_call | solution.py:195
  1.1 5.0 %collective-permute-start = (f32[1,512]{1,0:T(1,128)S(1)}, f32[1,512]{1,0:T(1,128)S(1)}, u32[]{:S(2)}, u32[]{:S(2)}) collective-permute-start(f32[1,512]{1,0:T(1,128)S(1)} %get-tuple-element.15.one_ref), channel_id=1, source_target_pairs={{0,5},{1,4},{2,7},{3,6},{4,1},{5,0},{6,3},{7,2},{8,13},{9,12},{10,... | collective-permute-start | bytes 6152 | tf_op jit(solution)/shard_map/ppermute | solution.py:27
  6.1 0.3 collective-permute-start.6
  6.4 1.6 %collective-permute-start.5 = (bf16[528,128]{1,0:T(8,128)(2,1)S(1)}, bf16[528,128]{1,0:T(8,128)(2,1)S(1)}, u32[]{:S(2)}, u32[]{:S(2)}) collective-permute-start(bf16[528,128]{1,0:T(8,128)(2,1)S(1)} %get-tuple-element.16.refs_0_.refs_2_), channel_id=1, source_target_pairs={{0,2},{1,3},{2,0},{3,1},{4,6},{5,7},{6,4},{7,5},{8,10},{9,11},{10,... | collective-permute-start | bytes 405512 | tf_op jit(solution)/shard_map/ppermute | solution.py:27
  8.0 0.5 %collective-permute-start.4 = (bf16[528,128]{1,0:T(8,128)(2,1)S(1)}, bf16[528,128]{1,0:T(8,128)(2,1)S(1)}, u32[]{:S(2)}, u32[]{:S(2)}) collective-permute-start(bf16[528,128]{1,0:T(8,128)(2,1)S(1)} %get-tuple-element.16.refs_0_.refs_2_), channel_id=1, source_target_pairs={{0,1},{1,0},{2,3},{3,2},{4,5},{5,4},{6,7},{7,6},{8,9},{9,8},{10,11... | collective-permute-start | bytes 405512 | tf_op jit(solution)/shard_map/ppermute | solution.py:27
  8.6 1.6 %collective-permute-start.2 = (f32[1,512]{1,0:T(1,128)S(1)}, f32[1,512]{1,0:T(1,128)S(1)}, u32[]{:S(2)}, u32[]{:S(2)}) collective-permute-start(f32[1,512]{1,0:T(1,128)S(1)} %add.16), channel_id=1, source_target_pairs={{0,16},{8,24},{16,0},{24,8},{1,17},{9,25},{17,1},{25,9},{2,18},{10... | collective-permute-start | bytes 6152 | tf_op jit(solution)/shard_map/ppermute | solution.py:27
  10.2 1.4 %collective-permute-done.3 = f32[1,512]{1,0:T(1,128)S(1)} collective-permute-done((f32[1,512]{1,0:T(1,128)S(1)}, f32[1,512]{1,0:T(1,128)S(1)}, u32[]{:S(2)}, u32[]{:S(2)}) %collective-permute-start.3) | collective-permute-done | bytes 2080 | tf_op jit(solution)/shard_map/ppermute | solution.py:27
  11.8 0.5 %collective-permute-done.2 = f32[1,512]{1,0:T(1,128)S(1)} collective-permute-done((f32[1,512]{1,0:T(1,128)S(1)}, f32[1,512]{1,0:T(1,128)S(1)}, u32[]{:S(2)}, u32[]{:S(2)}) %collective-permute-start.2) | collective-permute-done | bytes 2080 | tf_op jit(solution)/shard_map/ppermute | solution.py:27
  12.2 0.5 %collective-permute-done.1 = f32[1,512]{1,0:T(1,128)S(1)} collective-permute-done((f32[1,512]{1,0:T(1,128)S(1)}, f32[1,512]{1,0:T(1,128)S(1)}, u32[]{:S(2)}, u32[]{:S(2)}) %collective-permute-start.1) | collective-permute-done | bytes 2080 | tf_op jit(solution)/shard_map/ppermute | solution.py:27
  12.7 2.2 %collective-permute-done.6.refs_3_.refs_5_ = bf16[528,128]{1,0:T(8,128)(2,1)S(1)} collective-permute-done((bf16[528,128]{1,0:T(8,128)(2,1)S(1)}, bf16[528,128]{1,0:T(8,128)(2,1)S(1)}, u32[]{:S(2)}, u32[]{:S(2)}) %collective-permute-start.6) | collective-permute-done | bytes 135200 | tf_op jit(solution)/shard_map/ppermute | solution.py:27
  15.1 1.6 %collective-permute-start.7 = (bf16[1056,128]{1,0:T(8,128)(2,1)S(1)}, bf16[1056,128]{1,0:T(8,128)(2,1)S(1)}, u32[]{:S(2)}, u32[]{:S(2)}) collective-permute-start(bf16[1056,128]{1,0:T(8,128)(2,1)S(1)} %get-tuple-element.17), channel_id=1, source_target_pairs={{0,16},{8,24},{16,0},{24,8},{1,17},{9,25},{17,1},{25,9},{2,18},{10... | collective-permute-start | bytes 811016 | tf_op jit(solution)/shard_map/ppermute | solution.py:27
  16.7 0.5 %collective-permute-start.8 = (bf16[1088,128]{1,0:T(8,128)(2,1)S(1)}, bf16[1088,128]{1,0:T(8,128)(2,1)S(1)}, u32[]{:S(2)}, u32[]{:S(2)}) collective-permute-start(bf16[1088,128]{1,0:T(8,128)(2,1)S(1)} %get-tuple-element.18), channel_id=1, source_target_pairs={{0,1},{1,0},{2,3},{3,2},{4,5},{5,4},{6,7},{7,6},{8,9},{9,8},{10,11... | collective-permute-start | bytes 835592 | tf_op jit(solution)/shard_map/ppermute | solution.py:27
  17.3 2.9 %collective-permute-start.10 = (bf16[560,128]{1,0:T(8,128)(2,1)S(1)}, bf16[560,128]{1,0:T(8,128)(2,1)S(1)}, u32[]{:S(2)}, u32[]{:S(2)}) collective-permute-start(bf16[560,128]{1,0:T(8,128)(2,1)S(1)} %get-tuple-element.20), channel_id=1, source_target_pairs={{0,6},{1,7},{2,4},{3,5},{4,2},{5,3},{6,0},{7,1},{8,14},{9,15},{10,... | collective-permute-start | bytes 430088 | tf_op jit(solution)/shard_map/ppermute | solution.py:27
  20.2 2.2 %all_gather.6.refs_0_ = bf16[2112,128]{1,0:T(8,128)(2,1)S(1)} all-gather(bf16[1056,128]{1,0:T(8,128)(2,1)S(1)} %get-tuple-element.17), channel_id=1, replica_groups={{0,8},{16,24},{1,9},{17,25},{2,10},{18,26},{3,11},{19,27},{4,12},{20,28..., dimensions={0}, use_global_device_ids=true | all-gather | bytes 811008 | tf_op jit(solution)/shard_map/all_gather | solution.py:257
  22.4 0.5 %spread.1 = (bf16[2048,512]{1,0:T(8,128)(2,1)S(1)}, bf16[512,2048]{1,0:T(8,128)(2,1)S(1)}) custom-call(bf16[528,128]{1,0:T(8,128)(2,1)S(1)} %get-tuple-element.16.refs_0_.refs_2_, bf16[528,128]{1,0:T(8,128)(2,1)S(1)} %collective-permute-done.4.refs_1_.refs_3_, bf16[528,128]{1,0:T(8,128)(2,1)S(1)} %collective-permute-done.5.refs_2_.refs_4_, ...), custom_call_target="tpu_custom_call" | custom-call | tf_op jit(solution)/shard_map/spread/pallas_call | solution.py:259
  22.9 2.2 %all_gather.7.refs_1_ = bf16[2112,128]{1,0:T(8,128)(2,1)S(1)} all-gather(bf16[1056,128]{1,0:T(8,128)(2,1)S(1)} %collective-permute-done.7), channel_id=1, replica_groups={{0,8},{16,24},{1,9},{17,25},{2,10},{18,26},{3,11},{19,27},{4,12},{20,28..., dimensions={0}, use_global_device_ids=true | all-gather | bytes 811008 | tf_op jit(solution)/shard_map/all_gather | solution.py:257
  25.1 1.3 %collective-permute-done.10.refs_8_ = bf16[560,128]{1,0:T(8,128)(2,1)S(1)} collective-permute-done((bf16[560,128]{1,0:T(8,128)(2,1)S(1)}, bf16[560,128]{1,0:T(8,128)(2,1)S(1)}, u32[]{:S(2)}, u32[]{:S(2)}) %collective-permute-start.10) | collective-permute-done | bytes 143392 | tf_op jit(solution)/shard_map/ppermute | solution.py:27
  26.4 2.2 %expand.1 = (f32[256,512]{1,0:T(8,128)S(1)}, f32[1,512]{1,0:T(1,128)S(1)}, bf16[2048,512]{1,0:T(8,128)(2,1)S(1)}, bf16[512,2048]{1,0:T(8,128)(2,1)S(1)}) custom-call(f32[4,512]{1,0:T(4,128)S(1)} %pad_maximum_fusion.sums_ref, bf16[2112,128]{1,0:T(8,128)(2,1)S(1)} %all_gather.6.refs_0_, ...), custom_call_target="tpu_custom_call", output_to_operand_aliasing={{2}: (10, {}), {3}: (11, {})} | custom-call | tf_op jit(solution)/shard_map/expand/pallas_call | solution.py:280
  28.6 1.7 %collective-permute-start.13 = (f32[1,512]{1,0:T(1,128)S(1)}, f32[1,512]{1,0:T(1,128)S(1)}, u32[]{:S(2)}, u32[]{:S(2)}) collective-permute-start(f32[1,512]{1,0:T(1,128)S(1)} %get-tuple-element.24), channel_id=1, source_target_pairs={{0,6},{1,7},{2,4},{3,5},{4,2},{5,3},{6,0},{7,1},{8,14},{9,15},{10,... | collective-permute-start | bytes 6152 | tf_op jit(solution)/shard_map/ppermute | solution.py:27
  30.3 0.5 %collective-permute-start.12 = (f32[1,512]{1,0:T(1,128)S(1)}, f32[1,512]{1,0:T(1,128)S(1)}, u32[]{:S(2)}, u32[]{:S(2)}) collective-permute-start(f32[1,512]{1,0:T(1,128)S(1)} %get-tuple-element.24), channel_id=1, source_target_pairs={{0,4},{1,5},{2,6},{3,7},{4,0},{5,1},{6,2},{7,3},{8,12},{9,13},{10,... | collective-permute-start | bytes 6152 | tf_op jit(solution)/shard_map/ppermute | solution.py:27
  30.8 2.2 %collective-permute-start.11 = (f32[1,512]{1,0:T(1,128)S(1)}, f32[1,512]{1,0:T(1,128)S(1)}, u32[]{:S(2)}, u32[]{:S(2)}) collective-permute-start(f32[1,512]{1,0:T(1,128)S(1)} %get-tuple-element.24), channel_id=1, source_target_pairs={{0,2},{1,3},{2,0},{3,1},{4,6},{5,7},{6,4},{7,5},{8,10},{9,11},{10,... | collective-permute-start | bytes 6152 | tf_op jit(solution)/shard_map/ppermute | solution.py:27
  33.1 1.0 %collective-permute-done.13 = f32[1,512]{1,0:T(1,128)S(1)} collective-permute-done((f32[1,512]{1,0:T(1,128)S(1)}, f32[1,512]{1,0:T(1,128)S(1)}, u32[]{:S(2)}, u32[]{:S(2)}) %collective-permute-start.13) | collective-permute-done | bytes 2080 | tf_op jit(solution)/shard_map/ppermute | solution.py:27
  34.1 0.7 %collective-permute-done.12 = f32[1,512]{1,0:T(1,128)S(1)} collective-permute-done((f32[1,512]{1,0:T(1,128)S(1)}, f32[1,512]{1,0:T(1,128)S(1)}, u32[]{:S(2)}, u32[]{:S(2)}) %collective-permute-start.12) | collective-permute-done | bytes 2080 | tf_op jit(solution)/shard_map/ppermute | solution.py:27
  34.8 0.8 %multiply_convert_fusion = bf16[256,512]{1,0:T(8,128)(2,1)} fusion(f32[256,512]{1,0:T(8,128)S(1)} %get-tuple-element.23, f32[512]{0:T(512)S(1)} %bitcast.1), kind=kLoop, calls=%fused_computation | loop fusion | flops 393216 | bytes 788480 | tf_op jit(solution)/shard_map/convert_element_type | solution.py:292
  (14 shorter events, 0.4 us)
Async XLA Ops:
  1.1 7.5 %collective-permute-start = (f32[1,512]{1,0:T(1,128)S(1)}, f32[1,512]{1,0:T(1,128)S(1)}, u32[]{:S(2)}, u32[]{:S(2)}) collective-permute-start(f32[1,512]{1,0:T(1,128)S(1)} %get-tuple-element.15.one_ref), channel_id=1, source_target_pairs={{0,5},{1,4},{2,7},{3,6},{4,1},{5,0},{6,3},{7,2},{8,13},{9,12},{10,... | collective-permute-start | bytes 6152 | tf_op jit(solution)/shard_map/ppermute | solution.py:27
  6.1 8.9 %collective-permute-start.6 = (bf16[528,128]{1,0:T(8,128)(2,1)S(1)}, bf16[528,128]{1,0:T(8,128)(2,1)S(1)}, u32[]{:S(2)}, u32[]{:S(2)}) collective-permute-start(bf16[528,128]{1,0:T(8,128)(2,1)S(1)} %get-tuple-element.16.refs_0_.refs_2_), channel_id=1, source_target_pairs={{0,4},{1,5},{2,6},{3,7},{4,0},{5,1},{6,2},{7,3},{8,12},{9,13},{10,... | collective-permute-start | bytes 405512 | tf_op jit(solution)/shard_map/ppermute | solution.py:27
  6.4 8.6 %collective-permute-start.5 = (bf16[528,128]{1,0:T(8,128)(2,1)S(1)}, bf16[528,128]{1,0:T(8,128)(2,1)S(1)}, u32[]{:S(2)}, u32[]{:S(2)}) collective-permute-start(bf16[528,128]{1,0:T(8,128)(2,1)S(1)} %get-tuple-element.16.refs_0_.refs_2_), channel_id=1, source_target_pairs={{0,2},{1,3},{2,0},{3,1},{4,6},{5,7},{6,4},{7,5},{8,10},{9,11},{10,... | collective-permute-start | bytes 405512 | tf_op jit(solution)/shard_map/ppermute | solution.py:27
  8.0 7.0 %collective-permute-start.4 = (bf16[528,128]{1,0:T(8,128)(2,1)S(1)}, bf16[528,128]{1,0:T(8,128)(2,1)S(1)}, u32[]{:S(2)}, u32[]{:S(2)}) collective-permute-start(bf16[528,128]{1,0:T(8,128)(2,1)S(1)} %get-tuple-element.16.refs_0_.refs_2_), channel_id=1, source_target_pairs={{0,1},{1,0},{2,3},{3,2},{4,5},{5,4},{6,7},{7,6},{8,9},{9,8},{10,11... | collective-permute-start | bytes 405512 | tf_op jit(solution)/shard_map/ppermute | solution.py:27
  8.6 3.0 %collective-permute-start.3 = (f32[1,512]{1,0:T(1,128)S(1)}, f32[1,512]{1,0:T(1,128)S(1)}, u32[]{:S(2)}, u32[]{:S(2)}) collective-permute-start(f32[1,512]{1,0:T(1,128)S(1)} %add.16), channel_id=1, source_target_pairs={{0,24},{8,16},{16,8},{24,0},{1,25},{9,17},{17,9},{25,1},{2,26},{10... | collective-permute-start | bytes 6152 | tf_op jit(solution)/shard_map/ppermute | solution.py:27
  8.6 3.7 %collective-permute-start.2 = (f32[1,512]{1,0:T(1,128)S(1)}, f32[1,512]{1,0:T(1,128)S(1)}, u32[]{:S(2)}, u32[]{:S(2)}) collective-permute-start(f32[1,512]{1,0:T(1,128)S(1)} %add.16), channel_id=1, source_target_pairs={{0,16},{8,24},{16,0},{24,8},{1,17},{9,25},{17,1},{25,9},{2,18},{10... | collective-permute-start | bytes 6152 | tf_op jit(solution)/shard_map/ppermute | solution.py:27
  11.6 1.2 %collective-permute-start.1 = (f32[1,512]{1,0:T(1,128)S(1)}, f32[1,512]{1,0:T(1,128)S(1)}, u32[]{:S(2)}, u32[]{:S(2)}) collective-permute-start(f32[1,512]{1,0:T(1,128)S(1)} %add.16), channel_id=1, source_target_pairs={{0,8},{8,0},{16,24},{24,16},{1,9},{9,1},{17,25},{25,17},{2,10},{10... | collective-permute-start | bytes 6152 | tf_op jit(solution)/shard_map/ppermute | solution.py:27
  15.1 7.8 %collective-permute-start.7 = (bf16[1056,128]{1,0:T(8,128)(2,1)S(1)}, bf16[1056,128]{1,0:T(8,128)(2,1)S(1)}, u32[]{:S(2)}, u32[]{:S(2)}) collective-permute-start(bf16[1056,128]{1,0:T(8,128)(2,1)S(1)} %get-tuple-element.17), channel_id=1, source_target_pairs={{0,16},{8,24},{16,0},{24,8},{1,17},{9,25},{17,1},{25,9},{2,18},{10... | collective-permute-start | bytes 811016 | tf_op jit(solution)/shard_map/ppermute | solution.py:27
  16.7 9.7 %collective-permute-start.8 = (bf16[1088,128]{1,0:T(8,128)(2,1)S(1)}, bf16[1088,128]{1,0:T(8,128)(2,1)S(1)}, u32[]{:S(2)}, u32[]{:S(2)}) collective-permute-start(bf16[1088,128]{1,0:T(8,128)(2,1)S(1)} %get-tuple-element.18), channel_id=1, source_target_pairs={{0,1},{1,0},{2,3},{3,2},{4,5},{5,4},{6,7},{7,6},{8,9},{9,8},{10,11... | collective-permute-start | bytes 835592 | tf_op jit(solution)/shard_map/ppermute | solution.py:27
  17.2 7.9 %collective-permute-start.9 = (bf16[560,128]{1,0:T(8,128)(2,1)S(1)}, bf16[560,128]{1,0:T(8,128)(2,1)S(1)}, u32[]{:S(2)}, u32[]{:S(2)}) collective-permute-start(bf16[560,128]{1,0:T(8,128)(2,1)S(1)} %get-tuple-element.19), channel_id=1, source_target_pairs={{0,2},{1,3},{2,0},{3,1},{4,6},{5,7},{6,4},{7,5},{8,10},{9,11},{10,... | collective-permute-start | bytes 430088 | tf_op jit(solution)/shard_map/ppermute | solution.py:27
  17.3 9.1 %collective-permute-start.10 = (bf16[560,128]{1,0:T(8,128)(2,1)S(1)}, bf16[560,128]{1,0:T(8,128)(2,1)S(1)}, u32[]{:S(2)}, u32[]{:S(2)}) collective-permute-start(bf16[560,128]{1,0:T(8,128)(2,1)S(1)} %get-tuple-element.20), channel_id=1, source_target_pairs={{0,6},{1,7},{2,4},{3,5},{4,2},{5,3},{6,0},{7,1},{8,14},{9,15},{10,... | collective-permute-start | bytes 430088 | tf_op jit(solution)/shard_map/ppermute | solution.py:27
  28.6 5.4 %collective-permute-start.13 = (f32[1,512]{1,0:T(1,128)S(1)}, f32[1,512]{1,0:T(1,128)S(1)}, u32[]{:S(2)}, u32[]{:S(2)}) collective-permute-start(f32[1,512]{1,0:T(1,128)S(1)} %get-tuple-element.24), channel_id=1, source_target_pairs={{0,6},{1,7},{2,4},{3,5},{4,2},{5,3},{6,0},{7,1},{8,14},{9,15},{10,... | collective-permute-start | bytes 6152 | tf_op jit(solution)/shard_map/ppermute | solution.py:27
  30.3 4.5 %collective-permute-start.12 = (f32[1,512]{1,0:T(1,128)S(1)}, f32[1,512]{1,0:T(1,128)S(1)}, u32[]{:S(2)}, u32[]{:S(2)}) collective-permute-start(f32[1,512]{1,0:T(1,128)S(1)} %get-tuple-element.24), channel_id=1, source_target_pairs={{0,4},{1,5},{2,6},{3,7},{4,0},{5,1},{6,2},{7,3},{8,12},{9,13},{10,... | collective-permute-start | bytes 6152 | tf_op jit(solution)/shard_map/ppermute | solution.py:27
  30.8 4.0 %collective-permute-start.11 = (f32[1,512]{1,0:T(1,128)S(1)}, f32[1,512]{1,0:T(1,128)S(1)}, u32[]{:S(2)}, u32[]{:S(2)}) collective-permute-start(f32[1,512]{1,0:T(1,128)S(1)} %get-tuple-element.24), channel_id=1, source_target_pairs={{0,2},{1,3},{2,0},{3,1},{4,6},{5,7},{6,4},{7,5},{8,10},{9,11},{10,... | collective-permute-start | bytes 6152 | tf_op jit(solution)/shard_map/ppermute | solution.py:27

commit v8 on v7

--- a/solution.py
+++ b/solution.py
@@ -38,7 +38,8 @@
 
 def places_in(packet, size):
     meta = packet[pl.ds(SLOTS * size, META), :].astype(jnp.float32)
-    return [jnp.max(meta[s : s + 1, :]).astype(jnp.int32) for s in range(SLOTS)]
+    meta = meta.astype(jnp.int32)
+    return [meta[s, 0] for s in range(SLOTS)]
 
 
 def pack_kernel(flags_hbm, kept_hbm, weights_hbm, packet_ref, sums_ref, flags_ref, kept_ref, weights_ref, sems):

time: 35.7 us -> 35.6 us (level)
  no operation moved by 1% of the time
where the time goes in v8:
time: 35.6 us; the launch traced here: 35.5 us
  starting transfers between devices  18.9 us (53%)
  waiting for transfers between devices  7.71 us (22%)
  blocking collectives  4.37 us (12%)
  Pallas kernels  3.68 us (10%)
  other arithmetic  0.78 us (2%)
    ppermute x14, starting transfers between devices, swap(): lax.ppermute(x, axis, [(i, i ^ mask) for i in range(lax.axis_size(axis))])  18.9 us
    ppermute x14, waiting for transfers between devices, swap(): lax.ppermute(x, axis, [(i, i ^ mask) for i in range(lax.axis_size(axis))])  7.71 us
    all_gather x2, blocking collectives, shards(): lax.all_gather(pair, 'gr', axis_index_groups=cores, tiled=True)  4.37 us
    pallas_call x1, Pallas kernels, shards(): pl.pallas_call(functools.partial(expand_kernel, late_at, riders, list(pai...  2.08 us
    pallas_call x1, Pallas kernels, shards(): pl.pallas_call(pack_kernel, out_shape=(jax.ShapeDtypeStruct((rows, size),...  1.07 us
    convert_element_type x1, other arithmetic, shards(): return (inflated / output_total * float(order_size)).astype(jnp.bfloat16)  0.76 us
  transfers between devices with their start and end apart: 14, of which 7 were waited for; matrix products, arithmetic and copies ran while one was open for 0% of the time, Pallas kernels for 1%

profile of v8, /device:TPU:0, one launch (start us, length us, event | category | flops | bytes accessed | tf_op | source)
XLA Modules:
  0.0 35.5 jit_solution(15856073802953044232)
XLA Ops:
  0.0 1.1 %pack.1 = (bf16[528,128]{1,0:T(8,128)(2,1)S(1)}, f32[1,512]{1,0:T(1,128)S(1)}) custom-call(s32[2,4]{1,0:T(2,128)} %flags_hbm.1, s32[2,4]{1,0:T(2,128)} %kept_hbm.1, bf16[256,512]{1,0:T(8,128)(2,1)} %weights_hbm.1), custom_call_target="tpu_custom_call" | custom-call | tf_op jit(solution)/shard_map/pack/pallas_call | solution.py:196
  1.1 5.0 %collective-permute-start = (f32[1,512]{1,0:T(1,128)S(1)}, f32[1,512]{1,0:T(1,128)S(1)}, u32[]{:S(2)}, u32[]{:S(2)}) collective-permute-start(f32[1,512]{1,0:T(1,128)S(1)} %get-tuple-element.15.one_ref), channel_id=1, source_target_pairs={{0,5},{1,4},{2,7},{3,6},{4,1},{5,0},{6,3},{7,2},{8,13},{9,12},{10,... | collective-permute-start | bytes 6152 | tf_op jit(solution)/shard_map/ppermute | solution.py:27
  6.1 0.3 collective-permute-start.6
  6.4 1.6 %collective-permute-start.5 = (bf16[528,128]{1,0:T(8,128)(2,1)S(1)}, bf16[528,128]{1,0:T(8,128)(2,1)S(1)}, u32[]{:S(2)}, u32[]{:S(2)}) collective-permute-start(bf16[528,128]{1,0:T(8,128)(2,1)S(1)} %get-tuple-element.16.refs_0_.refs_2_), channel_id=1, source_target_pairs={{0,2},{1,3},{2,0},{3,1},{4,6},{5,7},{6,4},{7,5},{8,10},{9,11},{10,... | collective-permute-start | bytes 405512 | tf_op jit(solution)/shard_map/ppermute | solution.py:27
  8.0 0.5 %collective-permute-start.4 = (bf16[528,128]{1,0:T(8,128)(2,1)S(1)}, bf16[528,128]{1,0:T(8,128)(2,1)S(1)}, u32[]{:S(2)}, u32[]{:S(2)}) collective-permute-start(bf16[528,128]{1,0:T(8,128)(2,1)S(1)} %get-tuple-element.16.refs_0_.refs_2_), channel_id=1, source_target_pairs={{0,1},{1,0},{2,3},{3,2},{4,5},{5,4},{6,7},{7,6},{8,9},{9,8},{10,11... | collective-permute-start | bytes 405512 | tf_op jit(solution)/shard_map/ppermute | solution.py:27
  8.6 1.6 %collective-permute-start.2 = (f32[1,512]{1,0:T(1,128)S(1)}, f32[1,512]{1,0:T(1,128)S(1)}, u32[]{:S(2)}, u32[]{:S(2)}) collective-permute-start(f32[1,512]{1,0:T(1,128)S(1)} %add.16), channel_id=1, source_target_pairs={{0,16},{8,24},{16,0},{24,8},{1,17},{9,25},{17,1},{25,9},{2,18},{10... | collective-permute-start | bytes 6152 | tf_op jit(solution)/shard_map/ppermute | solution.py:27
  10.2 1.4 %collective-permute-done.3 = f32[1,512]{1,0:T(1,128)S(1)} collective-permute-done((f32[1,512]{1,0:T(1,128)S(1)}, f32[1,512]{1,0:T(1,128)S(1)}, u32[]{:S(2)}, u32[]{:S(2)}) %collective-permute-start.3) | collective-permute-done | bytes 2080 | tf_op jit(solution)/shard_map/ppermute | solution.py:27
  11.8 0.5 %collective-permute-done.2 = f32[1,512]{1,0:T(1,128)S(1)} collective-permute-done((f32[1,512]{1,0:T(1,128)S(1)}, f32[1,512]{1,0:T(1,128)S(1)}, u32[]{:S(2)}, u32[]{:S(2)}) %collective-permute-start.2) | collective-permute-done | bytes 2080 | tf_op jit(solution)/shard_map/ppermute | solution.py:27
  12.2 0.5 %collective-permute-done.1 = f32[1,512]{1,0:T(1,128)S(1)} collective-permute-done((f32[1,512]{1,0:T(1,128)S(1)}, f32[1,512]{1,0:T(1,128)S(1)}, u32[]{:S(2)}, u32[]{:S(2)}) %collective-permute-start.1) | collective-permute-done | bytes 2080 | tf_op jit(solution)/shard_map/ppermute | solution.py:27
  12.7 2.2 %collective-permute-done.6.refs_3_.refs_5_ = bf16[528,128]{1,0:T(8,128)(2,1)S(1)} collective-permute-done((bf16[528,128]{1,0:T(8,128)(2,1)S(1)}, bf16[528,128]{1,0:T(8,128)(2,1)S(1)}, u32[]{:S(2)}, u32[]{:S(2)}) %collective-permute-start.6) | collective-permute-done | bytes 135200 | tf_op jit(solution)/shard_map/ppermute | solution.py:27
  15.1 1.6 %collective-permute-start.7 = (bf16[1056,128]{1,0:T(8,128)(2,1)S(1)}, bf16[1056,128]{1,0:T(8,128)(2,1)S(1)}, u32[]{:S(2)}, u32[]{:S(2)}) collective-permute-start(bf16[1056,128]{1,0:T(8,128)(2,1)S(1)} %get-tuple-element.17), channel_id=1, source_target_pairs={{0,16},{8,24},{16,0},{24,8},{1,17},{9,25},{17,1},{25,9},{2,18},{10... | collective-permute-start | bytes 811016 | tf_op jit(solution)/shard_map/ppermute | solution.py:27
  16.7 0.5 %collective-permute-start.8 = (bf16[1088,128]{1,0:T(8,128)(2,1)S(1)}, bf16[1088,128]{1,0:T(8,128)(2,1)S(1)}, u32[]{:S(2)}, u32[]{:S(2)}) collective-permute-start(bf16[1088,128]{1,0:T(8,128)(2,1)S(1)} %get-tuple-element.18), channel_id=1, source_target_pairs={{0,1},{1,0},{2,3},{3,2},{4,5},{5,4},{6,7},{7,6},{8,9},{9,8},{10,11... | collective-permute-start | bytes 835592 | tf_op jit(solution)/shard_map/ppermute | solution.py:27
  17.3 2.9 %collective-permute-start.10 = (bf16[560,128]{1,0:T(8,128)(2,1)S(1)}, bf16[560,128]{1,0:T(8,128)(2,1)S(1)}, u32[]{:S(2)}, u32[]{:S(2)}) collective-permute-start(bf16[560,128]{1,0:T(8,128)(2,1)S(1)} %get-tuple-element.20), channel_id=1, source_target_pairs={{0,6},{1,7},{2,4},{3,5},{4,2},{5,3},{6,0},{7,1},{8,14},{9,15},{10,... | collective-permute-start | bytes 430088 | tf_op jit(solution)/shard_map/ppermute | solution.py:27
  20.3 2.2 %all_gather.6.refs_0_ = bf16[2112,128]{1,0:T(8,128)(2,1)S(1)} all-gather(bf16[1056,128]{1,0:T(8,128)(2,1)S(1)} %get-tuple-element.17), channel_id=1, replica_groups={{0,8},{16,24},{1,9},{17,25},{2,10},{18,26},{3,11},{19,27},{4,12},{20,28..., dimensions={0}, use_global_device_ids=true | all-gather | bytes 811008 | tf_op jit(solution)/shard_map/all_gather | solution.py:258
  22.4 0.4 %spread.1 = (bf16[2048,512]{1,0:T(8,128)(2,1)S(1)}, bf16[512,2048]{1,0:T(8,128)(2,1)S(1)}) custom-call(bf16[528,128]{1,0:T(8,128)(2,1)S(1)} %get-tuple-element.16.refs_0_.refs_2_, bf16[528,128]{1,0:T(8,128)(2,1)S(1)} %collective-permute-done.4.refs_1_.refs_3_, bf16[528,128]{1,0:T(8,128)(2,1)S(1)} %collective-permute-done.5.refs_2_.refs_4_, ...), custom_call_target="tpu_custom_call" | custom-call | tf_op jit(solution)/shard_map/spread/pallas_call | solution.py:260
  22.9 2.2 %all_gather.7.refs_1_ = bf16[2112,128]{1,0:T(8,128)(2,1)S(1)} all-gather(bf16[1056,128]{1,0:T(8,128)(2,1)S(1)} %collective-permute-done.7), channel_id=1, replica_groups={{0,8},{16,24},{1,9},{17,25},{2,10},{18,26},{3,11},{19,27},{4,12},{20,28..., dimensions={0}, use_global_device_ids=true | all-gather | bytes 811008 | tf_op jit(solution)/shard_map/all_gather | solution.py:258
  25.1 1.3 %collective-permute-done.10.refs_8_ = bf16[560,128]{1,0:T(8,128)(2,1)S(1)} collective-permute-done((bf16[560,128]{1,0:T(8,128)(2,1)S(1)}, bf16[560,128]{1,0:T(8,128)(2,1)S(1)}, u32[]{:S(2)}, u32[]{:S(2)}) %collective-permute-start.10) | collective-permute-done | bytes 143392 | tf_op jit(solution)/shard_map/ppermute | solution.py:27
  26.4 2.1 %expand.1 = (f32[256,512]{1,0:T(8,128)S(1)}, f32[1,512]{1,0:T(1,128)S(1)}, bf16[2048,512]{1,0:T(8,128)(2,1)S(1)}, bf16[512,2048]{1,0:T(8,128)(2,1)S(1)}) custom-call(f32[4,512]{1,0:T(4,128)S(1)} %pad_maximum_fusion.sums_ref, bf16[2112,128]{1,0:T(8,128)(2,1)S(1)} %all_gather.6.refs_0_, ...), custom_call_target="tpu_custom_call", output_to_operand_aliasing={{2}: (10, {}), {3}: (11, {})} | custom-call | tf_op jit(solution)/shard_map/expand/pallas_call | solution.py:281
  28.5 1.7 %collective-permute-start.13 = (f32[1,512]{1,0:T(1,128)S(1)}, f32[1,512]{1,0:T(1,128)S(1)}, u32[]{:S(2)}, u32[]{:S(2)}) collective-permute-start(f32[1,512]{1,0:T(1,128)S(1)} %get-tuple-element.24), channel_id=1, source_target_pairs={{0,6},{1,7},{2,4},{3,5},{4,2},{5,3},{6,0},{7,1},{8,14},{9,15},{10,... | collective-permute-start | bytes 6152 | tf_op jit(solution)/shard_map/ppermute | solution.py:27
  30.2 0.5 %collective-permute-start.12 = (f32[1,512]{1,0:T(1,128)S(1)}, f32[1,512]{1,0:T(1,128)S(1)}, u32[]{:S(2)}, u32[]{:S(2)}) collective-permute-start(f32[1,512]{1,0:T(1,128)S(1)} %get-tuple-element.24), channel_id=1, source_target_pairs={{0,4},{1,5},{2,6},{3,7},{4,0},{5,1},{6,2},{7,3},{8,12},{9,13},{10,... | collective-permute-start | bytes 6152 | tf_op jit(solution)/shard_map/ppermute | solution.py:27
  30.7 2.2 %collective-permute-start.11 = (f32[1,512]{1,0:T(1,128)S(1)}, f32[1,512]{1,0:T(1,128)S(1)}, u32[]{:S(2)}, u32[]{:S(2)}) collective-permute-start(f32[1,512]{1,0:T(1,128)S(1)} %get-tuple-element.24), channel_id=1, source_target_pairs={{0,2},{1,3},{2,0},{3,1},{4,6},{5,7},{6,4},{7,5},{8,10},{9,11},{10,... | collective-permute-start | bytes 6152 | tf_op jit(solution)/shard_map/ppermute | solution.py:27
  32.9 1.0 %collective-permute-done.13 = f32[1,512]{1,0:T(1,128)S(1)} collective-permute-done((f32[1,512]{1,0:T(1,128)S(1)}, f32[1,512]{1,0:T(1,128)S(1)}, u32[]{:S(2)}, u32[]{:S(2)}) %collective-permute-start.13) | collective-permute-done | bytes 2080 | tf_op jit(solution)/shard_map/ppermute | solution.py:27
  33.9 0.8 %collective-permute-done.12 = f32[1,512]{1,0:T(1,128)S(1)} collective-permute-done((f32[1,512]{1,0:T(1,128)S(1)}, f32[1,512]{1,0:T(1,128)S(1)}, u32[]{:S(2)}, u32[]{:S(2)}) %collective-permute-start.12) | collective-permute-done | bytes 2080 | tf_op jit(solution)/shard_map/ppermute | solution.py:27
  34.7 0.8 %multiply_convert_fusion = bf16[256,512]{1,0:T(8,128)(2,1)} fusion(f32[256,512]{1,0:T(8,128)S(1)} %get-tuple-element.23, f32[512]{0:T(512)S(1)} %bitcast.1), kind=kLoop, calls=%fused_computation | loop fusion | flops 393216 | bytes 788480 | tf_op jit(solution)/shard_map/convert_element_type | solution.py:293
  (14 shorter events, 0.4 us)
Async XLA Ops:
  1.1 7.5 %collective-permute-start = (f32[1,512]{1,0:T(1,128)S(1)}, f32[1,512]{1,0:T(1,128)S(1)}, u32[]{:S(2)}, u32[]{:S(2)}) collective-permute-start(f32[1,512]{1,0:T(1,128)S(1)} %get-tuple-element.15.one_ref), channel_id=1, source_target_pairs={{0,5},{1,4},{2,7},{3,6},{4,1},{5,0},{6,3},{7,2},{8,13},{9,12},{10,... | collective-permute-start | bytes 6152 | tf_op jit(solution)/shard_map/ppermute | solution.py:27
  6.1 8.9 %collective-permute-start.6 = (bf16[528,128]{1,0:T(8,128)(2,1)S(1)}, bf16[528,128]{1,0:T(8,128)(2,1)S(1)}, u32[]{:S(2)}, u32[]{:S(2)}) collective-permute-start(bf16[528,128]{1,0:T(8,128)(2,1)S(1)} %get-tuple-element.16.refs_0_.refs_2_), channel_id=1, source_target_pairs={{0,4},{1,5},{2,6},{3,7},{4,0},{5,1},{6,2},{7,3},{8,12},{9,13},{10,... | collective-permute-start | bytes 405512 | tf_op jit(solution)/shard_map/ppermute | solution.py:27
  6.4 8.6 %collective-permute-start.5 = (bf16[528,128]{1,0:T(8,128)(2,1)S(1)}, bf16[528,128]{1,0:T(8,128)(2,1)S(1)}, u32[]{:S(2)}, u32[]{:S(2)}) collective-permute-start(bf16[528,128]{1,0:T(8,128)(2,1)S(1)} %get-tuple-element.16.refs_0_.refs_2_), channel_id=1, source_target_pairs={{0,2},{1,3},{2,0},{3,1},{4,6},{5,7},{6,4},{7,5},{8,10},{9,11},{10,... | collective-permute-start | bytes 405512 | tf_op jit(solution)/shard_map/ppermute | solution.py:27
  8.0 7.0 %collective-permute-start.4 = (bf16[528,128]{1,0:T(8,128)(2,1)S(1)}, bf16[528,128]{1,0:T(8,128)(2,1)S(1)}, u32[]{:S(2)}, u32[]{:S(2)}) collective-permute-start(bf16[528,128]{1,0:T(8,128)(2,1)S(1)} %get-tuple-element.16.refs_0_.refs_2_), channel_id=1, source_target_pairs={{0,1},{1,0},{2,3},{3,2},{4,5},{5,4},{6,7},{7,6},{8,9},{9,8},{10,11... | collective-permute-start | bytes 405512 | tf_op jit(solution)/shard_map/ppermute | solution.py:27
  8.6 3.0 %collective-permute-start.3 = (f32[1,512]{1,0:T(1,128)S(1)}, f32[1,512]{1,0:T(1,128)S(1)}, u32[]{:S(2)}, u32[]{:S(2)}) collective-permute-start(f32[1,512]{1,0:T(1,128)S(1)} %add.16), channel_id=1, source_target_pairs={{0,24},{8,16},{16,8},{24,0},{1,25},{9,17},{17,9},{25,1},{2,26},{10... | collective-permute-start | bytes 6152 | tf_op jit(solution)/shard_map/ppermute | solution.py:27
  8.6 3.7 %collective-permute-start.2 = (f32[1,512]{1,0:T(1,128)S(1)}, f32[1,512]{1,0:T(1,128)S(1)}, u32[]{:S(2)}, u32[]{:S(2)}) collective-permute-start(f32[1,512]{1,0:T(1,128)S(1)} %add.16), channel_id=1, source_target_pairs={{0,16},{8,24},{16,0},{24,8},{1,17},{9,25},{17,1},{25,9},{2,18},{10... | collective-permute-start | bytes 6152 | tf_op jit(solution)/shard_map/ppermute | solution.py:27
  11.6 1.2 %collective-permute-start.1 = (f32[1,512]{1,0:T(1,128)S(1)}, f32[1,512]{1,0:T(1,128)S(1)}, u32[]{:S(2)}, u32[]{:S(2)}) collective-permute-start(f32[1,512]{1,0:T(1,128)S(1)} %add.16), channel_id=1, source_target_pairs={{0,8},{8,0},{16,24},{24,16},{1,9},{9,1},{17,25},{25,17},{2,10},{10... | collective-permute-start | bytes 6152 | tf_op jit(solution)/shard_map/ppermute | solution.py:27
  15.1 7.8 %collective-permute-start.7 = (bf16[1056,128]{1,0:T(8,128)(2,1)S(1)}, bf16[1056,128]{1,0:T(8,128)(2,1)S(1)}, u32[]{:S(2)}, u32[]{:S(2)}) collective-permute-start(bf16[1056,128]{1,0:T(8,128)(2,1)S(1)} %get-tuple-element.17), channel_id=1, source_target_pairs={{0,16},{8,24},{16,0},{24,8},{1,17},{9,25},{17,1},{25,9},{2,18},{10... | collective-permute-start | bytes 811016 | tf_op jit(solution)/shard_map/ppermute | solution.py:27
  16.7 9.7 %collective-permute-start.8 = (bf16[1088,128]{1,0:T(8,128)(2,1)S(1)}, bf16[1088,128]{1,0:T(8,128)(2,1)S(1)}, u32[]{:S(2)}, u32[]{:S(2)}) collective-permute-start(bf16[1088,128]{1,0:T(8,128)(2,1)S(1)} %get-tuple-element.18), channel_id=1, source_target_pairs={{0,1},{1,0},{2,3},{3,2},{4,5},{5,4},{6,7},{7,6},{8,9},{9,8},{10,11... | collective-permute-start | bytes 835592 | tf_op jit(solution)/shard_map/ppermute | solution.py:27
  17.2 7.9 %collective-permute-start.9 = (bf16[560,128]{1,0:T(8,128)(2,1)S(1)}, bf16[560,128]{1,0:T(8,128)(2,1)S(1)}, u32[]{:S(2)}, u32[]{:S(2)}) collective-permute-start(bf16[560,128]{1,0:T(8,128)(2,1)S(1)} %get-tuple-element.19), channel_id=1, source_target_pairs={{0,2},{1,3},{2,0},{3,1},{4,6},{5,7},{6,4},{7,5},{8,10},{9,11},{10,... | collective-permute-start | bytes 430088 | tf_op jit(solution)/shard_map/ppermute | solution.py:27
  17.3 9.1 %collective-permute-start.10 = (bf16[560,128]{1,0:T(8,128)(2,1)S(1)}, bf16[560,128]{1,0:T(8,128)(2,1)S(1)}, u32[]{:S(2)}, u32[]{:S(2)}) collective-permute-start(bf16[560,128]{1,0:T(8,128)(2,1)S(1)} %get-tuple-element.20), channel_id=1, source_target_pairs={{0,6},{1,7},{2,4},{3,5},{4,2},{5,3},{6,0},{7,1},{8,14},{9,15},{10,... | collective-permute-start | bytes 430088 | tf_op jit(solution)/shard_map/ppermute | solution.py:27
  28.5 5.4 %collective-permute-start.13 = (f32[1,512]{1,0:T(1,128)S(1)}, f32[1,512]{1,0:T(1,128)S(1)}, u32[]{:S(2)}, u32[]{:S(2)}) collective-permute-start(f32[1,512]{1,0:T(1,128)S(1)} %get-tuple-element.24), channel_id=1, source_target_pairs={{0,6},{1,7},{2,4},{3,5},{4,2},{5,3},{6,0},{7,1},{8,14},{9,15},{10,... | collective-permute-start | bytes 6152 | tf_op jit(solution)/shard_map/ppermute | solution.py:27
  30.2 4.5 %collective-permute-start.12 = (f32[1,512]{1,0:T(1,128)S(1)}, f32[1,512]{1,0:T(1,128)S(1)}, u32[]{:S(2)}, u32[]{:S(2)}) collective-permute-start(f32[1,512]{1,0:T(1,128)S(1)} %get-tuple-element.24), channel_id=1, source_target_pairs={{0,4},{1,5},{2,6},{3,7},{4,0},{5,1},{6,2},{7,3},{8,12},{9,13},{10,... | collective-permute-start | bytes 6152 | tf_op jit(solution)/shard_map/ppermute | solution.py:27
  30.7 4.0 %collective-permute-start.11 = (f32[1,512]{1,0:T(1,128)S(1)}, f32[1,512]{1,0:T(1,128)S(1)}, u32[]{:S(2)}, u32[]{:S(2)}) collective-permute-start(f32[1,512]{1,0:T(1,128)S(1)} %get-tuple-element.24), channel_id=1, source_target_pairs={{0,2},{1,3},{2,0},{3,1},{4,6},{5,7},{6,4},{7,5},{8,10},{9,11},{10,... | collective-permute-start | bytes 6152 | tf_op jit(solution)/shard_map/ppermute | solution.py:27

commit v9 on v8

--- a/solution.py
+++ b/solution.py
@@ -9,6 +9,7 @@
 
 SLOTS = 4
 META = 16
+CHUNKS = 2
 VMEM = pl.BlockSpec(memory_space=pltpu.VMEM)
 HBM = pl.BlockSpec(memory_space=pltpu.HBM)
 PARAMS = pltpu.CompilerParams(vmem_limit_bytes=16 << 20)
@@ -185,6 +186,21 @@
         total_ref[:, at] = total
 
 
+def scale_kernel(order_size, inflated_ref, *refs):
+    *total_refs, out_hbm, out_ref, sems = refs
+    total = sum(ref[...] for ref in total_refs[1:]) + total_refs[0][...]
+    scale = order_size / total
+    rows = out_ref.shape[0] // CHUNKS
+    copies = []
+    for n in range(CHUNKS):
+        at = pl.ds(n * rows, rows)
+        out_ref[at, :] = (inflated_ref[at, :] * scale).astype(out_ref.dtype)
+        copies.append(pltpu.make_async_copy(out_ref.at[at, :], out_hbm.at[at, :], sems.at[n]))
+        copies[-1].start()
+    for copy in copies:
+        copy.wait()
+
+
 def shards(weights, in_pattern, out_pattern):
     blk_rows, blk_cols = in_pattern.shape
     local_rows, local_cols = weights.shape
@@ -287,10 +303,19 @@
         compiler_params=PARAMS,
         name="expand",
     )(sums, *lefts, *arrays, right, left)
-    output_total = sums
-    for mask in range(2, gc_size, 2):
-        output_total = output_total + swap(sums, "gc", mask)
-    return (inflated / output_total * float(order_size)).astype(jnp.bfloat16)
+    totals = [sums] + [swap(sums, "gc", mask) for mask in range(2, gc_size, 2)]
+    return pl.pallas_call(
+        functools.partial(scale_kernel, float(order_size)),
+        out_shape=jax.ShapeDtypeStruct(weights.shape, weights.dtype),
+        in_specs=[VMEM] * (1 + len(totals)),
+        out_specs=HBM,
+        scratch_shapes=[
+            pltpu.VMEM(weights.shape, weights.dtype),
+            pltpu.SemaphoreType.DMA((CHUNKS,)),
+        ],
+        compiler_params=PARAMS,
+        name="scale",
+    )(inflated, *totals)
 
 
 def solution(mesh):

time: 35.6 us -> 35.6 us (level)
  other arithmetic: 0.78 us -> 0.01 us
  Pallas kernels: 3.68 us -> 4.42 us
    convert_element_type x1 -> x0, other arithmetic: 0.76 us -> none  [shards(): return (inflated / output_total * float(order_size)).astype(jnp.bfloat16)]
    pallas_call x0 -> x1, Pallas kernels: none -> 0.74 us  [shards(): pl.pallas_call(functools.partial(scale_kernel, float(order_size)), out_sh...]
where the time goes in v9:
time: 35.6 us; the launch traced here: 35.4 us
  starting transfers between devices  18.9 us (53%)
  waiting for transfers between devices  7.7 us (22%)
  Pallas kernels  4.42 us (12%)
  blocking collectives  4.37 us (12%)
    ppermute x14, starting transfers between devices, swap(): lax.ppermute(x, axis, [(i, i ^ mask) for i in range(lax.axis_size(axis))])  18.9 us
    ppermute x14, waiting for transfers between devices, swap(): lax.ppermute(x, axis, [(i, i ^ mask) for i in range(lax.axis_size(axis))])  7.7 us
    all_gather x2, blocking collectives, shards(): lax.all_gather(pair, 'gr', axis_index_groups=cores, tiled=True)  4.37 us
    pallas_call x1, Pallas kernels, shards(): pl.pallas_call(functools.partial(expand_kernel, late_at, riders, list(pai...  2.08 us
    pallas_call x1, Pallas kernels, shards(): pl.pallas_call(pack_kernel, out_shape=(jax.ShapeDtypeStruct((rows, size),...  1.06 us
    pallas_call x1, Pallas kernels, shards(): pl.pallas_call(functools.partial(scale_kernel, float(order_size)), out_sh...  0.74 us
  transfers between devices with their start and end apart: 14, of which 7 were waited for; matrix products, arithmetic and copies ran while one was open for 0% of the time, Pallas kernels for 1%

profile of v9, /device:TPU:0, one launch (start us, length us, event | category | flops | bytes accessed | tf_op | source)
XLA Modules:
  0.0 35.4 jit_solution(14118276137232569134)
XLA Ops:
  0.0 1.1 %pack.1 = (bf16[528,128]{1,0:T(8,128)(2,1)S(1)}, f32[1,512]{1,0:T(1,128)S(1)}) custom-call(s32[2,4]{1,0:T(2,128)} %flags_hbm.1, s32[2,4]{1,0:T(2,128)} %kept_hbm.1, bf16[256,512]{1,0:T(8,128)(2,1)} %weights_hbm.1), custom_call_target="tpu_custom_call" | custom-call | tf_op jit(solution)/shard_map/pack/pallas_call | solution.py:212
  1.1 5.0 %collective-permute-start = (f32[1,512]{1,0:T(1,128)S(1)}, f32[1,512]{1,0:T(1,128)S(1)}, u32[]{:S(2)}, u32[]{:S(2)}) collective-permute-start(f32[1,512]{1,0:T(1,128)S(1)} %get-tuple-element.15.one_ref), channel_id=1, source_target_pairs={{0,5},{1,4},{2,7},{3,6},{4,1},{5,0},{6,3},{7,2},{8,13},{9,12},{10,... | collective-permute-start | bytes 6152 | tf_op jit(solution)/shard_map/ppermute | solution.py:28
  6.1 0.3 collective-permute-start.6
  6.4 1.6 %collective-permute-start.5 = (bf16[528,128]{1,0:T(8,128)(2,1)S(1)}, bf16[528,128]{1,0:T(8,128)(2,1)S(1)}, u32[]{:S(2)}, u32[]{:S(2)}) collective-permute-start(bf16[528,128]{1,0:T(8,128)(2,1)S(1)} %get-tuple-element.16.refs_0_.refs_2_), channel_id=1, source_target_pairs={{0,2},{1,3},{2,0},{3,1},{4,6},{5,7},{6,4},{7,5},{8,10},{9,11},{10,... | collective-permute-start | bytes 405512 | tf_op jit(solution)/shard_map/ppermute | solution.py:28
  8.0 0.5 %collective-permute-start.4 = (bf16[528,128]{1,0:T(8,128)(2,1)S(1)}, bf16[528,128]{1,0:T(8,128)(2,1)S(1)}, u32[]{:S(2)}, u32[]{:S(2)}) collective-permute-start(bf16[528,128]{1,0:T(8,128)(2,1)S(1)} %get-tuple-element.16.refs_0_.refs_2_), channel_id=1, source_target_pairs={{0,1},{1,0},{2,3},{3,2},{4,5},{5,4},{6,7},{7,6},{8,9},{9,8},{10,11... | collective-permute-start | bytes 405512 | tf_op jit(solution)/shard_map/ppermute | solution.py:28
  8.6 1.6 %collective-permute-start.2 = (f32[1,512]{1,0:T(1,128)S(1)}, f32[1,512]{1,0:T(1,128)S(1)}, u32[]{:S(2)}, u32[]{:S(2)}) collective-permute-start(f32[1,512]{1,0:T(1,128)S(1)} %add.1), channel_id=1, source_target_pairs={{0,16},{8,24},{16,0},{24,8},{1,17},{9,25},{17,1},{25,9},{2,18},{10... | collective-permute-start | bytes 6152 | tf_op jit(solution)/shard_map/ppermute | solution.py:28
  10.2 1.4 %collective-permute-done.3 = f32[1,512]{1,0:T(1,128)S(1)} collective-permute-done((f32[1,512]{1,0:T(1,128)S(1)}, f32[1,512]{1,0:T(1,128)S(1)}, u32[]{:S(2)}, u32[]{:S(2)}) %collective-permute-start.3) | collective-permute-done | bytes 2080 | tf_op jit(solution)/shard_map/ppermute | solution.py:28
  11.8 0.5 %collective-permute-done.2 = f32[1,512]{1,0:T(1,128)S(1)} collective-permute-done((f32[1,512]{1,0:T(1,128)S(1)}, f32[1,512]{1,0:T(1,128)S(1)}, u32[]{:S(2)}, u32[]{:S(2)}) %collective-permute-start.2) | collective-permute-done | bytes 2080 | tf_op jit(solution)/shard_map/ppermute | solution.py:28
  12.2 0.5 %collective-permute-done.1 = f32[1,512]{1,0:T(1,128)S(1)} collective-permute-done((f32[1,512]{1,0:T(1,128)S(1)}, f32[1,512]{1,0:T(1,128)S(1)}, u32[]{:S(2)}, u32[]{:S(2)}) %collective-permute-start.1) | collective-permute-done | bytes 2080 | tf_op jit(solution)/shard_map/ppermute | solution.py:28
  12.7 2.2 %collective-permute-done.6.refs_3_.refs_5_ = bf16[528,128]{1,0:T(8,128)(2,1)S(1)} collective-permute-done((bf16[528,128]{1,0:T(8,128)(2,1)S(1)}, bf16[528,128]{1,0:T(8,128)(2,1)S(1)}, u32[]{:S(2)}, u32[]{:S(2)}) %collective-permute-start.6) | collective-permute-done | bytes 135200 | tf_op jit(solution)/shard_map/ppermute | solution.py:28
  15.1 1.6 %collective-permute-start.7 = (bf16[1056,128]{1,0:T(8,128)(2,1)S(1)}, bf16[1056,128]{1,0:T(8,128)(2,1)S(1)}, u32[]{:S(2)}, u32[]{:S(2)}) collective-permute-start(bf16[1056,128]{1,0:T(8,128)(2,1)S(1)} %get-tuple-element.17), channel_id=1, source_target_pairs={{0,16},{8,24},{16,0},{24,8},{1,17},{9,25},{17,1},{25,9},{2,18},{10... | collective-permute-start | bytes 811016 | tf_op jit(solution)/shard_map/ppermute | solution.py:28
  16.7 0.5 %collective-permute-start.8 = (bf16[1088,128]{1,0:T(8,128)(2,1)S(1)}, bf16[1088,128]{1,0:T(8,128)(2,1)S(1)}, u32[]{:S(2)}, u32[]{:S(2)}) collective-permute-start(bf16[1088,128]{1,0:T(8,128)(2,1)S(1)} %get-tuple-element.18), channel_id=1, source_target_pairs={{0,1},{1,0},{2,3},{3,2},{4,5},{5,4},{6,7},{7,6},{8,9},{9,8},{10,11... | collective-permute-start | bytes 835592 | tf_op jit(solution)/shard_map/ppermute | solution.py:28
  17.3 2.9 %collective-permute-start.10 = (bf16[560,128]{1,0:T(8,128)(2,1)S(1)}, bf16[560,128]{1,0:T(8,128)(2,1)S(1)}, u32[]{:S(2)}, u32[]{:S(2)}) collective-permute-start(bf16[560,128]{1,0:T(8,128)(2,1)S(1)} %get-tuple-element.20), channel_id=1, source_target_pairs={{0,6},{1,7},{2,4},{3,5},{4,2},{5,3},{6,0},{7,1},{8,14},{9,15},{10,... | collective-permute-start | bytes 430088 | tf_op jit(solution)/shard_map/ppermute | solution.py:28
  20.3 2.2 %all_gather.6.refs_0_ = bf16[2112,128]{1,0:T(8,128)(2,1)S(1)} all-gather(bf16[1056,128]{1,0:T(8,128)(2,1)S(1)} %get-tuple-element.17), channel_id=1, replica_groups={{0,8},{16,24},{1,9},{17,25},{2,10},{18,26},{3,11},{19,27},{4,12},{20,28..., dimensions={0}, use_global_device_ids=true | all-gather | bytes 811008 | tf_op jit(solution)/shard_map/all_gather | solution.py:274
  22.4 0.4 %spread.1 = (bf16[2048,512]{1,0:T(8,128)(2,1)S(1)}, bf16[512,2048]{1,0:T(8,128)(2,1)S(1)}) custom-call(bf16[528,128]{1,0:T(8,128)(2,1)S(1)} %get-tuple-element.16.refs_0_.refs_2_, bf16[528,128]{1,0:T(8,128)(2,1)S(1)} %collective-permute-done.4.refs_1_.refs_3_, bf16[528,128]{1,0:T(8,128)(2,1)S(1)} %collective-permute-done.5.refs_2_.refs_4_, ...), custom_call_target="tpu_custom_call" | custom-call | tf_op jit(solution)/shard_map/spread/pallas_call | solution.py:276
  22.9 2.2 %all_gather.7.refs_1_ = bf16[2112,128]{1,0:T(8,128)(2,1)S(1)} all-gather(bf16[1056,128]{1,0:T(8,128)(2,1)S(1)} %collective-permute-done.7), channel_id=1, replica_groups={{0,8},{16,24},{1,9},{17,25},{2,10},{18,26},{3,11},{19,27},{4,12},{20,28..., dimensions={0}, use_global_device_ids=true | all-gather | bytes 811008 | tf_op jit(solution)/shard_map/all_gather | solution.py:274
  25.1 1.3 %collective-permute-done.10.refs_8_ = bf16[560,128]{1,0:T(8,128)(2,1)S(1)} collective-permute-done((bf16[560,128]{1,0:T(8,128)(2,1)S(1)}, bf16[560,128]{1,0:T(8,128)(2,1)S(1)}, u32[]{:S(2)}, u32[]{:S(2)}) %collective-permute-start.10) | collective-permute-done | bytes 143392 | tf_op jit(solution)/shard_map/ppermute | solution.py:28
  26.4 2.1 %expand.1 = (f32[256,512]{1,0:T(8,128)S(1)}, f32[1,512]{1,0:T(1,128)S(1)}, bf16[2048,512]{1,0:T(8,128)(2,1)S(1)}, bf16[512,2048]{1,0:T(8,128)(2,1)S(1)}) custom-call(f32[4,512]{1,0:T(4,128)S(1)} %pad_maximum_fusion.sums_ref, bf16[2112,128]{1,0:T(8,128)(2,1)S(1)} %all_gather.6.refs_0_, ...), custom_call_target="tpu_custom_call", output_to_operand_aliasing={{2}: (10, {}), {3}: (11, {})} | custom-call | tf_op jit(solution)/shard_map/expand/pallas_call | solution.py:297
  28.5 1.7 %collective-permute-start.13 = (f32[1,512]{1,0:T(1,128)S(1)}, f32[1,512]{1,0:T(1,128)S(1)}, u32[]{:S(2)}, u32[]{:S(2)}) collective-permute-start(f32[1,512]{1,0:T(1,128)S(1)} %get-tuple-element.24.refs_0_), channel_id=1, source_target_pairs={{0,6},{1,7},{2,4},{3,5},{4,2},{5,3},{6,0},{7,1},{8,14},{9,15},{10,... | collective-permute-start | bytes 6152 | tf_op jit(solution)/shard_map/ppermute | solution.py:28
  30.2 0.5 %collective-permute-start.12 = (f32[1,512]{1,0:T(1,128)S(1)}, f32[1,512]{1,0:T(1,128)S(1)}, u32[]{:S(2)}, u32[]{:S(2)}) collective-permute-start(f32[1,512]{1,0:T(1,128)S(1)} %get-tuple-element.24.refs_0_), channel_id=1, source_target_pairs={{0,4},{1,5},{2,6},{3,7},{4,0},{5,1},{6,2},{7,3},{8,12},{9,13},{10,... | collective-permute-start | bytes 6152 | tf_op jit(solution)/shard_map/ppermute | solution.py:28
  30.7 2.2 %collective-permute-start.11 = (f32[1,512]{1,0:T(1,128)S(1)}, f32[1,512]{1,0:T(1,128)S(1)}, u32[]{:S(2)}, u32[]{:S(2)}) collective-permute-start(f32[1,512]{1,0:T(1,128)S(1)} %get-tuple-element.24.refs_0_), channel_id=1, source_target_pairs={{0,2},{1,3},{2,0},{3,1},{4,6},{5,7},{6,4},{7,5},{8,10},{9,11},{10,... | collective-permute-start | bytes 6152 | tf_op jit(solution)/shard_map/ppermute | solution.py:28
  32.9 1.0 %collective-permute-done.13.refs_3_ = f32[1,512]{1,0:T(1,128)S(1)} collective-permute-done((f32[1,512]{1,0:T(1,128)S(1)}, f32[1,512]{1,0:T(1,128)S(1)}, u32[]{:S(2)}, u32[]{:S(2)}) %collective-permute-start.13) | collective-permute-done | bytes 2080 | tf_op jit(solution)/shard_map/ppermute | solution.py:28
  33.9 0.8 %collective-permute-done.12.refs_2_ = f32[1,512]{1,0:T(1,128)S(1)} collective-permute-done((f32[1,512]{1,0:T(1,128)S(1)}, f32[1,512]{1,0:T(1,128)S(1)}, u32[]{:S(2)}, u32[]{:S(2)}) %collective-permute-start.12) | collective-permute-done | bytes 2080 | tf_op jit(solution)/shard_map/ppermute | solution.py:28
  34.7 0.7 %scale.1 = bf16[256,512]{1,0:T(8,128)(2,1)} custom-call(f32[256,512]{1,0:T(8,128)S(1)} %get-tuple-element.23.inflated_ref, f32[1,512]{1,0:T(1,128)S(1)} %get-tuple-element.24.refs_0_, f32[1,512]{1,0:T(1,128)S(1)} %collective-permute-done.11.refs_1_, f32[1,512]{1,0:T(1,128)S(1)} %collective-permute-done.12.refs_2_, f32[1,512]{1,0:T(1,128)S(1)} %collective-permute-done.13.refs_3_), custom_call_target="tpu_custom_call" | custom-call | tf_op jit(solution)/shard_map/scale/pallas_call | solution.py:307
  (13 shorter events, 0.4 us)
Async XLA Ops:
  1.1 7.5 %collective-permute-start = (f32[1,512]{1,0:T(1,128)S(1)}, f32[1,512]{1,0:T(1,128)S(1)}, u32[]{:S(2)}, u32[]{:S(2)}) collective-permute-start(f32[1,512]{1,0:T(1,128)S(1)} %get-tuple-element.15.one_ref), channel_id=1, source_target_pairs={{0,5},{1,4},{2,7},{3,6},{4,1},{5,0},{6,3},{7,2},{8,13},{9,12},{10,... | collective-permute-start | bytes 6152 | tf_op jit(solution)/shard_map/ppermute | solution.py:28
  6.1 8.9 %collective-permute-start.6 = (bf16[528,128]{1,0:T(8,128)(2,1)S(1)}, bf16[528,128]{1,0:T(8,128)(2,1)S(1)}, u32[]{:S(2)}, u32[]{:S(2)}) collective-permute-start(bf16[528,128]{1,0:T(8,128)(2,1)S(1)} %get-tuple-element.16.refs_0_.refs_2_), channel_id=1, source_target_pairs={{0,4},{1,5},{2,6},{3,7},{4,0},{5,1},{6,2},{7,3},{8,12},{9,13},{10,... | collective-permute-start | bytes 405512 | tf_op jit(solution)/shard_map/ppermute | solution.py:28
  6.4 8.6 %collective-permute-start.5 = (bf16[528,128]{1,0:T(8,128)(2,1)S(1)}, bf16[528,128]{1,0:T(8,128)(2,1)S(1)}, u32[]{:S(2)}, u32[]{:S(2)}) collective-permute-start(bf16[528,128]{1,0:T(8,128)(2,1)S(1)} %get-tuple-element.16.refs_0_.refs_2_), channel_id=1, source_target_pairs={{0,2},{1,3},{2,0},{3,1},{4,6},{5,7},{6,4},{7,5},{8,10},{9,11},{10,... | collective-permute-start | bytes 405512 | tf_op jit(solution)/shard_map/ppermute | solution.py:28
  8.0 7.0 %collective-permute-start.4 = (bf16[528,128]{1,0:T(8,128)(2,1)S(1)}, bf16[528,128]{1,0:T(8,128)(2,1)S(1)}, u32[]{:S(2)}, u32[]{:S(2)}) collective-permute-start(bf16[528,128]{1,0:T(8,128)(2,1)S(1)} %get-tuple-element.16.refs_0_.refs_2_), channel_id=1, source_target_pairs={{0,1},{1,0},{2,3},{3,2},{4,5},{5,4},{6,7},{7,6},{8,9},{9,8},{10,11... | collective-permute-start | bytes 405512 | tf_op jit(solution)/shard_map/ppermute | solution.py:28
  8.6 3.0 %collective-permute-start.3 = (f32[1,512]{1,0:T(1,128)S(1)}, f32[1,512]{1,0:T(1,128)S(1)}, u32[]{:S(2)}, u32[]{:S(2)}) collective-permute-start(f32[1,512]{1,0:T(1,128)S(1)} %add.1), channel_id=1, source_target_pairs={{0,24},{8,16},{16,8},{24,0},{1,25},{9,17},{17,9},{25,1},{2,26},{10... | collective-permute-start | bytes 6152 | tf_op jit(solution)/shard_map/ppermute | solution.py:28
  8.6 3.7 %collective-permute-start.2 = (f32[1,512]{1,0:T(1,128)S(1)}, f32[1,512]{1,0:T(1,128)S(1)}, u32[]{:S(2)}, u32[]{:S(2)}) collective-permute-start(f32[1,512]{1,0:T(1,128)S(1)} %add.1), channel_id=1, source_target_pairs={{0,16},{8,24},{16,0},{24,8},{1,17},{9,25},{17,1},{25,9},{2,18},{10... | collective-permute-start | bytes 6152 | tf_op jit(solution)/shard_map/ppermute | solution.py:28
  11.6 1.2 %collective-permute-start.1 = (f32[1,512]{1,0:T(1,128)S(1)}, f32[1,512]{1,0:T(1,128)S(1)}, u32[]{:S(2)}, u32[]{:S(2)}) collective-permute-start(f32[1,512]{1,0:T(1,128)S(1)} %add.1), channel_id=1, source_target_pairs={{0,8},{8,0},{16,24},{24,16},{1,9},{9,1},{17,25},{25,17},{2,10},{10... | collective-permute-start | bytes 6152 | tf_op jit(solution)/shard_map/ppermute | solution.py:28
  15.1 7.8 %collective-permute-start.7 = (bf16[1056,128]{1,0:T(8,128)(2,1)S(1)}, bf16[1056,128]{1,0:T(8,128)(2,1)S(1)}, u32[]{:S(2)}, u32[]{:S(2)}) collective-permute-start(bf16[1056,128]{1,0:T(8,128)(2,1)S(1)} %get-tuple-element.17), channel_id=1, source_target_pairs={{0,16},{8,24},{16,0},{24,8},{1,17},{9,25},{17,1},{25,9},{2,18},{10... | collective-permute-start | bytes 811016 | tf_op jit(solution)/shard_map/ppermute | solution.py:28
  16.7 9.7 %collective-permute-start.8 = (bf16[1088,128]{1,0:T(8,128)(2,1)S(1)}, bf16[1088,128]{1,0:T(8,128)(2,1)S(1)}, u32[]{:S(2)}, u32[]{:S(2)}) collective-permute-start(bf16[1088,128]{1,0:T(8,128)(2,1)S(1)} %get-tuple-element.18), channel_id=1, source_target_pairs={{0,1},{1,0},{2,3},{3,2},{4,5},{5,4},{6,7},{7,6},{8,9},{9,8},{10,11... | collective-permute-start | bytes 835592 | tf_op jit(solution)/shard_map/ppermute | solution.py:28
  17.2 7.9 %collective-permute-start.9 = (bf16[560,128]{1,0:T(8,128)(2,1)S(1)}, bf16[560,128]{1,0:T(8,128)(2,1)S(1)}, u32[]{:S(2)}, u32[]{:S(2)}) collective-permute-start(bf16[560,128]{1,0:T(8,128)(2,1)S(1)} %get-tuple-element.19), channel_id=1, source_target_pairs={{0,2},{1,3},{2,0},{3,1},{4,6},{5,7},{6,4},{7,5},{8,10},{9,11},{10,... | collective-permute-start | bytes 430088 | tf_op jit(solution)/shard_map/ppermute | solution.py:28
  17.3 9.1 %collective-permute-start.10 = (bf16[560,128]{1,0:T(8,128)(2,1)S(1)}, bf16[560,128]{1,0:T(8,128)(2,1)S(1)}, u32[]{:S(2)}, u32[]{:S(2)}) collective-permute-start(bf16[560,128]{1,0:T(8,128)(2,1)S(1)} %get-tuple-element.20), channel_id=1, source_target_pairs={{0,6},{1,7},{2,4},{3,5},{4,2},{5,3},{6,0},{7,1},{8,14},{9,15},{10,... | collective-permute-start | bytes 430088 | tf_op jit(solution)/shard_map/ppermute | solution.py:28
  28.5 5.4 %collective-permute-start.13 = (f32[1,512]{1,0:T(1,128)S(1)}, f32[1,512]{1,0:T(1,128)S(1)}, u32[]{:S(2)}, u32[]{:S(2)}) collective-permute-start(f32[1,512]{1,0:T(1,128)S(1)} %get-tuple-element.24.refs_0_), channel_id=1, source_target_pairs={{0,6},{1,7},{2,4},{3,5},{4,2},{5,3},{6,0},{7,1},{8,14},{9,15},{10,... | collective-permute-start | bytes 6152 | tf_op jit(solution)/shard_map/ppermute | solution.py:28
  30.2 4.5 %collective-permute-start.12 = (f32[1,512]{1,0:T(1,128)S(1)}, f32[1,512]{1,0:T(1,128)S(1)}, u32[]{:S(2)}, u32[]{:S(2)}) collective-permute-start(f32[1,512]{1,0:T(1,128)S(1)} %get-tuple-element.24.refs_0_), channel_id=1, source_target_pairs={{0,4},{1,5},{2,6},{3,7},{4,0},{5,1},{6,2},{7,3},{8,12},{9,13},{10,... | collective-permute-start | bytes 6152 | tf_op jit(solution)/shard_map/ppermute | solution.py:28
  30.7 4.0 %collective-permute-start.11 = (f32[1,512]{1,0:T(1,128)S(1)}, f32[1,512]{1,0:T(1,128)S(1)}, u32[]{:S(2)}, u32[]{:S(2)}) collective-permute-start(f32[1,512]{1,0:T(1,128)S(1)} %get-tuple-element.24.refs_0_), channel_id=1, source_target_pairs={{0,2},{1,3},{2,0},{3,1},{4,6},{5,7},{6,4},{7,5},{8,10},{9,11},{10,... | collective-permute-start | bytes 6152 | tf_op jit(solution)/shard_map/ppermute | solution.py:28

commit v10 on v8

--- a/solution.py
+++ b/solution.py
@@ -250,6 +250,13 @@
         compiler_params=PARAMS,
         name="relay",
     )(sums, *arrays)
+    first = list(arrays)
+    first_at = dict(right_at)
+    early, riders = set(right_at), []
+    for (hop, masks), buffer in zip(hops.items(), sent):
+        keep(swap(buffer, "gc", hop), [m for m, _ in masks])
+        if riding:
+            riders.append((len(arrays) - 1, len(masks)))
     cores = [[i, i + 1] for i in range(0, gr_size, 2)]
     pairs = {0: sent[-1]}
     for bit in bits_of(gr_size)[:-1]:
@@ -258,21 +265,16 @@
         lax.all_gather(pair, "gr", axis_index_groups=cores, tiled=True) for pair in pairs.values()
     ]
     right, left = pl.pallas_call(
-        functools.partial(spread_kernel, blk_rows, blk_cols, dict(right_at)),
+        functools.partial(spread_kernel, blk_rows, blk_cols, first_at),
         out_shape=(
             jax.ShapeDtypeStruct((order_size, local_cols), weights.dtype),
             jax.ShapeDtypeStruct((2 * local_rows, order_size), weights.dtype),
         ),
-        in_specs=[VMEM] * len(arrays),
+        in_specs=[VMEM] * len(first),
         out_specs=(VMEM, VMEM),
         compiler_params=PARAMS,
         name="spread",
-    )(*arrays)
-    early, riders = set(right_at), []
-    for (hop, masks), buffer in zip(hops.items(), sent):
-        keep(swap(buffer, "gc", hop), [m for m, _ in masks])
-        if riding:
-            riders.append((len(arrays) - 1, len(masks)))
+    )(*first)
     for mask in sorted(set(range(gc_size)) - set(right_at), key=lambda m: m.bit_count()):
         parent, hop = way_to(mask, "gc")
         n, at = right_at[parent]

time: 35.6 us -> 35.6 us (level)
  no operation moved by 1% of the time
where the time goes in v10:
time: 35.6 us; the launch traced here: 35.5 us
  starting transfers between devices  18.9 us (53%)
  waiting for transfers between devices  7.7 us (22%)
  blocking collectives  4.37 us (12%)
  Pallas kernels  3.68 us (10%)
  other arithmetic  0.78 us (2%)
    ppermute x14, starting transfers between devices, swap(): lax.ppermute(x, axis, [(i, i ^ mask) for i in range(lax.axis_size(axis))])  18.9 us
    ppermute x14, waiting for transfers between devices, swap(): lax.ppermute(x, axis, [(i, i ^ mask) for i in range(lax.axis_size(axis))])  7.7 us
    all_gather x2, blocking collectives, shards(): lax.all_gather(pair, 'gr', axis_index_groups=cores, tiled=True)  4.37 us
    pallas_call x1, Pallas kernels, shards(): pl.pallas_call(functools.partial(expand_kernel, late_at, riders, list(pai...  2.08 us
    pallas_call x1, Pallas kernels, shards(): pl.pallas_call(pack_kernel, out_shape=(jax.ShapeDtypeStruct((rows, size),...  1.07 us
    convert_element_type x1, other arithmetic, shards(): return (inflated / output_total * float(order_size)).astype(jnp.bfloat16)  0.76 us
  transfers between devices with their start and end apart: 14, of which 7 were waited for; matrix products, arithmetic and copies ran while one was open for 0% of the time, Pallas kernels for 1%

profile of v10, /device:TPU:0, one launch (start us, length us, event | category | flops | bytes accessed | tf_op | source)
XLA Modules:
  0.0 35.5 jit_solution(15856073802953044232)
XLA Ops:
  0.0 1.1 %pack.1 = (bf16[528,128]{1,0:T(8,128)(2,1)S(1)}, f32[1,512]{1,0:T(1,128)S(1)}) custom-call(s32[2,4]{1,0:T(2,128)} %flags_hbm.1, s32[2,4]{1,0:T(2,128)} %kept_hbm.1, bf16[256,512]{1,0:T(8,128)(2,1)} %weights_hbm.1), custom_call_target="tpu_custom_call" | custom-call | tf_op jit(solution)/shard_map/pack/pallas_call | solution.py:196
  1.1 5.0 %collective-permute-start = (f32[1,512]{1,0:T(1,128)S(1)}, f32[1,512]{1,0:T(1,128)S(1)}, u32[]{:S(2)}, u32[]{:S(2)}) collective-permute-start(f32[1,512]{1,0:T(1,128)S(1)} %get-tuple-element.15.one_ref), channel_id=1, source_target_pairs={{0,5},{1,4},{2,7},{3,6},{4,1},{5,0},{6,3},{7,2},{8,13},{9,12},{10,... | collective-permute-start | bytes 6152 | tf_op jit(solution)/shard_map/ppermute | solution.py:27
  6.1 0.3 collective-permute-start.6
  6.4 1.6 %collective-permute-start.5 = (bf16[528,128]{1,0:T(8,128)(2,1)S(1)}, bf16[528,128]{1,0:T(8,128)(2,1)S(1)}, u32[]{:S(2)}, u32[]{:S(2)}) collective-permute-start(bf16[528,128]{1,0:T(8,128)(2,1)S(1)} %get-tuple-element.16.refs_0_.refs_2_), channel_id=1, source_target_pairs={{0,2},{1,3},{2,0},{3,1},{4,6},{5,7},{6,4},{7,5},{8,10},{9,11},{10,... | collective-permute-start | bytes 405512 | tf_op jit(solution)/shard_map/ppermute | solution.py:27
  8.0 0.5 %collective-permute-start.4 = (bf16[528,128]{1,0:T(8,128)(2,1)S(1)}, bf16[528,128]{1,0:T(8,128)(2,1)S(1)}, u32[]{:S(2)}, u32[]{:S(2)}) collective-permute-start(bf16[528,128]{1,0:T(8,128)(2,1)S(1)} %get-tuple-element.16.refs_0_.refs_2_), channel_id=1, source_target_pairs={{0,1},{1,0},{2,3},{3,2},{4,5},{5,4},{6,7},{7,6},{8,9},{9,8},{10,11... | collective-permute-start | bytes 405512 | tf_op jit(solution)/shard_map/ppermute | solution.py:27
  8.6 1.6 %collective-permute-start.2 = (f32[1,512]{1,0:T(1,128)S(1)}, f32[1,512]{1,0:T(1,128)S(1)}, u32[]{:S(2)}, u32[]{:S(2)}) collective-permute-start(f32[1,512]{1,0:T(1,128)S(1)} %add.16), channel_id=1, source_target_pairs={{0,16},{8,24},{16,0},{24,8},{1,17},{9,25},{17,1},{25,9},{2,18},{10... | collective-permute-start | bytes 6152 | tf_op jit(solution)/shard_map/ppermute | solution.py:27
  10.2 1.4 %collective-permute-done.3 = f32[1,512]{1,0:T(1,128)S(1)} collective-permute-done((f32[1,512]{1,0:T(1,128)S(1)}, f32[1,512]{1,0:T(1,128)S(1)}, u32[]{:S(2)}, u32[]{:S(2)}) %collective-permute-start.3) | collective-permute-done | bytes 2080 | tf_op jit(solution)/shard_map/ppermute | solution.py:27
  11.8 0.5 %collective-permute-done.2 = f32[1,512]{1,0:T(1,128)S(1)} collective-permute-done((f32[1,512]{1,0:T(1,128)S(1)}, f32[1,512]{1,0:T(1,128)S(1)}, u32[]{:S(2)}, u32[]{:S(2)}) %collective-permute-start.2) | collective-permute-done | bytes 2080 | tf_op jit(solution)/shard_map/ppermute | solution.py:27
  12.2 0.5 %collective-permute-done.1 = f32[1,512]{1,0:T(1,128)S(1)} collective-permute-done((f32[1,512]{1,0:T(1,128)S(1)}, f32[1,512]{1,0:T(1,128)S(1)}, u32[]{:S(2)}, u32[]{:S(2)}) %collective-permute-start.1) | collective-permute-done | bytes 2080 | tf_op jit(solution)/shard_map/ppermute | solution.py:27
  12.7 2.2 %collective-permute-done.6.refs_3_.refs_5_ = bf16[528,128]{1,0:T(8,128)(2,1)S(1)} collective-permute-done((bf16[528,128]{1,0:T(8,128)(2,1)S(1)}, bf16[528,128]{1,0:T(8,128)(2,1)S(1)}, u32[]{:S(2)}, u32[]{:S(2)}) %collective-permute-start.6) | collective-permute-done | bytes 135200 | tf_op jit(solution)/shard_map/ppermute | solution.py:27
  15.1 1.6 %collective-permute-start.7 = (bf16[1056,128]{1,0:T(8,128)(2,1)S(1)}, bf16[1056,128]{1,0:T(8,128)(2,1)S(1)}, u32[]{:S(2)}, u32[]{:S(2)}) collective-permute-start(bf16[1056,128]{1,0:T(8,128)(2,1)S(1)} %get-tuple-element.17), channel_id=1, source_target_pairs={{0,16},{8,24},{16,0},{24,8},{1,17},{9,25},{17,1},{25,9},{2,18},{10... | collective-permute-start | bytes 811016 | tf_op jit(solution)/shard_map/ppermute | solution.py:27
  16.7 0.5 %collective-permute-start.8 = (bf16[1088,128]{1,0:T(8,128)(2,1)S(1)}, bf16[1088,128]{1,0:T(8,128)(2,1)S(1)}, u32[]{:S(2)}, u32[]{:S(2)}) collective-permute-start(bf16[1088,128]{1,0:T(8,128)(2,1)S(1)} %get-tuple-element.18), channel_id=1, source_target_pairs={{0,1},{1,0},{2,3},{3,2},{4,5},{5,4},{6,7},{7,6},{8,9},{9,8},{10,11... | collective-permute-start | bytes 835592 | tf_op jit(solution)/shard_map/ppermute | solution.py:27
  17.3 2.9 %collective-permute-start.10 = (bf16[560,128]{1,0:T(8,128)(2,1)S(1)}, bf16[560,128]{1,0:T(8,128)(2,1)S(1)}, u32[]{:S(2)}, u32[]{:S(2)}) collective-permute-start(bf16[560,128]{1,0:T(8,128)(2,1)S(1)} %get-tuple-element.20), channel_id=1, source_target_pairs={{0,6},{1,7},{2,4},{3,5},{4,2},{5,3},{6,0},{7,1},{8,14},{9,15},{10,... | collective-permute-start | bytes 430088 | tf_op jit(solution)/shard_map/ppermute | solution.py:27
  20.3 2.2 %all_gather.6.refs_0_ = bf16[2112,128]{1,0:T(8,128)(2,1)S(1)} all-gather(bf16[1056,128]{1,0:T(8,128)(2,1)S(1)} %get-tuple-element.17), channel_id=1, replica_groups={{0,8},{16,24},{1,9},{17,25},{2,10},{18,26},{3,11},{19,27},{4,12},{20,28..., dimensions={0}, use_global_device_ids=true | all-gather | bytes 811008 | tf_op jit(solution)/shard_map/all_gather | solution.py:265
  22.4 0.4 %spread.1 = (bf16[2048,512]{1,0:T(8,128)(2,1)S(1)}, bf16[512,2048]{1,0:T(8,128)(2,1)S(1)}) custom-call(bf16[528,128]{1,0:T(8,128)(2,1)S(1)} %get-tuple-element.16.refs_0_.refs_2_, bf16[528,128]{1,0:T(8,128)(2,1)S(1)} %collective-permute-done.4.refs_1_.refs_3_, bf16[528,128]{1,0:T(8,128)(2,1)S(1)} %collective-permute-done.5.refs_2_.refs_4_, ...), custom_call_target="tpu_custom_call" | custom-call | tf_op jit(solution)/shard_map/spread/pallas_call | solution.py:267
  22.9 2.2 %all_gather.7.refs_1_ = bf16[2112,128]{1,0:T(8,128)(2,1)S(1)} all-gather(bf16[1056,128]{1,0:T(8,128)(2,1)S(1)} %collective-permute-done.7), channel_id=1, replica_groups={{0,8},{16,24},{1,9},{17,25},{2,10},{18,26},{3,11},{19,27},{4,12},{20,28..., dimensions={0}, use_global_device_ids=true | all-gather | bytes 811008 | tf_op jit(solution)/shard_map/all_gather | solution.py:265
  25.1 1.3 %collective-permute-done.10.refs_8_ = bf16[560,128]{1,0:T(8,128)(2,1)S(1)} collective-permute-done((bf16[560,128]{1,0:T(8,128)(2,1)S(1)}, bf16[560,128]{1,0:T(8,128)(2,1)S(1)}, u32[]{:S(2)}, u32[]{:S(2)}) %collective-permute-start.10) | collective-permute-done | bytes 143392 | tf_op jit(solution)/shard_map/ppermute | solution.py:27
  26.4 2.1 %expand.1 = (f32[256,512]{1,0:T(8,128)S(1)}, f32[1,512]{1,0:T(1,128)S(1)}, bf16[2048,512]{1,0:T(8,128)(2,1)S(1)}, bf16[512,2048]{1,0:T(8,128)(2,1)S(1)}) custom-call(f32[4,512]{1,0:T(4,128)S(1)} %pad_maximum_fusion.sums_ref, bf16[2112,128]{1,0:T(8,128)(2,1)S(1)} %all_gather.6.refs_0_, ...), custom_call_target="tpu_custom_call", output_to_operand_aliasing={{2}: (10, {}), {3}: (11, {})} | custom-call | tf_op jit(solution)/shard_map/expand/pallas_call | solution.py:283
  28.5 1.7 %collective-permute-start.13 = (f32[1,512]{1,0:T(1,128)S(1)}, f32[1,512]{1,0:T(1,128)S(1)}, u32[]{:S(2)}, u32[]{:S(2)}) collective-permute-start(f32[1,512]{1,0:T(1,128)S(1)} %get-tuple-element.24), channel_id=1, source_target_pairs={{0,6},{1,7},{2,4},{3,5},{4,2},{5,3},{6,0},{7,1},{8,14},{9,15},{10,... | collective-permute-start | bytes 6152 | tf_op jit(solution)/shard_map/ppermute | solution.py:27
  30.2 0.5 %collective-permute-start.12 = (f32[1,512]{1,0:T(1,128)S(1)}, f32[1,512]{1,0:T(1,128)S(1)}, u32[]{:S(2)}, u32[]{:S(2)}) collective-permute-start(f32[1,512]{1,0:T(1,128)S(1)} %get-tuple-element.24), channel_id=1, source_target_pairs={{0,4},{1,5},{2,6},{3,7},{4,0},{5,1},{6,2},{7,3},{8,12},{9,13},{10,... | collective-permute-start | bytes 6152 | tf_op jit(solution)/shard_map/ppermute | solution.py:27
  30.7 2.2 %collective-permute-start.11 = (f32[1,512]{1,0:T(1,128)S(1)}, f32[1,512]{1,0:T(1,128)S(1)}, u32[]{:S(2)}, u32[]{:S(2)}) collective-permute-start(f32[1,512]{1,0:T(1,128)S(1)} %get-tuple-element.24), channel_id=1, source_target_pairs={{0,2},{1,3},{2,0},{3,1},{4,6},{5,7},{6,4},{7,5},{8,10},{9,11},{10,... | collective-permute-start | bytes 6152 | tf_op jit(solution)/shard_map/ppermute | solution.py:27
  32.9 1.0 %collective-permute-done.13 = f32[1,512]{1,0:T(1,128)S(1)} collective-permute-done((f32[1,512]{1,0:T(1,128)S(1)}, f32[1,512]{1,0:T(1,128)S(1)}, u32[]{:S(2)}, u32[]{:S(2)}) %collective-permute-start.13) | collective-permute-done | bytes 2080 | tf_op jit(solution)/shard_map/ppermute | solution.py:27
  33.9 0.8 %collective-permute-done.12 = f32[1,512]{1,0:T(1,128)S(1)} collective-permute-done((f32[1,512]{1,0:T(1,128)S(1)}, f32[1,512]{1,0:T(1,128)S(1)}, u32[]{:S(2)}, u32[]{:S(2)}) %collective-permute-start.12) | collective-permute-done | bytes 2080 | tf_op jit(solution)/shard_map/ppermute | solution.py:27
  34.7 0.8 %multiply_convert_fusion = bf16[256,512]{1,0:T(8,128)(2,1)} fusion(f32[256,512]{1,0:T(8,128)S(1)} %get-tuple-element.23, f32[512]{0:T(512)S(1)} %bitcast.1), kind=kLoop, calls=%fused_computation | loop fusion | flops 393216 | bytes 788480 | tf_op jit(solution)/shard_map/convert_element_type | solution.py:295
  (14 shorter events, 0.4 us)
Async XLA Ops:
  1.1 7.5 %collective-permute-start = (f32[1,512]{1,0:T(1,128)S(1)}, f32[1,512]{1,0:T(1,128)S(1)}, u32[]{:S(2)}, u32[]{:S(2)}) collective-permute-start(f32[1,512]{1,0:T(1,128)S(1)} %get-tuple-element.15.one_ref), channel_id=1, source_target_pairs={{0,5},{1,4},{2,7},{3,6},{4,1},{5,0},{6,3},{7,2},{8,13},{9,12},{10,... | collective-permute-start | bytes 6152 | tf_op jit(solution)/shard_map/ppermute | solution.py:27
  6.1 8.9 %collective-permute-start.6 = (bf16[528,128]{1,0:T(8,128)(2,1)S(1)}, bf16[528,128]{1,0:T(8,128)(2,1)S(1)}, u32[]{:S(2)}, u32[]{:S(2)}) collective-permute-start(bf16[528,128]{1,0:T(8,128)(2,1)S(1)} %get-tuple-element.16.refs_0_.refs_2_), channel_id=1, source_target_pairs={{0,4},{1,5},{2,6},{3,7},{4,0},{5,1},{6,2},{7,3},{8,12},{9,13},{10,... | collective-permute-start | bytes 405512 | tf_op jit(solution)/shard_map/ppermute | solution.py:27
  6.4 8.6 %collective-permute-start.5 = (bf16[528,128]{1,0:T(8,128)(2,1)S(1)}, bf16[528,128]{1,0:T(8,128)(2,1)S(1)}, u32[]{:S(2)}, u32[]{:S(2)}) collective-permute-start(bf16[528,128]{1,0:T(8,128)(2,1)S(1)} %get-tuple-element.16.refs_0_.refs_2_), channel_id=1, source_target_pairs={{0,2},{1,3},{2,0},{3,1},{4,6},{5,7},{6,4},{7,5},{8,10},{9,11},{10,... | collective-permute-start | bytes 405512 | tf_op jit(solution)/shard_map/ppermute | solution.py:27
  8.0 7.0 %collective-permute-start.4 = (bf16[528,128]{1,0:T(8,128)(2,1)S(1)}, bf16[528,128]{1,0:T(8,128)(2,1)S(1)}, u32[]{:S(2)}, u32[]{:S(2)}) collective-permute-start(bf16[528,128]{1,0:T(8,128)(2,1)S(1)} %get-tuple-element.16.refs_0_.refs_2_), channel_id=1, source_target_pairs={{0,1},{1,0},{2,3},{3,2},{4,5},{5,4},{6,7},{7,6},{8,9},{9,8},{10,11... | collective-permute-start | bytes 405512 | tf_op jit(solution)/shard_map/ppermute | solution.py:27
  8.6 3.0 %collective-permute-start.3 = (f32[1,512]{1,0:T(1,128)S(1)}, f32[1,512]{1,0:T(1,128)S(1)}, u32[]{:S(2)}, u32[]{:S(2)}) collective-permute-start(f32[1,512]{1,0:T(1,128)S(1)} %add.16), channel_id=1, source_target_pairs={{0,24},{8,16},{16,8},{24,0},{1,25},{9,17},{17,9},{25,1},{2,26},{10... | collective-permute-start | bytes 6152 | tf_op jit(solution)/shard_map/ppermute | solution.py:27
  8.6 3.7 %collective-permute-start.2 = (f32[1,512]{1,0:T(1,128)S(1)}, f32[1,512]{1,0:T(1,128)S(1)}, u32[]{:S(2)}, u32[]{:S(2)}) collective-permute-start(f32[1,512]{1,0:T(1,128)S(1)} %add.16), channel_id=1, source_target_pairs={{0,16},{8,24},{16,0},{24,8},{1,17},{9,25},{17,1},{25,9},{2,18},{10... | collective-permute-start | bytes 6152 | tf_op jit(solution)/shard_map/ppermute | solution.py:27
  11.6 1.2 %collective-permute-start.1 = (f32[1,512]{1,0:T(1,128)S(1)}, f32[1,512]{1,0:T(1,128)S(1)}, u32[]{:S(2)}, u32[]{:S(2)}) collective-permute-start(f32[1,512]{1,0:T(1,128)S(1)} %add.16), channel_id=1, source_target_pairs={{0,8},{8,0},{16,24},{24,16},{1,9},{9,1},{17,25},{25,17},{2,10},{10... | collective-permute-start | bytes 6152 | tf_op jit(solution)/shard_map/ppermute | solution.py:27
  15.1 7.8 %collective-permute-start.7 = (bf16[1056,128]{1,0:T(8,128)(2,1)S(1)}, bf16[1056,128]{1,0:T(8,128)(2,1)S(1)}, u32[]{:S(2)}, u32[]{:S(2)}) collective-permute-start(bf16[1056,128]{1,0:T(8,128)(2,1)S(1)} %get-tuple-element.17), channel_id=1, source_target_pairs={{0,16},{8,24},{16,0},{24,8},{1,17},{9,25},{17,1},{25,9},{2,18},{10... | collective-permute-start | bytes 811016 | tf_op jit(solution)/shard_map/ppermute | solution.py:27
  16.7 9.7 %collective-permute-start.8 = (bf16[1088,128]{1,0:T(8,128)(2,1)S(1)}, bf16[1088,128]{1,0:T(8,128)(2,1)S(1)}, u32[]{:S(2)}, u32[]{:S(2)}) collective-permute-start(bf16[1088,128]{1,0:T(8,128)(2,1)S(1)} %get-tuple-element.18), channel_id=1, source_target_pairs={{0,1},{1,0},{2,3},{3,2},{4,5},{5,4},{6,7},{7,6},{8,9},{9,8},{10,11... | collective-permute-start | bytes 835592 | tf_op jit(solution)/shard_map/ppermute | solution.py:27
  17.2 7.9 %collective-permute-start.9 = (bf16[560,128]{1,0:T(8,128)(2,1)S(1)}, bf16[560,128]{1,0:T(8,128)(2,1)S(1)}, u32[]{:S(2)}, u32[]{:S(2)}) collective-permute-start(bf16[560,128]{1,0:T(8,128)(2,1)S(1)} %get-tuple-element.19), channel_id=1, source_target_pairs={{0,2},{1,3},{2,0},{3,1},{4,6},{5,7},{6,4},{7,5},{8,10},{9,11},{10,... | collective-permute-start | bytes 430088 | tf_op jit(solution)/shard_map/ppermute | solution.py:27
  17.3 9.1 %collective-permute-start.10 = (bf16[560,128]{1,0:T(8,128)(2,1)S(1)}, bf16[560,128]{1,0:T(8,128)(2,1)S(1)}, u32[]{:S(2)}, u32[]{:S(2)}) collective-permute-start(bf16[560,128]{1,0:T(8,128)(2,1)S(1)} %get-tuple-element.20), channel_id=1, source_target_pairs={{0,6},{1,7},{2,4},{3,5},{4,2},{5,3},{6,0},{7,1},{8,14},{9,15},{10,... | collective-permute-start | bytes 430088 | tf_op jit(solution)/shard_map/ppermute | solution.py:27
  28.5 5.4 %collective-permute-start.13 = (f32[1,512]{1,0:T(1,128)S(1)}, f32[1,512]{1,0:T(1,128)S(1)}, u32[]{:S(2)}, u32[]{:S(2)}) collective-permute-start(f32[1,512]{1,0:T(1,128)S(1)} %get-tuple-element.24), channel_id=1, source_target_pairs={{0,6},{1,7},{2,4},{3,5},{4,2},{5,3},{6,0},{7,1},{8,14},{9,15},{10,... | collective-permute-start | bytes 6152 | tf_op jit(solution)/shard_map/ppermute | solution.py:27
  30.2 4.5 %collective-permute-start.12 = (f32[1,512]{1,0:T(1,128)S(1)}, f32[1,512]{1,0:T(1,128)S(1)}, u32[]{:S(2)}, u32[]{:S(2)}) collective-permute-start(f32[1,512]{1,0:T(1,128)S(1)} %get-tuple-element.24), channel_id=1, source_target_pairs={{0,4},{1,5},{2,6},{3,7},{4,0},{5,1},{6,2},{7,3},{8,12},{9,13},{10,... | collective-permute-start | bytes 6152 | tf_op jit(solution)/shard_map/ppermute | solution.py:27
  30.7 4.0 %collective-permute-start.11 = (f32[1,512]{1,0:T(1,128)S(1)}, f32[1,512]{1,0:T(1,128)S(1)}, u32[]{:S(2)}, u32[]{:S(2)}) collective-permute-start(f32[1,512]{1,0:T(1,128)S(1)} %get-tuple-element.24), channel_id=1, source_target_pairs={{0,2},{1,3},{2,0},{3,1},{4,6},{5,7},{6,4},{7,5},{8,10},{9,11},{10,... | collective-permute-start | bytes 6152 | tf_op jit(solution)/shard_map/ppermute | solution.py:27
